TPU v7x, 32 devices: a whole 2x2x4 slice. The times are simulated.
32 devices in a mesh: batch: 8 (over z, core), head: 4 (over y, x).
Axes of the slice: x: 2, y: 2, z: 4, core: 2. Of those that a mesh axis runs over, the one named last changes fastest.
Arguments:
- tokens: bfloat16 [8192, 2048], P(('batch', 'head')), may hold values from -6 to 6
- attention_gain: float32 [2048], replicated, may hold values from 0.25 to 1.75
- query_down: bfloat16 [2048, 1024], replicated, may hold values from -0.125 to 0.125
- query_gain: float32 [1024], replicated, may hold values from 0.25 to 1.75
- query_up: bfloat16 [1024, 4096], P(None, 'head'), may hold values from -0.1875 to 0.1875
- key_weight: bfloat16 [2048, 256], replicated, may hold values from -0.25 to 0.25
- value_weight: bfloat16 [2048, 256], replicated, may hold values from -0.125 to 0.125
- out_weight: bfloat16 [4096, 2048], P('head'), may hold values from -0.375 to 0.375
- feed_gain: float32 [2048], replicated, may hold values from 0.25 to 1.75
- gate_weight: bfloat16 [2048, 5632], P(('batch', 'head')), may hold values from -0.125 to 0.125
- up_weight: bfloat16 [2048, 5632], P(('batch', 'head')), may hold values from -0.125 to 0.125
- down_weight: bfloat16 [5632, 2048], P(None, ('batch', 'head')), may hold values from -0.078125 to 0.078125
- lengths: int32 [8, 3], P('batch'), may hold values from 0 to 1024, as said below
- cotangent: bfloat16 [8192, 2048], P(('batch', 'head')), may hold values from -6 to 6
Outputs:
- output: bfloat16 [8192, 2048], P(('batch', 'head'))
- input_gradient: float32 [8192, 2048], P(('batch', 'head'))
- attention_gain_gradient: float32 [2048], replicated
- query_down_gradient: float32 [2048, 1024], replicated
- query_gain_gradient: float32 [1024], replicated
- query_up_gradient: float32 [1024, 4096], P(None, 'head')
- key_weight_gradient: float32 [2048, 256], replicated
- value_weight_gradient: float32 [2048, 256], replicated
- out_weight_gradient: float32 [4096, 2048], P('head')
- feed_gain_gradient: float32 [2048], replicated
- gate_weight_gradient: float32 [2048, 5632], P(('batch', 'head'))
- up_weight_gradient: float32 [2048, 5632], P(('batch', 'head'))
- down_weight_gradient: float32 [5632, 2048], P(None, ('batch', 'head'))
Inputs may be any that keep to these rules, and one draw needn't show every extreme that they name: In each batch group's row the first and the last length lie from 0 to 255 and the three lengths sum to 1024; batch group 0 is one whole document.
All inputs are finite; a program needn't handle non-finite values.
Results may differ from a plain program's by a relative error of at most 0.02.
Values may be sent and summed in bfloat16 or wider, within the bound.
No kernel may reach another device: no remote copies, remote signals or barrier semaphores. Data moves between devices by JAX's collectives and lax.ppermute only.
A program may use at most 576 MiB of HBM per device.

v0:
```python
import math

import jax
import jax.numpy as jnp
from jax import lax
from jax.sharding import PartitionSpec as P

BLOCK = 512


epsilon = 1e-05
masked_value = -1e30


def rescale(values, gain):
    factor = lax.rsqrt(jnp.mean(values * values, axis=-1, keepdims=True) + epsilon)
    return (values * factor * gain, factor)


def rescale_back(values, factor, gain, upstream):
    weighted = upstream * gain
    inner_mean = jnp.mean(values * weighted, axis=-1, keepdims=True)
    back = factor * weighted - values * (factor * factor * factor) * inner_mean
    return (back, jnp.sum(upstream * values * factor, axis=0))


def document_places(lengths, total):
    bounds = jnp.cumsum(lengths.reshape(-1), dtype=jnp.int32)
    index = jnp.arange(total, dtype=jnp.int32)
    segment = (index >= bounds[0]).astype(jnp.int32) + (index >= bounds[1]).astype(jnp.int32)
    begin = jnp.where(segment == 0, 0, jnp.where(segment == 1, bounds[0], bounds[1]))
    return (segment, index - begin)


def rotary_tables(place, width):
    half = width // 2
    rates = 10000.0 ** (-2.0 * jnp.arange(half, dtype=jnp.float32) / width)
    turns = place.astype(jnp.float32)[:, None] * rates[None, :]
    return (jnp.cos(turns), jnp.sin(turns))


def rotate(values, cosine, sine):
    half = values.shape[-1] // 2
    first = values[..., :half]
    second = values[..., half:]
    return jnp.concatenate(
        [first * cosine - second * sine, second * cosine + first * sine], axis=-1
    )


def rotate_back(grads, cosine, sine):
    half = grads.shape[-1] // 2
    first = grads[..., :half]
    second = grads[..., half:]
    return jnp.concatenate(
        [first * cosine + second * sine, second * cosine - first * sine], axis=-1
    )


def block_scores(query_low, keys_all, segment, number, scale_factor):
    begin = number * BLOCK
    limit = begin + BLOCK
    scores = (
        jnp.einsum(
            "qhd,kd->hqk",
            query_low[begin:limit],
            keys_all[:limit],
            preferred_element_type=jnp.float32,
        )
        * scale_factor
    )
    query_index = jnp.arange(begin, limit, dtype=jnp.int32)
    key_index = jnp.arange(limit, dtype=jnp.int32)
    allowed = (segment[begin:limit, None] == segment[None, :limit]) & (
        key_index[None, :] <= query_index[:, None]
    )
    return jnp.where(allowed[None], scores, masked_value)


def shards(
    tokens,
    attention_gain,
    query_down,
    query_gain,
    query_up,
    key_weight,
    value_weight,
    out_weight,
    feed_gain,
    gate_weight,
    up_weight,
    down_weight,
    lengths,
    cotangent,
):
    rows = tokens.shape[0]
    total = rows * lax.axis_size("head")
    offset = lax.axis_index("head") * rows
    head_width = key_weight.shape[1]
    local_heads = query_up.shape[1] // head_width
    scale_factor = 1.0 / math.sqrt(head_width)
    segment, place = document_places(lengths, total)
    cosine, sine = rotary_tables(place, head_width)
    own_cosine = lax.dynamic_slice_in_dim(cosine, offset, rows, 0)
    own_sine = lax.dynamic_slice_in_dim(sine, offset, rows, 0)
    inputs = tokens.astype(jnp.float32)
    normed, first_factor = rescale(inputs, attention_gain)
    normed_low = normed.astype(jnp.bfloat16)
    latent = jnp.dot(normed_low, query_down, preferred_element_type=jnp.float32)
    latent_in, latent_factor = rescale(latent, query_gain)
    latent_low = latent_in.astype(jnp.bfloat16)
    key_raw = jnp.dot(normed_low, key_weight, preferred_element_type=jnp.float32)
    key_low = rotate(key_raw, own_cosine, own_sine).astype(jnp.bfloat16)
    value_low = jnp.dot(normed_low, value_weight, preferred_element_type=jnp.float32).astype(
        jnp.bfloat16
    )
    latent_all, keys_all, values_all = (
        lax.all_gather(latent_low, "head", axis=0, tiled=True),
        lax.all_gather(key_low, "head", axis=0, tiled=True),
        lax.all_gather(value_low, "head", axis=0, tiled=True),
    )
    query_raw = jnp.dot(latent_all, query_up, preferred_element_type=jnp.float32).reshape(
        total, local_heads, head_width
    )
    query_low = rotate(query_raw, cosine[:, None, :], sine[:, None, :]).astype(jnp.bfloat16)
    count_blocks = total // BLOCK
    mixed_blocks = []
    tops = []
    sums = []
    for number in range(count_blocks):
        limit = (number + 1) * BLOCK
        scores = block_scores(query_low, keys_all, segment, number, scale_factor)
        top = jnp.max(scores, axis=-1, keepdims=True)
        raised = jnp.exp(scores - top)
        summed = jnp.sum(raised, axis=-1, keepdims=True)
        shares_low = (raised / summed).astype(jnp.bfloat16)
        mixed_blocks.append(
            jnp.einsum(
                "hqk,kd->qhd", shares_low, values_all[:limit], preferred_element_type=jnp.float32
            )
        )
        tops.append(top)
        sums.append(summed)
    mixed_low = (
        jnp.concatenate(mixed_blocks, axis=0)
        .reshape(total, local_heads * head_width)
        .astype(jnp.bfloat16)
    )
    mixed_rows = mixed_low
    attention_part = lax.psum_scatter(
        jnp.dot(mixed_rows, out_weight, preferred_element_type=jnp.float32).astype(jnp.bfloat16),
        "head",
        scatter_dimension=0,
        tiled=True,
    ).astype(jnp.float32)
    middle = inputs + attention_part
    inner, second_factor = rescale(middle, feed_gain)
    inner_low = inner.astype(jnp.bfloat16)
    width = gate_weight.shape[1]
    gate_whole, up_whole = (
        lax.all_gather(gate_weight, ("batch", "head"), axis=0, tiled=True),
        lax.all_gather(up_weight, ("batch", "head"), axis=0, tiled=True),
    )
    gate = jnp.dot(inner_low, gate_whole, preferred_element_type=jnp.float32)
    up = jnp.dot(inner_low, up_whole, preferred_element_type=jnp.float32)
    sigma = jax.nn.sigmoid(gate)
    swish = gate * sigma
    hidden_low = (swish * up).astype(jnp.bfloat16)
    down_whole = lax.all_gather(down_weight, ("batch", "head"), axis=1, tiled=True)
    feed_out = jnp.dot(hidden_low, down_whole, preferred_element_type=jnp.float32)
    output = (middle + feed_out).astype(jnp.bfloat16)
    down_whole = lax.all_gather(down_weight, ("batch", "head"), axis=1, tiled=True)
    grad_hidden = jnp.einsum("rd,fd->rf", cotangent, down_whole, preferred_element_type=jnp.float32)
    slope = sigma * (1.0 + gate * (1.0 - sigma))
    grad_gate_low = (grad_hidden * up * slope).astype(jnp.bfloat16)
    grad_up_low = (grad_hidden * swish).astype(jnp.bfloat16)
    gate_whole, up_whole = (
        lax.all_gather(gate_weight, ("batch", "head"), axis=0, tiled=True),
        lax.all_gather(up_weight, ("batch", "head"), axis=0, tiled=True),
    )
    grad_inner = jnp.einsum(
        "rf,df->rd", grad_gate_low, gate_whole, preferred_element_type=jnp.float32
    ) + jnp.einsum("rf,df->rd", grad_up_low, up_whole, preferred_element_type=jnp.float32)
    feed_sums = lax.psum_scatter(
        jnp.concatenate(
            [
                jnp.einsum(
                    "rc,rf->cf", inner_low, grad_gate_low, preferred_element_type=jnp.float32
                ),
                jnp.einsum("rc,rf->cf", inner_low, grad_up_low, preferred_element_type=jnp.float32),
                jnp.einsum("rc,rf->cf", cotangent, hidden_low, preferred_element_type=jnp.float32),
            ],
            axis=1,
        ),
        ("batch", "head"),
        scatter_dimension=0,
        tiled=True,
    )
    gate_gradient = feed_sums[:, :width]
    up_gradient = feed_sums[:, width : 2 * width]
    down_gradient = feed_sums[:, 2 * width :].T
    middle_part, feed_gain_part = rescale_back(middle, second_factor, feed_gain, grad_inner)
    grad_middle = cotangent.astype(jnp.float32) + middle_part
    grad_branch_low = grad_middle.astype(jnp.bfloat16)
    piece = lax.all_gather(grad_branch_low, "head", axis=0, tiled=True)
    mixed_rows = mixed_low
    weight_total = jnp.einsum("rk,rd->kd", mixed_rows, piece, preferred_element_type=jnp.float32)
    grad_rows = jnp.einsum("rd,kd->rk", piece, out_weight, preferred_element_type=jnp.float32)
    grad_mixed_low = grad_rows.astype(jnp.bfloat16).reshape(total, local_heads, head_width)
    query_grads = []
    key_grads = jnp.zeros((total, head_width), jnp.float32)
    value_grads = jnp.zeros((total, head_width), jnp.float32)
    for number in range(count_blocks):
        begin = number * BLOCK
        limit = begin + BLOCK
        scores = block_scores(query_low, keys_all, segment, number, scale_factor)
        shares = jnp.exp(scores - tops[number]) / sums[number]
        shares_low = shares.astype(jnp.bfloat16)
        grad_block = grad_mixed_low[begin:limit]
        grad_shares = jnp.einsum(
            "qhd,kd->hqk", grad_block, values_all[:limit], preferred_element_type=jnp.float32
        )
        centre = jnp.sum(shares * grad_shares, axis=-1, keepdims=True)
        grad_scores_low = (shares * (grad_shares - centre)).astype(jnp.bfloat16)
        query_grads.append(
            jnp.einsum(
                "hqk,kd->qhd", grad_scores_low, keys_all[:limit], preferred_element_type=jnp.float32
            )
            * scale_factor
        )
        key_grads = key_grads.at[:limit].add(
            jnp.einsum(
                "hqk,qhd->kd",
                grad_scores_low,
                query_low[begin:limit],
                preferred_element_type=jnp.float32,
            )
            * scale_factor
        )
        value_grads = value_grads.at[:limit].add(
            jnp.einsum("hqk,qhd->kd", shares_low, grad_block, preferred_element_type=jnp.float32)
        )
    query_grad = rotate_back(
        jnp.concatenate(query_grads, axis=0), cosine[:, None, :], sine[:, None, :]
    )
    query_grad_low = query_grad.reshape(total, local_heads * head_width).astype(jnp.bfloat16)
    query_up_gradient = jnp.einsum(
        "rl,rk->lk", latent_all, query_grad_low, preferred_element_type=jnp.float32
    )
    latent_part = jnp.einsum(
        "rk,lk->rl", query_grad_low, query_up, preferred_element_type=jnp.float32
    )
    latent_back, key_back, value_back = (
        lax.psum_scatter(
            latent_part.astype(jnp.bfloat16), "head", scatter_dimension=0, tiled=True
        ).astype(jnp.float32),
        lax.psum_scatter(
            key_grads.astype(jnp.bfloat16), "head", scatter_dimension=0, tiled=True
        ).astype(jnp.float32),
        lax.psum_scatter(
            value_grads.astype(jnp.bfloat16), "head", scatter_dimension=0, tiled=True
        ).astype(jnp.float32),
    )
    key_grad_low = rotate_back(key_back, own_cosine, own_sine).astype(jnp.bfloat16)
    value_grad_low = value_back.astype(jnp.bfloat16)
    latent_grad, query_gain_part = rescale_back(latent, latent_factor, query_gain, latent_back)
    latent_grad_low = latent_grad.astype(jnp.bfloat16)
    grad_normed = (
        jnp.einsum("rl,dl->rd", latent_grad_low, query_down, preferred_element_type=jnp.float32)
        + jnp.einsum("rl,dl->rd", key_grad_low, key_weight, preferred_element_type=jnp.float32)
        + jnp.einsum("rl,dl->rd", value_grad_low, value_weight, preferred_element_type=jnp.float32)
    )
    query_down_part = jnp.einsum(
        "rd,rl->dl", normed_low, latent_grad_low, preferred_element_type=jnp.float32
    )
    key_part = jnp.einsum("rd,rl->dl", normed_low, key_grad_low, preferred_element_type=jnp.float32)
    value_part = jnp.einsum(
        "rd,rl->dl", normed_low, value_grad_low, preferred_element_type=jnp.float32
    )
    input_part, attention_gain_part = rescale_back(
        inputs, first_factor, attention_gain, grad_normed
    )
    input_gradient = grad_middle + input_part
    shared = lax.psum(
        (
            query_down_part,
            query_gain_part,
            key_part,
            value_part,
            attention_gain_part,
            feed_gain_part,
        ),
        ("batch", "head"),
    )
    query_up_sum, out_sum = (
        lax.psum(query_up_gradient.astype(jnp.bfloat16), "batch").astype(jnp.float32),
        lax.psum(weight_total.astype(jnp.bfloat16), "batch").astype(jnp.float32),
    )
    return (
        output,
        input_gradient,
        shared[4],
        shared[0],
        shared[1],
        query_up_sum,
        shared[2],
        shared[3],
        out_sum,
        shared[5],
        gate_gradient,
        up_gradient,
        down_gradient,
    )


def solution(mesh):
    placed = (
        P(("batch", "head"), None),
        P(),
        P(),
        P(),
        P(None, "head"),
        P(),
        P(),
        P("head", None),
        P(),
        P(("batch", "head"), None),
        P(("batch", "head"), None),
        P(None, ("batch", "head")),
        P("batch", None),
        P(("batch", "head"), None),
    )
    return jax.shard_map(
        shards,
        mesh=mesh,
        in_specs=placed,
        out_specs=(
            P(("batch", "head"), None),
            P(("batch", "head"), None),
            P(),
            P(),
            P(),
            P(None, "head"),
            P(),
            P(),
            P("head", None),
            P(),
            P(("batch", "head"), None),
            P(("batch", "head"), None),
            P(None, ("batch", "head")),
        ),
        check_vma=False,
    )
```

profile of v0, /device:TPU:0, one launch (start us, length us, event | category | flops | bytes accessed | tf_op | source)
XLA Modules:
  0.0 3112.7 jit_solution(8026342265659568289)
XLA Ops:
  10.3 3.9 multiply_reduce_fusion.3
  18.6 2.8 multiply_cosine_fusion
  27.3 13.9 all_gather.24
  43.1 18.2 all_gather.25
  64.2 4.0 fusion.112
  70.5 3.0 copy.116
  73.5 2.9 copy.115
  76.4 3.0 subtract_convert_fusion.1
  81.8 8.3 fusion.103
  90.1 5.1 fusion.108
  95.2 5.0 fusion.37
  103.8 6.2 convolution_convert_fusion.1
  111.9 75.8 %reduce-scatter.5.cloned.1.call-done = bf16[256,2048]{1,0:T(8,128)(2,1)} async-done(((bf16[1024,2048]{1,0:T(8,128)(2,1)}), bf16[256,2048]{1,0:T(8,128)(2,1)}) %reduce-scatter.5.cloned.1.call-update) | async-done | bytes 1048592 | tf_op jit(solution)/shard_map/reduce_scatter | solution.py:150
  190.9 72.7 %all-gather.8.cloned.1.call-done = bf16[2048,5632]{1,0:T(8,128)(2,1)} async-done(((bf16[64,5632]{1,0:T(8,128)(2,1)}), bf16[2048,5632]{1,0:T(8,128)(2,1)}) %all-gather.8.cloned.1.call-update) | async-done | bytes 23068688 | tf_op jit(solution)/shard_map/all_gather | solution.py:161
  263.6 13.0 fusion.113
  276.6 132.5 %all-gather.10.cloned.1.call-done = bf16[2048,5632]{1,0:T(8,128)(2,1)} async-done(((bf16[64,5632]{1,0:T(8,128)(2,1)}), bf16[2048,5632]{1,0:T(8,128)(2,1)}) %all-gather.10.cloned.1.call-update) | async-done | bytes 23068688 | tf_op jit(solution)/shard_map/all_gather | solution.py:162
  409.1 12.6 fusion.114
  421.8 132.9 %all-gather.12.cloned.1.call-done = bf16[5632,2048]{0,1:T(8,128)(2,1)} async-done(((bf16[5632,64]{0,1:T(8,128)(2,1)}), bf16[5632,2048]{0,1:T(8,128)(2,1)}) %all-gather.12.cloned.1.call-update) | async-done | bytes 23068688 | tf_op jit(solution)/shard_map/all_gather | solution.py:169
  554.7 17.1 multiply_convert_fusion
  571.8 12.5 fusion.115
  584.3 14.1 multiply_reduce_fusion
  598.9 3.9 fusion.88
  602.9 20.3 fusion.117
  623.2 30.7 all-gather.14.cloned.1.call-done
  653.9 8.0 convolution_convert_fusion.4
  673.7 2.6 fusion.4
  676.3 3.1 multiply_bitcast_fusion
  681.6 5.9 fusion.49
  687.6 3.2 add_convert_fusion
  692.3 4.0 copy.86
  696.3 5.3 convolution_convert_fusion.3
  702.8 20.5 fusion.116
  723.3 18.0 convolution_bitcast_fusion
  741.3 6.1 convolution_convert_fusion.2
  747.4 6.1 convolution_convert_fusion
  753.5 89.0 %pad_maximum_fusion = f32[2048,16896]{1,0:T(8,128)} fusion(f32[2048,5632]{1,0:T(8,128)} %convolution_bitcast_fusion, f32[2048,5632]{1,0:T(8,128)} %fusion.117, f32[2048,5632]{1,0:T(8,128)} %fusion.116), kind=kLoop, calls=%fused_computation.2 | loop fusion | flops 69206016 | bytes 276824064 | tf_op jit(solution)/shard_map/concatenate | solution.py:185
  846.9 2.9 fusion.89
  851.2 6.0 fusion.92
  858.4 12.6 fusion.14
  871.0 42.3 %all-reduce.14.cloned.1.call-done = (bf16[1024,1024]{1,0:T(8,128)(2,1)}, bf16[1024,2048]{1,0:T(8,128)(2,1)}) async-done(((bf16[1024,1024]{1,0:T(8,128)(2,1)}, bf16[1024,2048]{1,0:T(8,128)(2,1)}), (bf16[1024,1024]{1,0:T(8,128)(2,1)}, bf16[1024,2048]{1,0:T(8,128)(2,1)})) %all-reduce.14.cloned.1.call-update) | async-done | bytes 6291472 | tf_op jit(solution)/shard_map/psum | solution.py:296
  913.4 4.2 convert_element_type.158
  917.6 4.4 convert_element_type.160
  926.9 42.7 %all-reduce.3 = (f32[2048]{0:T(1024)}, f32[1024]{0:T(1024)}, f32[2048]{0:T(1024)}) all-reduce(f32[2048]{0:T(1024)S(1)} %get-tuple-element.79, f32[1024]{0:T(1024)S(1)} %get-tuple-element.81, f32[2048]{0:T(1024)S(1)} %copy-done.53), channel_id=1, replica_groups=mesh['batch'=8,'head'=4] {'batch','head'}, use_global_device_ids=true, to_apply=%region_18.19 | all-reduce | flops 5120 | bytes 40960 | tf_op jit(solution)/shard_map/psum | solution.py:284
  969.7 5.0 fusion.21
  974.7 1878.4 %all-reduce.10.cloned.1.call-done = f32[2048,16896]{1,0:T(8,128)} async-done(((f32[2048,16896]{1,0:T(8,128)}), f32[2048,16896]{1,0:T(8,128)}) %all-reduce.10.cloned.1.call-update) | async-done | bytes 138412048
  2853.1 5.1 dynamic-slice_bitcast_fusion
  2858.2 234.7 %all-reduce.12.cloned.1.call-done = (f32[2048,1024]{1,0:T(8,128)}, f32[2048,256]{1,0:T(8,128)}, f32[2048,256]{1,0:T(8,128)}) async-done(((f32[2048,1024]{1,0:T(8,128)}, f32[2048,256]{1,0:T(8,128)}, f32[2048,256]{1,0:T(8,128)}), (f32[2048,1024]{1,0:T(8,128)}, f32[2048,256]{1,0:T(8,128)}, f32[2048,256]{1,0:T(8,128)})) %all-reduce.12.cloned.1.call-update) | async-done | bytes 12582928 | tf_op jit(solution)/shard_map/psum | solution.py:284
  3092.9 8.6 copy.123
  (196 shorter events, 63.1 us)
Async XLA Ops:
  8.0 56.2 %copy-start = (bf16[1024,1024]{1,0:T(8,128)(2,1)S(1)}, bf16[1024,1024]{1,0:T(8,128)(2,1)}, u32[]{:S(2)}) copy-start(bf16[1024,1024]{1,0:T(8,128)(2,1)} %param.30) | copy-start | bytes 6291460
  8.0 56.1 %all-gather.6.cloned.1.call-start = ((), (), s32[]{:S(2)}) async-start(), calls=%async_computation.4 | async-start | bytes 2621440 | tf_op jit(solution)/shard_map/all_gather | solution.py:118
  10.3 31.0 copy-start.44
  10.3 5.2 copy-start.38
  16.4 9.1 copy-start.2
  16.4 9.1 copy-start.36
  16.4 171.3 %reduce-scatter.5.cloned.1.call-start = ((), (), s32[]{:S(2)}) async-start(), calls=%async_computation.5 | async-start | bytes 5242880 | tf_op jit(solution)/shard_map/reduce_scatter | solution.py:150
  25.5 15.8 copy-start.29
  95.1 5.0 copy-start.14
  95.1 5.0 copy-start.34
  100.9 2.9 copy-start.55
  110.1 79.4 %copy-start.40 = (f32[2048]{0:T(1024)S(1)}, f32[2048]{0:T(1024)}, u32[]{:S(2)}) copy-start(f32[2048]{0:T(1024)} %param.34) | copy-start | bytes 24580
  110.1 153.5 %all-gather.8.cloned.1.call-start = ((), (), s32[]{:S(2)}) async-start(), calls=%async_computation.6 | async-start | bytes 23789568 | tf_op jit(solution)/shard_map/all_gather | solution.py:161
  110.7 298.5 %all-gather.10.cloned.1.call-start = ((), (), s32[]{:S(2)}) async-start(), calls=%async_computation.7 | async-start | bytes 23789568 | tf_op jit(solution)/shard_map/all_gather | solution.py:162
  111.2 443.4 %all-gather.12.cloned.1.call-start = ((), (), s32[]{:S(2)}) async-start(), calls=%async_computation.8 | async-start | bytes 23789568 | tf_op jit(solution)/shard_map/all_gather | solution.py:169
  111.8 542.1 %all-gather.14.cloned.1.call-start = ((), (), s32[]{:S(2)}) async-start(), calls=%async_computation.9 | async-start | bytes 5242880 | tf_op jit(solution)/shard_map/all_gather | solution.py:205
  189.4 408.9 %copy-start.47 = (f32[256]{0:T(256)}, f32[256]{0:T(256)S(1)}, u32[]{:S(2)}) copy-start(f32[256]{0:T(256)S(1)} %get-tuple-element.118) | copy-start | bytes 3076
  189.4 408.9 %copy-start.49 = (f32[256]{0:T(256)}, f32[256]{0:T(256)S(1)}, u32[]{:S(2)}) copy-start(f32[256]{0:T(256)S(1)} %get-tuple-element.117) | copy-start | bytes 3076
  602.9 240.0 %reduce-scatter.9.cloned.1.call-start = ((), (), s32[]{:S(2)}) async-start(), calls=%async_computation.11 | async-start | bytes 655360 | tf_op jit(solution)/shard_map/reduce_scatter | solution.py:257
  653.9 8.2 copy-start.35
  662.1 8.9 copy-start.32
  665.3 3.5 copy-start.28
  666.5 4.6 slice-start
  676.3 3.1 copy-start.18
  676.3 3.1 copy-start.20
  681.5 6.0 copy-start.11
  681.5 6.0 copy-start.12
  681.5 165.3 %reduce-scatter.11.cloned.1.call-start = ((), (), s32[]{:S(2)}) async-start(), calls=%async_computation.12 | async-start | bytes 655360 | tf_op jit(solution)/shard_map/reduce_scatter | solution.py:260
  687.5 162.3 %reduce-scatter.7.cloned.1.call-start = ((), (), s32[]{:S(2)}) async-start(), calls=%async_computation.10 | async-start | bytes 2621440 | tf_op jit(solution)/shard_map/reduce_scatter | solution.py:254
  701.6 21.7 copy-start.9
  701.6 211.7 %all-reduce.14.cloned.1.call-start = ((), (), s32[]{:S(2)}) async-start(), calls=%async_computation.15 | async-start | bytes 12582912 | tf_op jit(solution)/shard_map/psum | solution.py:296
  702.8 20.5 copy-start.22
  741.3 6.1 copy-start.24
  741.3 6.1 copy-start.56
  753.5 2099.6 %all-reduce.10.cloned.1.call-start = ((), (), s32[]{:S(2)}) async-start(), calls=%async_computation.13 | async-start | bytes 276824064
  842.6 2250.2 %all-reduce.12.cloned.1.call-start = ((), (), s32[]{:S(2)}) async-start(), calls=%async_computation.14 | async-start | bytes 25165824 | tf_op jit(solution)/shard_map/psum | solution.py:284
  846.8 4.4 copy-start.46
  913.4 4.2 copy-start.16
  917.6 4.5 copy-start.13
  917.6 4.5 copy-start.21
  924.7 45.0 %copy-start.10 = (bf16[256,2048]{1,0:T(8,128)(2,1)S(1)}, bf16[256,2048]{1,0:T(8,128)(2,1)}, u32[]{:S(2)}) copy-start(bf16[256,2048]{1,0:T(8,128)(2,1)} %param.39) | copy-start | bytes 3145732
  924.7 45.0 %copy-start.41 = (f32[2048]{0:T(1024)S(1)}, f32[2048]{0:T(1024)}, u32[]{:S(2)}) copy-start(f32[2048]{0:T(1024)} %param.34) | copy-start | bytes 24580
  924.7 45.0 %copy-start.48 = (f32[256]{0:T(256)S(1)}, f32[256]{0:T(256)}, u32[]{:S(2)}) copy-start(f32[256]{0:T(256)} %copy-done.47) | copy-start | bytes 3076
  924.7 45.0 %copy-start.50 = (f32[256]{0:T(256)S(1)}, f32[256]{0:T(256)}, u32[]{:S(2)}) copy-start(f32[256]{0:T(256)} %copy-done.49) | copy-start | bytes 3076
  924.7 45.0 %copy-start.52 = (f32[256]{0:T(256)S(1)}, f32[256]{0:T(256)}, u32[]{:S(2)}) copy-start(f32[256]{0:T(256)} %copy-done.51) | copy-start | bytes 3076
  924.7 45.0 %copy-start.54 = (f32[256]{0:T(256)S(1)}, f32[256]{0:T(256)}, u32[]{:S(2)}) copy-start(f32[256]{0:T(256)} %get-tuple-element.113) | copy-start | bytes 3076
  3092.9 8.6 copy-start.26
  3101.5 3.7 copy-start.1
  (24 other events, 42.7 us)
Sparse Core Ops, SparseCore 0:
  16.5 42.2 all-gather.5
  110.2 77.4 reduce-scatter.4
  603.0 50.8 all-gather.13
  681.6 24.7 reduce-scatter.8
  709.7 24.7 reduce-scatter.10
  738.1 35.1 reduce-scatter.6
  776.9 136.3 all-reduce.13
  919.8 1933.2 all-reduce.9
  2860.1 232.7 all-reduce.11
Sparse Core Ops, SparseCore 1:
  113.8 149.7 all-gather.7
  266.8 142.3 all-gather.9
  412.3 142.3 all-gather.11
where the time goes:
time: 3120 us; the launch traced here: 3110 us
  waiting for transfers between devices  2600 us (83%)
  matrix products  235 us (8%)
  other arithmetic  138 us (4%)
  blocking collectives  74.9 us (2%)
  local copies, waits for them, and re-layouts  45.9 us (1%)
    unnamed x13, waiting for transfers between devices  1880 us
    psum x1, waiting for transfers between devices, shards(): lax.psum((query_down_part, query_gain_part, key_part, value_part, attenti...  235 us
    all_gather x1, waiting for transfers between devices, shards(): lax.all_gather(down_weight, ('batch', 'head'), axis=1, tiled=True)  133 us
    all_gather x1, waiting for transfers between devices, shards(): lax.all_gather(up_weight, ('batch', 'head'), axis=0, tiled=True)  133 us
    concatenate x1, other arithmetic, shards(): jnp.concatenate([jnp.einsum('rc,rf->cf', inner_low, grad_gate_low, prefer...  89 us
    reduce_scatter x1, waiting for transfers between devices, shards(): lax.psum_scatter(jnp.dot(mixed_rows, out_weight, preferred_element_type=j...  75.8 us
    all_gather x1, waiting for transfers between devices, shards(): lax.all_gather(gate_weight, ('batch', 'head'), axis=0, tiled=True)  72.7 us
  transfers between devices with their start and end apart: 12, of which 8 were waited for; matrix products, arithmetic and copies ran while one was open for 9% of the time, Pallas kernels for 0%

commit v1 on v0

v1 whole, which is shorter than its diff:
```python
import math

import jax
import jax.numpy as jnp
from jax import lax
from jax.sharding import PartitionSpec as P

epsilon = 1e-05
masked_value = -1e30
low = jnp.bfloat16


def dot(left, right, contract=(1, 0)):
    return lax.dot_general(
        left,
        right,
        (((contract[0],), (contract[1],)), ((), ())),
        preferred_element_type=jnp.float32,
    )


def rescale(values, gain):
    factor = lax.rsqrt(jnp.mean(values * values, axis=-1, keepdims=True) + epsilon)
    return (values * factor * gain, factor)


def rescale_back(values, factor, gain, upstream):
    weighted = upstream * gain
    inner_mean = jnp.mean(values * weighted, axis=-1, keepdims=True)
    back = factor * weighted - values * (factor * factor * factor) * inner_mean
    return (back, jnp.sum(upstream * values * factor, axis=0))


def rotate(values, cosine, sine):
    half = values.shape[-1] // 2
    first = values[..., :half]
    second = values[..., half:]
    return jnp.concatenate(
        [first * cosine - second * sine, second * cosine + first * sine], axis=-1
    )


def rotate_back(grads, cosine, sine):
    return rotate(grads, cosine, -sine)


def swap(values, axis, bit):
    size = lax.axis_size(axis)
    return lax.ppermute(values, axis, [(i, i ^ bit) for i in range(size)])


def gather_near(own):
    size = lax.axis_size("head")
    if size == 4:
        cut = own.shape[0] // 2
        first, second = swap(own, "head", 1), swap(own, "head", 2)
        third = jnp.concatenate(
            [swap(first[:cut], "head", 2), swap(second[cut:], "head", 1)], axis=0
        )
        return [own, first, second, third]
    blocks = [own]
    bit = 1
    while bit < size:
        blocks = blocks + [swap(block, "head", bit) for block in blocks]
        bit *= 2
    return blocks


def scatter_near(parts):
    size = len(parts)
    if size == 4:
        cut = parts[0].shape[0] // 2
        via_first = swap(parts[3][:cut], "head", 1)
        via_second = swap(parts[3][cut:], "head", 2)
        second = jnp.concatenate([parts[2][:cut] + via_first, parts[2][cut:]], axis=0)
        first = jnp.concatenate([parts[1][:cut], parts[1][cut:] + via_second], axis=0)
        return (
            parts[0].astype(jnp.float32)
            + swap(first, "head", 1).astype(jnp.float32)
            + swap(second, "head", 2).astype(jnp.float32)
        )
    bit = size // 2
    while bit:
        parts = [parts[k] + swap(parts[k + bit], "head", bit) for k in range(bit)]
        bit //= 2
    return parts[0].astype(jnp.float32)


def spread(pieces):
    return [pieces[0]] + [swap(pieces[k], "head", k) for k in range(1, len(pieces))]


def shards(
    tokens,
    attention_gain,
    query_down,
    query_gain,
    query_up,
    key_weight,
    value_weight,
    out_weight,
    feed_gain,
    gate_weight,
    up_weight,
    down_weight,
    lengths,
    cotangent,
):
    rows, width = tokens.shape
    count = lax.axis_size("head")
    me = lax.axis_index("head")
    total = rows * count
    head_width = key_weight.shape[1]
    local_heads = query_up.shape[1] // head_width
    rank = query_up.shape[0]
    scale_factor = 1.0 / math.sqrt(head_width)
    feed = gate_weight.shape[1]
    feed_part = feed // count
    strip = gate_weight.shape[0]

    stacked = jnp.stack([gate_weight, up_weight, down_weight.T])
    pieces = [
        lax.dynamic_slice_in_dim(stacked, (me ^ k) * feed_part, feed_part, 2) for k in range(count)
    ]
    arrived = spread(pieces)
    columns = jnp.zeros((3, strip * count, feed_part), low)
    for k in range(count):
        columns = lax.dynamic_update_slice(columns, arrived[k], (0, (me ^ k) * strip, 0))
    gate_whole, up_whole, down_whole = (
        lax.all_gather(columns[i], "batch", axis=0, tiled=True) for i in range(3)
    )

    bounds = jnp.cumsum(lengths.reshape(-1), dtype=jnp.int32)
    index = jnp.concatenate(
        [(me ^ k) * rows + jnp.arange(rows, dtype=jnp.int32) for k in range(count)]
    )
    segment = (index >= bounds[0]).astype(jnp.int32) + (index >= bounds[1]).astype(jnp.int32)
    begin = jnp.where(segment == 0, 0, jnp.where(segment == 1, bounds[0], bounds[1]))
    half = head_width // 2
    rates = 10000.0 ** (-2.0 * jnp.arange(half, dtype=jnp.float32) / head_width)
    turns = (index - begin).astype(jnp.float32)[:, None] * rates[None, :]
    cosine, sine = jnp.cos(turns), jnp.sin(turns)
    own_cosine, own_sine = cosine[:rows], sine[:rows]
    allowed = (segment[:, None] == segment[None, :]) & (index[None, :] <= index[:, None])

    inputs = tokens.astype(jnp.float32)
    normed, first_factor = rescale(inputs, attention_gain)
    normed_low = normed.astype(low)
    latent = dot(normed_low, query_down)
    latent_in, latent_factor = rescale(latent, query_gain)
    key_own = rotate(dot(normed_low, key_weight), own_cosine, own_sine).astype(low)
    value_own = dot(normed_low, value_weight).astype(low)
    lkv = jnp.concatenate(
        gather_near(jnp.concatenate([latent_in.astype(low), key_own, value_own], axis=1)), axis=0
    )
    latent_all = lkv[:, :rank]
    keys_all = lkv[:, rank : rank + head_width]
    values_all = lkv[:, rank + head_width :]

    query_raw = dot(latent_all, query_up).reshape(total, local_heads, head_width)
    query_low = rotate(query_raw, cosine[:, None, :], sine[:, None, :]).astype(low)
    scores = (
        jnp.einsum("qhd,kd->hqk", query_low, keys_all, preferred_element_type=jnp.float32)
        * scale_factor
    )
    scores = jnp.where(allowed[None], scores, masked_value)
    top = jnp.max(scores, axis=-1, keepdims=True)
    raised = jnp.exp(scores - top)
    summed = jnp.sum(raised, axis=-1, keepdims=True)
    shares = raised / summed
    shares_low = shares.astype(low)
    mixed_low = (
        jnp.einsum("hqk,kd->qhd", shares_low, values_all, preferred_element_type=jnp.float32)
        .astype(low)
        .reshape(total, local_heads * head_width)
    )
    attention_partial = dot(mixed_low, out_weight).astype(low)
    attention_part = scatter_near(
        [attention_partial[k * rows : (k + 1) * rows] for k in range(count)]
    )
    middle = inputs + attention_part
    inner, second_factor = rescale(middle, feed_gain)
    inner_all = jnp.concatenate(gather_near(inner.astype(low)), axis=0)
    cotangent_all = jnp.concatenate(gather_near(cotangent), axis=0)
    gate = dot(inner_all, gate_whole)
    up = dot(inner_all, up_whole)
    sigma = jax.nn.sigmoid(gate)
    swish = gate * sigma
    hidden_low = (swish * up).astype(low)
    feed_partial = dot(hidden_low, down_whole, (1, 1)).astype(low)
    feed_out = scatter_near([feed_partial[k * rows : (k + 1) * rows] for k in range(count)])
    output = (middle + feed_out).astype(low)

    grad_hidden = dot(cotangent_all, down_whole)
    slope = sigma * (1.0 + gate * (1.0 - sigma))
    grad_gate_low = (grad_hidden * up * slope).astype(low)
    grad_up_low = (grad_hidden * swish).astype(low)
    grad_inner_partial = (
        dot(grad_gate_low, gate_whole, (1, 1)) + dot(grad_up_low, up_whole, (1, 1))
    ).astype(low)
    grad_inner = scatter_near(
        [grad_inner_partial[k * rows : (k + 1) * rows] for k in range(count)]
    )
    sums = [
        lax.psum_scatter(dot(a, b, (0, 0)).astype(low), "batch", scatter_dimension=0, tiled=True)
        for a, b in (
            (cotangent_all, hidden_low),
            (inner_all, grad_gate_low),
            (inner_all, grad_up_low),
        )
    ]
    summed_weights = jnp.stack([sums[1], sums[2], sums[0]])
    pieces = [
        lax.dynamic_slice_in_dim(summed_weights, (me ^ k) * strip, strip, 1) for k in range(count)
    ]
    arrived = spread(pieces)
    feed_gradients = jnp.zeros((3, strip, feed), jnp.float32)
    for k in range(count):
        feed_gradients = lax.dynamic_update_slice(
            feed_gradients, arrived[k].astype(jnp.float32), (0, 0, (me ^ k) * feed_part)
        )

    middle_part, feed_gain_part = rescale_back(middle, second_factor, feed_gain, grad_inner)
    grad_middle = cotangent.astype(jnp.float32) + middle_part
    branch_all = jnp.concatenate(gather_near(grad_middle.astype(low)), axis=0)
    out_gradient = lax.psum(dot(mixed_low, branch_all, (0, 0)).astype(low), "batch")
    grad_mixed_low = dot(branch_all, out_weight, (1, 1)).astype(low).reshape(
        total, local_heads, head_width
    )
    grad_shares = jnp.einsum(
        "qhd,kd->hqk", grad_mixed_low, values_all, preferred_element_type=jnp.float32
    )
    centre = jnp.sum(shares * grad_shares, axis=-1, keepdims=True)
    grad_scores_low = (shares * (grad_shares - centre)).astype(low)
    query_grad = (
        jnp.einsum("hqk,kd->qhd", grad_scores_low, keys_all, preferred_element_type=jnp.float32)
        * scale_factor
    )
    key_grads = (
        jnp.einsum("hqk,qhd->kd", grad_scores_low, query_low, preferred_element_type=jnp.float32)
        * scale_factor
    )
    value_grads = jnp.einsum(
        "hqk,qhd->kd", shares_low, grad_mixed_low, preferred_element_type=jnp.float32
    )
    query_grad_low = (
        rotate_back(query_grad, cosine[:, None, :], sine[:, None, :])
        .astype(low)
        .reshape(total, local_heads * head_width)
    )
    latent_partial = dot(query_grad_low, query_up, (1, 1))
    lkv_partial = jnp.concatenate([latent_partial, key_grads, value_grads], axis=1).astype(low)
    query_up_gradient = lax.psum(dot(latent_all, query_grad_low, (0, 0)).astype(low), "batch")
    lkv_back = scatter_near([lkv_partial[k * rows : (k + 1) * rows] for k in range(count)])
    latent_grad, query_gain_part = rescale_back(
        latent, latent_factor, query_gain, lkv_back[:, :rank]
    )
    key_back = rotate_back(lkv_back[:, rank : rank + head_width], own_cosine, own_sine)
    lkv_grad_low = jnp.concatenate(
        [latent_grad, key_back, lkv_back[:, rank + head_width :]], axis=1
    ).astype(low)

    slice_width = width // count
    normed_slices = jnp.concatenate(
        spread(
            [
                lax.dynamic_slice_in_dim(normed_low, (me ^ k) * slice_width, slice_width, 1)
                for k in range(count)
            ]
        ),
        axis=0,
    )
    lkv_grad_all = jnp.concatenate(gather_near(lkv_grad_low), axis=0)
    shared_part = dot(normed_slices, lkv_grad_all, (0, 0)).astype(low)
    shared_sum = lax.psum(shared_part, "batch")
    shared_all = lax.all_gather(shared_sum, "head", axis=0, tiled=True).astype(jnp.float32)

    grad_normed = (
        dot(lkv_grad_low[:, :rank], query_down, (1, 1))
        + dot(lkv_grad_low[:, rank : rank + head_width], key_weight, (1, 1))
        + dot(lkv_grad_low[:, rank + head_width :], value_weight, (1, 1))
    )
    input_part, attention_gain_part = rescale_back(
        inputs, first_factor, attention_gain, grad_normed
    )
    input_gradient = grad_middle + input_part
    gains = lax.psum(
        jnp.concatenate([attention_gain_part, feed_gain_part, query_gain_part]), ("batch", "head")
    )
    return (
        output,
        input_gradient,
        gains[:width],
        shared_all[:, :rank],
        gains[2 * width :],
        query_up_gradient.astype(jnp.float32),
        shared_all[:, rank : rank + head_width],
        shared_all[:, rank + head_width :],
        out_gradient.astype(jnp.float32),
        gains[width : 2 * width],
        feed_gradients[0],
        feed_gradients[1],
        feed_gradients[2].T,
    )


def solution(mesh):
    rows = P(("batch", "head"), None)
    columns = P(None, ("batch", "head"))
    return jax.shard_map(
        shards,
        mesh=mesh,
        in_specs=(
            rows,
            P(),
            P(),
            P(),
            P(None, "head"),
            P(),
            P(),
            P("head", None),
            P(),
            rows,
            rows,
            columns,
            P("batch", None),
            rows,
        ),
        out_specs=(
            rows,
            rows,
            P(),
            P(),
            P(),
            P(None, "head"),
            P(),
            P(),
            P("head", None),
            P(),
            rows,
            rows,
            columns,
        ),
        check_vma=False,
    )
```

time: 3120 us -> 1030 us (0.33)
  waiting for transfers between devices: 2600 us -> 586 us
  other arithmetic: 138 us -> 61.1 us
  starting transfers between devices: 0.67 us -> 51.4 us
    unnamed x13 -> x8, waiting for transfers between devices: 1880 us -> 0.13 us
    all_gather x5 -> x4, waiting for transfers between devices: 369 us -> 0.01 us  [the longest x3 0.01 us: shards(): lax.all_gather(columns[i], 'batch', axis=0, tiled=True)]
    ppermute x0 -> x45, waiting for transfers between devices: none -> 263 us  [swap(): return lax.ppermute(values, axis, [(i, i ^ bit) for i in range(size)])]
    psum x2 -> x1, waiting for transfers between devices: 277 us -> 133 us  [shards(): shared_sum = lax.psum(shared_part, 'batch')]
    reduce_scatter x4 -> x3, waiting for transfers between devices: 75.9 us -> 190 us  [shards(): lax.psum_scatter(dot(a, b, (0, 0)).astype(low), 'batch', scatter_dimensio...]
    concatenate x3 -> x11, other arithmetic: 90.9 us -> 1.17 us  [the longest x4 0.42 us: scatter_near(): jnp.concatenate([parts[1][:cut], parts[1][cut:] + via_second], axis=0)]
    ppermute x0 -> x45, starting transfers between devices: none -> 50.5 us  [swap(): return lax.ppermute(values, axis, [(i, i ^ bit) for i in range(size)])]
    all_gather x2 -> x0, blocking collectives: 32.2 us -> none  [the longest x1 18.2 us: shards(): lax.all_gather(key_low, 'head', axis=0, tiled=True)]
  transfers between devices with their start and end apart: 12 -> 53, of which waited for: 8 -> 36; matrix products, arithmetic and copies ran while one was open for 9% -> 20% of each run, Pallas kernels for 0% -> 0%
where the time goes in v1:
time: 1030 us
  waiting for transfers between devices  586 us (57%)
  matrix products  210 us (20%)
  other arithmetic  61.1 us (6%)
  local copies, waits for them, and re-layouts  53 us (5%)
  blocking collectives  52.8 us (5%)
  starting transfers between devices  51.4 us (5%)
  between operations  15.6 us (2%)
    ppermute x45, waiting for transfers between devices, swap(): return lax.ppermute(values, axis, [(i, i ^ bit) for i in range(size)])  263 us
    reduce_scatter x3, waiting for transfers between devices, shards(): lax.psum_scatter(dot(a, b, (0, 0)).astype(low), 'batch', scatter_dimensio...  190 us
    dot_general x22, matrix products, dot(): lax.dot_general(left, right, (((contract[0],), (contract[1],)), ((), ()))...  161 us
    psum x1, waiting for transfers between devices, shards(): shared_sum = lax.psum(shared_part, 'batch')  133 us
    psum x1, blocking collectives, shards(): lax.psum(jnp.concatenate([attention_gain_part, feed_gain_part, query_gain...  52.8 us
    ppermute x45, starting transfers between devices, swap(): return lax.ppermute(values, axis, [(i, i ^ bit) for i in range(size)])  50.5 us
  transfers between devices with their start and end apart: 53, of which 36 were waited for; matrix products, arithmetic and copies ran while one was open for 20% of the time, Pallas kernels for 0%

profile of v1, /device:TPU:0, one launch (start us, length us, event | category | flops | bytes accessed | tf_op | source)
XLA Modules:
  0.0 1030.0 jit_solution(11552646435010576515)
XLA Ops:
  16.4 11.8 %collective-permute-done.12 = bf16[3,64,1408]{2,1,0:T(8,128)(2,1)S(1)} collective-permute-done((bf16[3,64,1408]{2,1,0:T(8,128)(2,1)}, bf16[3,64,1408]{2,1,0:T(8,128)(2,1)S(1)}, u32[]{:S(2)}, u32[]{:S(2)}) %collective-permute-start.12) | collective-permute-done | bytes 540704 | tf_op jit(solution)/shard_map/ppermute | solution.py:49
  29.0 11.4 %collective-permute-done.13 = bf16[3,64,1408]{2,1,0:T(8,128)(2,1)S(1)} collective-permute-done((bf16[3,64,1408]{2,1,0:T(8,128)(2,1)}, bf16[3,64,1408]{2,1,0:T(8,128)(2,1)S(1)}, u32[]{:S(2)}, u32[]{:S(2)}) %collective-permute-start.13) | collective-permute-done | bytes 540704 | tf_op jit(solution)/shard_map/ppermute | solution.py:49
  48.2 4.8 multiply_reduce_fusion.5
  67.5 11.8 %collective-permute-done = bf16[256,1536]{1,0:T(8,128)(2,1)S(1)} collective-permute-done((bf16[256,1536]{1,0:T(8,128)(2,1)S(1)}, bf16[256,1536]{1,0:T(8,128)(2,1)S(1)}, u32[]{:S(2)}, u32[]{:S(2)}) %collective-permute-start) | collective-permute-done | bytes 786464 | tf_op jit(solution)/shard_map/ppermute | solution.py:49
  82.2 6.7 collective-permute-done.2
  100.4 4.3 subtract_convert_fusion.1
  104.7 11.1 %fusion.97 = (f32[4,1024]{1,0:T(4,128)S(1)}, f32[4,1024,1024]{1,2,0:T(8,128)}) fusion(pred[1024,1024]{0,1:T(8,128)(4,1)} %compare_and_fusion, bf16[1024,4,128]{2,0,1:T(8,128)(2,1)} %get-tuple-element.37, bf16[1024,4,128]{2,0,1:T(8,128)(2,1)} %get-tuple-element.36, bf16[1024,1536]{1,0:T(8,128)(2,1)} %copy-done.38), kind=kOutput, calls=%fused_computation.231 | convolution fusion | flops 2168456192 | bytes 20463616 | tf_op jit(solution)/shard_map/sub | solution.py:168
  115.8 9.0 fusion.39
  124.8 16.9 %convolution_convert_fusion.4 = bf16[1024,2048]{1,0:T(8,128)(2,1)S(1)} fusion(bf16[1024,1024]{0,1:T(8,128)(2,1)S(1)} %bitcast.148, bf16[1024,2048]{1,0:T(8,128)(2,1)S(1)} %copy-done.53), kind=kOutput, calls=%fused_computation.48 | convolution fusion | flops 4297064448 | bytes 10485760 | tf_op jit(solution)/shard_map/dot_general | solution.py:14
  147.2 9.3 collective-permute-done.4
  162.8 21.9 %collective-permute-done.5 = bf16[256,2048]{1,0:T(8,128)(2,1)S(1)} collective-permute-done((bf16[256,2048]{1,0:T(8,128)(2,1)S(1)}, bf16[256,2048]{1,0:T(8,128)(2,1)S(1)}, u32[]{:S(2)}, u32[]{:S(2)}) %collective-permute-start.5) | collective-permute-done | bytes 1048608 | tf_op jit(solution)/shard_map/ppermute | solution.py:49
  190.3 16.8 %collective-permute-done.19 = bf16[256,2048]{1,0:T(8,128)(2,1)S(1)} collective-permute-done((bf16[256,2048]{1,0:T(8,128)(2,1)S(1)}, bf16[256,2048]{1,0:T(8,128)(2,1)S(1)}, u32[]{:S(2)}, u32[]{:S(2)}) %collective-permute-start.19) | collective-permute-done | bytes 1048608 | tf_op jit(solution)/shard_map/ppermute | solution.py:49
  210.6 11.5 %collective-permute-done.21 = bf16[128,2048]{1,0:T(8,128)(2,1)S(1)} collective-permute-done((bf16[128,2048]{1,0:T(8,128)(2,1)S(1)}, bf16[128,2048]{1,0:T(8,128)(2,1)S(1)}, u32[]{:S(2)}, u32[]{:S(2)}) %collective-permute-start.21) | collective-permute-done | bytes 524320 | tf_op jit(solution)/shard_map/ppermute | solution.py:49
  222.1 7.4 collective-permute-done.8
  231.2 6.7 collective-permute-done.22
  251.9 11.7 %fusion.14 = f32[1024,1408]{1,0:T(8,128)} fusion(bf16[1024,2048]{1,0:T(8,128)(2,1)} %constant_dynamic-update-slice_fusion.5, bf16[1,2048,1408]{2,1,0:T(8,128)(2,1)} %all-gather.12.cloned.1.call-done), kind=kOutput, calls=%fused_computation.23 | convolution fusion | flops 5905580032 | bytes 15728640 | tf_op jit(solution)/shard_map/dot_general | solution.py:14
  263.6 11.7 %fusion.8 = f32[1024,1408]{1,0:T(8,128)} fusion(bf16[1024,2048]{1,0:T(8,128)(2,1)} %copy-done.37, bf16[1,2048,1408]{2,1,0:T(8,128)(2,1)} %all-gather.14.cloned.1.call-done), kind=kOutput, calls=%fused_computation.17 | convolution fusion | flops 5905580032 | bytes 15728640 | tf_op jit(solution)/shard_map/dot_general | solution.py:14
  275.3 16.0 %multiply_convert_fusion.1 = (bf16[1024,1408]{1,0:T(8,128)(2,1)}, bf16[1024,1408]{1,0:T(8,128)(2,1)S(1)}, bf16[1024,1408]{1,0:T(8,128)(2,1)S(1)}) fusion(f32[1024,1408]{1,0:T(8,128)} %fusion.8, f32[1024,1408]{1,0:T(8,128)} %fusion.14, bf16[1024,2048]{1,0:T(8,128)(2,1)} %constant_dynamic-update-slice_fusion.5, ...), kind=kOutput, calls=%fused_computation.30 | convolution fusion | flops 5927206912 | bytes 30146560 | tf_op jit(solution)/shard_map/dot_general | solution.py:14
  292.9 6.9 fusion.25
  303.3 10.8 %fusion.12 = f32[1024,2048]{1,0:T(8,128)} fusion(bf16[1024,1408]{1,0:T(8,128)(2,1)S(1)} %get-tuple-element.30, bf16[1,2048,1408]{2,1,0:T(8,128)(2,1)} %all-gather.12.cloned.1.call-done), kind=kOutput, calls=%fused_computation.21 | convolution fusion | flops 5905580032 | bytes 17039360 | tf_op jit(solution)/shard_map/dot_general | solution.py:14
  314.2 10.4 %add_convert_fusion = bf16[1024,2048]{1,0:T(8,128)(2,1)S(1)} fusion(f32[1024,2048]{1,0:T(8,128)} %fusion.12, bf16[1024,1408]{1,0:T(8,128)(2,1)} %get-tuple-element.29, bf16[1,2048,1408]{2,1,0:T(8,128)(2,1)S(1)} %bitcast.146), kind=kOutput, calls=%fused_computation.9 | convolution fusion | flops 5909774336 | bytes 21233664 | tf_op jit(solution)/shard_map/dot_general | solution.py:14
  329.4 10.3 %collective-permute-done.23 = bf16[128,2048]{1,0:T(8,128)(2,1)S(1)} collective-permute-done((bf16[128,2048]{1,0:T(8,128)(2,1)S(1)}, bf16[128,2048]{1,0:T(8,128)(2,1)S(1)}, u32[]{:S(2)}, u32[]{:S(2)}) %collective-permute-start.23) | collective-permute-done | bytes 524320 | tf_op jit(solution)/shard_map/ppermute | solution.py:49
  342.6 19.6 %collective-permute-done.16 = bf16[256,2048]{1,0:T(8,128)(2,1)S(1)} collective-permute-done((bf16[256,2048]{1,0:T(8,128)(2,1)S(1)}, bf16[256,2048]{1,0:T(8,128)(2,1)S(1)}, u32[]{:S(2)}, u32[]{:S(2)}) %collective-permute-start.16) | collective-permute-done | bytes 1048608 | tf_op jit(solution)/shard_map/ppermute | solution.py:49
  362.2 14.2 %collective-permute-done.24 = bf16[256,2048]{1,0:T(8,128)(2,1)S(1)} collective-permute-done((bf16[256,2048]{1,0:T(8,128)(2,1)S(1)}, bf16[256,2048]{1,0:T(8,128)(2,1)S(1)}, u32[]{:S(2)}, u32[]{:S(2)}) %collective-permute-start.24) | collective-permute-done | bytes 1048608 | tf_op jit(solution)/shard_map/ppermute | solution.py:49
  384.3 18.2 %collective-permute-done.27 = bf16[256,2048]{1,0:T(8,128)(2,1)S(1)} collective-permute-done((bf16[256,2048]{1,0:T(8,128)(2,1)S(1)}, bf16[256,2048]{1,0:T(8,128)(2,1)S(1)}, u32[]{:S(2)}, u32[]{:S(2)}) %collective-permute-start.27) | collective-permute-done | bytes 1048608 | tf_op jit(solution)/shard_map/ppermute | solution.py:49
  407.0 4.8 collective-permute-done.29
  414.6 8.1 convolution_convert_fusion.8
  422.7 10.2 fusion.1
  432.9 10.7 %fusion.3 = bf16[4,1024,1024]{1,2,0:T(8,128)(2,1)} fusion(f32[1024,1024,4]{1,0,2:T(8,128)} %get-tuple-element.108, f32[4,1024]{1,0:T(4,128)S(1)} %get-tuple-element.107, f32[4,1024,1024]{1,2,0:T(8,128)S(1)} %bitcast.135, f32[4,1024]{1,0:T(4,128)S(1)} %get-tuple-element.105), kind=kLoop, calls=%fused_computation.5 | loop fusion | flops 16777216 | bytes 41975808 | tf_op jit(solution)/shard_map/convert_element_type | solution.py:234
  443.6 7.3 multiply_bitcast_fusion
  451.0 6.5 fusion.57
  457.5 4.9 fusion.58
  473.7 13.5 %collective-permute-done.31 = bf16[128,1536]{1,0:T(8,128)(2,1)S(1)} collective-permute-done((bf16[128,1536]{1,0:T(8,128)(2,1)S(1)}, bf16[128,1536]{1,0:T(8,128)(2,1)S(1)}, u32[]{:S(2)}, u32[]{:S(2)}) %collective-permute-start.31) | collective-permute-done | bytes 393248 | tf_op jit(solution)/shard_map/ppermute | solution.py:49
  491.7 4.3 collective-permute-done.33
  503.6 15.6 %collective-permute-done.32 = bf16[256,1536]{1,0:T(8,128)(2,1)S(1)} collective-permute-done((bf16[256,1536]{1,0:T(8,128)(2,1)S(1)}, bf16[256,1536]{1,0:T(8,128)(2,1)S(1)}, u32[]{:S(2)}, u32[]{:S(2)}) %collective-permute-start.32) | collective-permute-done | bytes 786464 | tf_op jit(solution)/shard_map/ppermute | solution.py:49
  523.8 8.2 convolution_convert_fusion.3
  536.1 5.5 collective-permute-done.40
  545.6 11.5 %convolution_convert_fusion.2 = bf16[2048,1408]{1,0:T(8,128)(2,1)} fusion(bf16[1024,2048]{1,0:T(8,128)(2,1)} %constant_dynamic-update-slice_fusion.5, bf16[1024,1408]{1,0:T(8,128)(2,1)} %get-tuple-element.29), kind=kOutput, calls=%fused_computation.16 | convolution fusion | flops 5908463616 | bytes 12845056 | tf_op jit(solution)/shard_map/dot_general | solution.py:14
  557.1 11.1 %convolution_convert_fusion.1 = bf16[2048,1408]{1,0:T(8,128)(2,1)} fusion(bf16[1024,2048]{1,0:T(8,128)(2,1)} %constant_dynamic-update-slice_fusion.5, bf16[1024,1408]{1,0:T(8,128)(2,1)} %copy-done.58), kind=kOutput, calls=%fused_computation.15 | convolution fusion | flops 5908463616 | bytes 12845056 | tf_op jit(solution)/shard_map/dot_general | solution.py:14
  568.3 11.0 %convolution_convert_fusion = bf16[2048,1408]{1,0:T(8,128)(2,1)} fusion(bf16[1024,2048]{1,0:T(8,128)(2,1)} %copy-done.37, bf16[1024,1408]{1,0:T(8,128)(2,1)} %copy-done.59), kind=kOutput, calls=%fused_computation.14 | convolution fusion | flops 5908463616 | bytes 12845056 | tf_op jit(solution)/shard_map/dot_general | solution.py:14
  579.5 133.1 %all-reduce.3.cloned.1.call-done = (bf16[512,1536]{1,0:T(8,128)(2,1)}, bf16[1024,1024]{1,0:T(8,128)(2,1)}, bf16[1024,2048]{1,0:T(8,128)(2,1)}) async-done(((bf16[512,1536]{1,0:T(8,128)(2,1)}, bf16[1024,1024]{1,0:T(8,128)(2,1)}, bf16[1024,2048]{1,0:T(8,128)(2,1)}), (bf16[512,1536]{1,0:T(8,128)(2,1)}, bf16[1024,1024]{1,0:T(8,128)(2,1)}, bf16[1024,2048]{1,0:T(8,128)(2,1)})) %all-reduce.3.cloned.1.call-update) | async-done | bytes 7864336 | tf_op jit(solution)/shard_map/psum | solution.py:275
  721.8 58.0 %reduce-scatter.4.cloned.1.call-done = bf16[256,1408]{1,0:T(8,128)(2,1)} async-done(((bf16[2048,1408]{1,0:T(8,128)(2,1)}), bf16[256,1408]{1,0:T(8,128)(2,1)}) %reduce-scatter.4.cloned.1.call-update) | async-done | bytes 720912 | tf_op jit(solution)/shard_map/reduce_scatter | solution.py:205
  779.7 66.0 %reduce-scatter.6.cloned.1.call-done = bf16[256,1408]{1,0:T(8,128)(2,1)} async-done(((bf16[2048,1408]{1,0:T(8,128)(2,1)}), bf16[256,1408]{1,0:T(8,128)(2,1)}) %reduce-scatter.6.cloned.1.call-update) | async-done | bytes 720912 | tf_op jit(solution)/shard_map/reduce_scatter | solution.py:205
  845.7 66.2 %reduce-scatter.8.cloned.1.call-done = bf16[256,1408]{1,0:T(8,128)(2,1)} async-done(((bf16[2048,1408]{1,0:T(8,128)(2,1)}), bf16[256,1408]{1,0:T(8,128)(2,1)}) %reduce-scatter.8.cloned.1.call-update) | async-done | bytes 720912 | tf_op jit(solution)/shard_map/reduce_scatter | solution.py:205
  917.4 52.8 %psum.28 = f32[5120]{0:T(1024)S(1)} all-reduce(f32[5120]{0:T(1024)S(1)} %pad_maximum_fusion.22), channel_id=1, replica_groups=mesh['batch'=8,'head'=4] {'batch','head'}, use_global_device_ids=true, to_apply=%region_13.14 | all-reduce | flops 5120 | bytes 40960 | tf_op jit(solution)/shard_map/psum | solution.py:287
  971.4 6.8 convert_element_type.216
  987.4 24.0 %collective-permute-done.43 = bf16[3,64,1408]{2,1,0:T(8,128)(2,1)S(1)} collective-permute-done((bf16[3,64,1408]{2,1,0:T(8,128)(2,1)S(1)}, bf16[3,64,1408]{2,1,0:T(8,128)(2,1)S(1)}, u32[]{:S(2)}, u32[]{:S(2)}) %collective-permute-start.43) | collective-permute-done | bytes 540704 | tf_op jit(solution)/shard_map/ppermute | solution.py:49
  1013.8 6.8 slice.370
  (339 shorter events, 176.4 us)
Async XLA Ops:
  7.2 244.7 %all-gather.12.cloned.1.call-start = ((), (), s32[]{:S(2)}) async-start(), calls=%async_computation.8 | async-start | bytes 6488064 | tf_op jit(solution)/shard_map/all_gather | solution.py:130
  11.9 16.2 %collective-permute-start.12 = (bf16[3,64,1408]{2,1,0:T(8,128)(2,1)}, bf16[3,64,1408]{2,1,0:T(8,128)(2,1)S(1)}, u32[]{:S(2)}, u32[]{:S(2)}) collective-permute-start(bf16[3,64,1408]{2,1,0:T(8,128)(2,1)} %get-tuple-element.75), channel_id=1, source_target_pairs={{0,1},{1,0},{2,3},{3,2},{4,5},{5,4},{6,7},{7,6},{8,9},{9,8},{10,11... | collective-permute-start | bytes 1622024 | tf_op jit(solution)/shard_map/ppermute | solution.py:49
  14.8 25.5 %collective-permute-start.13 = (bf16[3,64,1408]{2,1,0:T(8,128)(2,1)}, bf16[3,64,1408]{2,1,0:T(8,128)(2,1)S(1)}, u32[]{:S(2)}, u32[]{:S(2)}) collective-permute-start(bf16[3,64,1408]{2,1,0:T(8,128)(2,1)} %get-tuple-element.74), channel_id=1, source_target_pairs={{0,2},{1,3},{2,0},{3,1},{4,6},{5,7},{6,4},{7,5},{8,10},{9,11},{10,... | collective-permute-start | bytes 1622024 | tf_op jit(solution)/shard_map/ppermute | solution.py:49
  16.4 24.9 %collective-permute-start.14 = (bf16[3,64,1408]{2,1,0:T(8,128)(2,1)}, bf16[3,64,1408]{2,1,0:T(8,128)(2,1)}, u32[]{:S(2)}, u32[]{:S(2)}) collective-permute-start(bf16[3,64,1408]{2,1,0:T(8,128)(2,1)} %get-tuple-element.73), channel_id=1, source_target_pairs={{0,3},{1,2},{2,1},{3,0},{4,7},{5,6},{6,5},{7,4},{8,11},{9,10},{10,... | collective-permute-start | bytes 1622024 | tf_op jit(solution)/shard_map/ppermute | solution.py:49
  46.2 217.4 %all-gather.14.cloned.1.call-start = ((), (), s32[]{:S(2)}) async-start(), calls=%async_computation.9 | async-start | bytes 6488064 | tf_op jit(solution)/shard_map/all_gather | solution.py:130
  53.1 222.2 %all-gather.10.cloned.1.call-start = ((), (), s32[]{:S(2)}) async-start(), calls=%async_computation.7 | async-start | bytes 6488064 | tf_op jit(solution)/shard_map/all_gather | solution.py:130
  62.1 17.2 %collective-permute-start = (bf16[256,1536]{1,0:T(8,128)(2,1)S(1)}, bf16[256,1536]{1,0:T(8,128)(2,1)S(1)}, u32[]{:S(2)}, u32[]{:S(2)}) collective-permute-start(bf16[256,1536]{1,0:T(8,128)(2,1)S(1)} %get-tuple-element.86), channel_id=1, source_target_pairs={{0,1},{1,0},{2,3},{3,2},{4,5},{5,4},{6,7},{7,6},{8,9},{9,8},{10,11... | collective-permute-start | bytes 2359304 | tf_op jit(solution)/shard_map/ppermute | solution.py:49
  62.5 19.5 %collective-permute-start.1 = (bf16[256,1536]{1,0:T(8,128)(2,1)S(1)}, bf16[256,1536]{1,0:T(8,128)(2,1)S(1)}, u32[]{:S(2)}, u32[]{:S(2)}) collective-permute-start(bf16[256,1536]{1,0:T(8,128)(2,1)S(1)} %get-tuple-element.86), channel_id=1, source_target_pairs={{0,2},{1,3},{2,0},{3,1},{4,6},{5,7},{6,4},{7,5},{8,10},{9,11},{10,... | collective-permute-start | bytes 2359304 | tf_op jit(solution)/shard_map/ppermute | solution.py:49
  79.3 9.6 collective-permute-start.2
  145.0 11.5 %collective-permute-start.4 = (bf16[128,2048]{1,0:T(8,128)(2,1)}, bf16[128,2048]{1,0:T(8,128)(2,1)}, u32[]{:S(2)}, u32[]{:S(2)}) collective-permute-start(bf16[128,2048]{1,0:T(8,128)(2,1)} %get-tuple-element.56), channel_id=1, source_target_pairs={{0,2},{1,3},{2,0},{3,1},{4,6},{5,7},{6,4},{7,5},{8,10},{9,11},{10,... | collective-permute-start | bytes 1572872 | tf_op jit(solution)/shard_map/ppermute | solution.py:49
  146.2 10.5 %collective-permute-start.6 = (bf16[128,2048]{1,0:T(8,128)(2,1)}, bf16[128,2048]{1,0:T(8,128)(2,1)}, u32[]{:S(2)}, u32[]{:S(2)}) collective-permute-start(bf16[128,2048]{1,0:T(8,128)(2,1)} %get-tuple-element.55), channel_id=1, source_target_pairs={{0,1},{1,0},{2,3},{3,2},{4,5},{5,4},{6,7},{7,6},{8,9},{9,8},{10,11... | collective-permute-start | bytes 1572872 | tf_op jit(solution)/shard_map/ppermute | solution.py:49
  147.1 565.4 %all-reduce.3.cloned.1.call-start = ((), (), s32[]{:S(2)}) async-start(), calls=%async_computation.10 | async-start | bytes 15728640 | tf_op jit(solution)/shard_map/psum | solution.py:275
  158.5 26.2 %collective-permute-start.5 = (bf16[256,2048]{1,0:T(8,128)(2,1)S(1)}, bf16[256,2048]{1,0:T(8,128)(2,1)S(1)}, u32[]{:S(2)}, u32[]{:S(2)}) collective-permute-start(bf16[256,2048]{1,0:T(8,128)(2,1)S(1)} %pad_maximum_fusion.5), channel_id=1, source_target_pairs={{0,1},{1,0},{2,3},{3,2},{4,5},{5,4},{6,7},{7,6},{8,9},{9,8},{10,11... | collective-permute-start | bytes 3145736 | tf_op jit(solution)/shard_map/ppermute | solution.py:49
  159.6 26.2 %collective-permute-start.7 = (bf16[256,2048]{1,0:T(8,128)(2,1)S(1)}, bf16[256,2048]{1,0:T(8,128)(2,1)S(1)}, u32[]{:S(2)}, u32[]{:S(2)}) collective-permute-start(bf16[256,2048]{1,0:T(8,128)(2,1)S(1)} %pad_maximum_fusion.6), channel_id=1, source_target_pairs={{0,2},{1,3},{2,0},{3,1},{4,6},{5,7},{6,4},{7,5},{8,10},{9,11},{10,... | collective-permute-start | bytes 3145736 | tf_op jit(solution)/shard_map/ppermute | solution.py:49
  160.6 46.5 %collective-permute-start.19 = (bf16[256,2048]{1,0:T(8,128)(2,1)S(1)}, bf16[256,2048]{1,0:T(8,128)(2,1)S(1)}, u32[]{:S(2)}, u32[]{:S(2)}) collective-permute-start(bf16[256,2048]{1,0:T(8,128)(2,1)S(1)} %copy-done.27), channel_id=1, source_target_pairs={{0,1},{1,0},{2,3},{3,2},{4,5},{5,4},{6,7},{7,6},{8,9},{9,8},{10,11... | collective-permute-start | bytes 3145736 | tf_op jit(solution)/shard_map/ppermute | solution.py:49
  162.3 47.1 %collective-permute-start.20 = (bf16[256,2048]{1,0:T(8,128)(2,1)S(1)}, bf16[256,2048]{1,0:T(8,128)(2,1)S(1)}, u32[]{:S(2)}, u32[]{:S(2)}) collective-permute-start(bf16[256,2048]{1,0:T(8,128)(2,1)S(1)} %copy-done.27), channel_id=1, source_target_pairs={{0,2},{1,3},{2,0},{3,1},{4,6},{5,7},{6,4},{7,5},{8,10},{9,11},{10,... | collective-permute-start | bytes 3145736 | tf_op jit(solution)/shard_map/ppermute | solution.py:49
  189.1 40.4 %collective-permute-start.8 = (bf16[256,2048]{1,0:T(8,128)(2,1)S(1)}, bf16[256,2048]{1,0:T(8,128)(2,1)S(1)}, u32[]{:S(2)}, u32[]{:S(2)}) collective-permute-start(bf16[256,2048]{1,0:T(8,128)(2,1)S(1)} %get-tuple-element.26), channel_id=1, source_target_pairs={{0,1},{1,0},{2,3},{3,2},{4,5},{5,4},{6,7},{7,6},{8,9},{9,8},{10,11... | collective-permute-start | bytes 3145736 | tf_op jit(solution)/shard_map/ppermute | solution.py:49
  207.2 14.9 %collective-permute-start.21 = (bf16[128,2048]{1,0:T(8,128)(2,1)S(1)}, bf16[128,2048]{1,0:T(8,128)(2,1)S(1)}, u32[]{:S(2)}, u32[]{:S(2)}) collective-permute-start(bf16[128,2048]{1,0:T(8,128)(2,1)S(1)} %slice.349), channel_id=1, source_target_pairs={{0,2},{1,3},{2,0},{3,1},{4,6},{5,7},{6,4},{7,5},{8,10},{9,11},{10,... | collective-permute-start | bytes 1572872 | tf_op jit(solution)/shard_map/ppermute | solution.py:49
  208.7 33.0 %collective-permute-start.9 = (bf16[256,2048]{1,0:T(8,128)(2,1)S(1)}, bf16[256,2048]{1,0:T(8,128)(2,1)S(1)}, u32[]{:S(2)}, u32[]{:S(2)}) collective-permute-start(bf16[256,2048]{1,0:T(8,128)(2,1)S(1)} %get-tuple-element.26), channel_id=1, source_target_pairs={{0,2},{1,3},{2,0},{3,1},{4,6},{5,7},{6,4},{7,5},{8,10},{9,11},{10,... | collective-permute-start | bytes 3145736 | tf_op jit(solution)/shard_map/ppermute | solution.py:49
  209.4 28.4 %collective-permute-start.22 = (bf16[128,2048]{1,0:T(8,128)(2,1)S(1)}, bf16[128,2048]{1,0:T(8,128)(2,1)S(1)}, u32[]{:S(2)}, u32[]{:S(2)}) collective-permute-start(bf16[128,2048]{1,0:T(8,128)(2,1)S(1)} %slice.350), channel_id=1, source_target_pairs={{0,1},{1,0},{2,3},{3,2},{4,5},{5,4},{6,7},{7,6},{8,9},{9,8},{10,11... | collective-permute-start | bytes 1572872 | tf_op jit(solution)/shard_map/ppermute | solution.py:49
  229.6 17.8 %collective-permute-start.10 = (bf16[128,2048]{1,0:T(8,128)(2,1)S(1)}, bf16[128,2048]{1,0:T(8,128)(2,1)S(1)}, u32[]{:S(2)}, u32[]{:S(2)}) collective-permute-start(bf16[128,2048]{1,0:T(8,128)(2,1)S(1)} %slice.337), channel_id=1, source_target_pairs={{0,2},{1,3},{2,0},{3,1},{4,6},{5,7},{6,4},{7,5},{8,10},{9,11},{10,... | collective-permute-start | bytes 1572872 | tf_op jit(solution)/shard_map/ppermute | solution.py:49
  300.0 25.8 %collective-permute-start.15 = (bf16[128,2048]{1,0:T(8,128)(2,1)S(1)}, bf16[128,2048]{1,0:T(8,128)(2,1)S(1)}, u32[]{:S(2)}, u32[]{:S(2)}) collective-permute-start(bf16[128,2048]{1,0:T(8,128)(2,1)S(1)} %get-tuple-element.50), channel_id=1, source_target_pairs={{0,2},{1,3},{2,0},{3,1},{4,6},{5,7},{6,4},{7,5},{8,10},{9,11},{10,... | collective-permute-start | bytes 1572872 | tf_op jit(solution)/shard_map/ppermute | solution.py:49
  301.6 24.2 %collective-permute-start.17 = (bf16[128,2048]{1,0:T(8,128)(2,1)S(1)}, bf16[128,2048]{1,0:T(8,128)(2,1)S(1)}, u32[]{:S(2)}, u32[]{:S(2)}) collective-permute-start(bf16[128,2048]{1,0:T(8,128)(2,1)S(1)} %get-tuple-element.49), channel_id=1, source_target_pairs={{0,1},{1,0},{2,3},{3,2},{4,5},{5,4},{6,7},{7,6},{8,9},{9,8},{10,11... | collective-permute-start | bytes 1572872 | tf_op jit(solution)/shard_map/ppermute | solution.py:49
  324.9 14.9 %collective-permute-start.23 = (bf16[128,2048]{1,0:T(8,128)(2,1)S(1)}, bf16[128,2048]{1,0:T(8,128)(2,1)S(1)}, u32[]{:S(2)}, u32[]{:S(2)}) collective-permute-start(bf16[128,2048]{1,0:T(8,128)(2,1)S(1)} %get-tuple-element.44), channel_id=1, source_target_pairs={{0,2},{1,3},{2,0},{3,1},{4,6},{5,7},{6,4},{7,5},{8,10},{9,11},{10,... | collective-permute-start | bytes 1572872 | tf_op jit(solution)/shard_map/ppermute | solution.py:49
  325.5 14.9 %collective-permute-start.25 = (bf16[128,2048]{1,0:T(8,128)(2,1)S(1)}, bf16[128,2048]{1,0:T(8,128)(2,1)S(1)}, u32[]{:S(2)}, u32[]{:S(2)}) collective-permute-start(bf16[128,2048]{1,0:T(8,128)(2,1)S(1)} %get-tuple-element.43), channel_id=1, source_target_pairs={{0,1},{1,0},{2,3},{3,2},{4,5},{5,4},{6,7},{7,6},{8,9},{9,8},{10,11... | collective-permute-start | bytes 1572872 | tf_op jit(solution)/shard_map/ppermute | solution.py:49
  326.0 36.2 %collective-permute-start.16 = (bf16[256,2048]{1,0:T(8,128)(2,1)S(1)}, bf16[256,2048]{1,0:T(8,128)(2,1)S(1)}, u32[]{:S(2)}, u32[]{:S(2)}) collective-permute-start(bf16[256,2048]{1,0:T(8,128)(2,1)S(1)} %pad_maximum_fusion.7), channel_id=1, source_target_pairs={{0,1},{1,0},{2,3},{3,2},{4,5},{5,4},{6,7},{7,6},{8,9},{9,8},{10,11... | collective-permute-start | bytes 3145736 | tf_op jit(solution)/shard_map/ppermute | solution.py:49
  327.9 34.3 %collective-permute-start.18 = (bf16[256,2048]{1,0:T(8,128)(2,1)S(1)}, bf16[256,2048]{1,0:T(8,128)(2,1)S(1)}, u32[]{:S(2)}, u32[]{:S(2)}) collective-permute-start(bf16[256,2048]{1,0:T(8,128)(2,1)S(1)} %pad_maximum_fusion.8), channel_id=1, source_target_pairs={{0,2},{1,3},{2,0},{3,1},{4,6},{5,7},{6,4},{7,5},{8,10},{9,11},{10,... | collective-permute-start | bytes 3145736 | tf_op jit(solution)/shard_map/ppermute | solution.py:49
  340.6 35.8 %collective-permute-start.24 = (bf16[256,2048]{1,0:T(8,128)(2,1)S(1)}, bf16[256,2048]{1,0:T(8,128)(2,1)S(1)}, u32[]{:S(2)}, u32[]{:S(2)}) collective-permute-start(bf16[256,2048]{1,0:T(8,128)(2,1)S(1)} %pad_maximum_fusion.9), channel_id=1, source_target_pairs={{0,1},{1,0},{2,3},{3,2},{4,5},{5,4},{6,7},{7,6},{8,9},{9,8},{10,11... | collective-permute-start | bytes 3145736 | tf_op jit(solution)/shard_map/ppermute | solution.py:49
  341.1 35.4 %collective-permute-start.26 = (bf16[256,2048]{1,0:T(8,128)(2,1)S(1)}, bf16[256,2048]{1,0:T(8,128)(2,1)S(1)}, u32[]{:S(2)}, u32[]{:S(2)}) collective-permute-start(bf16[256,2048]{1,0:T(8,128)(2,1)S(1)} %pad_maximum_fusion.10), channel_id=1, source_target_pairs={{0,2},{1,3},{2,0},{3,1},{4,6},{5,7},{6,4},{7,5},{8,10},{9,11},{10,... | collective-permute-start | bytes 3145736 | tf_op jit(solution)/shard_map/ppermute | solution.py:49
  382.1 20.4 %collective-permute-start.27 = (bf16[256,2048]{1,0:T(8,128)(2,1)S(1)}, bf16[256,2048]{1,0:T(8,128)(2,1)S(1)}, u32[]{:S(2)}, u32[]{:S(2)}) collective-permute-start(bf16[256,2048]{1,0:T(8,128)(2,1)S(1)} %get-tuple-element.23), channel_id=1, source_target_pairs={{0,1},{1,0},{2,3},{3,2},{4,5},{5,4},{6,7},{7,6},{8,9},{9,8},{10,11... | collective-permute-start | bytes 3145736 | tf_op jit(solution)/shard_map/ppermute | solution.py:49
  382.8 21.7 %collective-permute-start.28 = (bf16[256,2048]{1,0:T(8,128)(2,1)S(1)}, bf16[256,2048]{1,0:T(8,128)(2,1)S(1)}, u32[]{:S(2)}, u32[]{:S(2)}) collective-permute-start(bf16[256,2048]{1,0:T(8,128)(2,1)S(1)} %get-tuple-element.23), channel_id=1, source_target_pairs={{0,2},{1,3},{2,0},{3,1},{4,6},{5,7},{6,4},{7,5},{8,10},{9,11},{10,... | collective-permute-start | bytes 3145736 | tf_op jit(solution)/shard_map/ppermute | solution.py:49
  402.6 9.2 collective-permute-start.29
  404.5 9.2 collective-permute-start.30
  472.9 14.3 %collective-permute-start.31 = (bf16[128,1536]{1,0:T(8,128)(2,1)S(1)}, bf16[128,1536]{1,0:T(8,128)(2,1)S(1)}, u32[]{:S(2)}, u32[]{:S(2)}) collective-permute-start(bf16[128,1536]{1,0:T(8,128)(2,1)S(1)} %pad_maximum_fusion.21), channel_id=1, source_target_pairs={{0,2},{1,3},{2,0},{3,1},{4,6},{5,7},{6,4},{7,5},{8,10},{9,11},{10,... | collective-permute-start | bytes 1179656 | tf_op jit(solution)/shard_map/ppermute | solution.py:49
  488.1 54.3 %collective-permute-start.35 = (bf16[256,512]{1,0:T(8,128)(2,1)S(1)}, bf16[256,512]{1,0:T(8,128)(2,1)S(1)}, u32[]{:S(2)}, u32[]{:S(2)}) collective-permute-start(bf16[256,512]{1,0:T(8,128)(2,1)S(1)} %get-tuple-element.83), channel_id=1, source_target_pairs={{0,1},{1,0},{2,3},{3,2},{4,5},{5,4},{6,7},{7,6},{8,9},{9,8},{10,11... | collective-permute-start | bytes 786440 | tf_op jit(solution)/shard_map/ppermute | solution.py:49
  490.2 52.3 %collective-permute-start.36 = (bf16[256,512]{1,0:T(8,128)(2,1)S(1)}, bf16[256,512]{1,0:T(8,128)(2,1)S(1)}, u32[]{:S(2)}, u32[]{:S(2)}) collective-permute-start(bf16[256,512]{1,0:T(8,128)(2,1)S(1)} %get-tuple-element.82), channel_id=1, source_target_pairs={{0,2},{1,3},{2,0},{3,1},{4,6},{5,7},{6,4},{7,5},{8,10},{9,11},{10,... | collective-permute-start | bytes 786440 | tf_op jit(solution)/shard_map/ppermute | solution.py:49
  490.6 51.9 %collective-permute-start.37 = (bf16[256,512]{1,0:T(8,128)(2,1)S(1)}, bf16[256,512]{1,0:T(8,128)(2,1)S(1)}, u32[]{:S(2)}, u32[]{:S(2)}) collective-permute-start(bf16[256,512]{1,0:T(8,128)(2,1)S(1)} %get-tuple-element.81), channel_id=1, source_target_pairs={{0,3},{1,2},{2,1},{3,0},{4,7},{5,6},{6,5},{7,4},{8,11},{9,10},{10,... | collective-permute-start | bytes 786440 | tf_op jit(solution)/shard_map/ppermute | solution.py:49
  497.3 21.9 %collective-permute-start.32 = (bf16[256,1536]{1,0:T(8,128)(2,1)S(1)}, bf16[256,1536]{1,0:T(8,128)(2,1)S(1)}, u32[]{:S(2)}, u32[]{:S(2)}) collective-permute-start(bf16[256,1536]{1,0:T(8,128)(2,1)S(1)} %get-tuple-element.61), channel_id=1, source_target_pairs={{0,1},{1,0},{2,3},{3,2},{4,5},{5,4},{6,7},{7,6},{8,9},{9,8},{10,11... | collective-permute-start | bytes 2359304 | tf_op jit(solution)/shard_map/ppermute | solution.py:49
  497.4 21.8 %collective-permute-start.34 = (bf16[256,1536]{1,0:T(8,128)(2,1)S(1)}, bf16[256,1536]{1,0:T(8,128)(2,1)S(1)}, u32[]{:S(2)}, u32[]{:S(2)}) collective-permute-start(bf16[256,1536]{1,0:T(8,128)(2,1)S(1)} %get-tuple-element.62), channel_id=1, source_target_pairs={{0,2},{1,3},{2,0},{3,1},{4,6},{5,7},{6,4},{7,5},{8,10},{9,11},{10,... | collective-permute-start | bytes 2359304 | tf_op jit(solution)/shard_map/ppermute | solution.py:49
  521.7 12.1 %collective-permute-start.38 = (bf16[256,1536]{1,0:T(8,128)(2,1)S(1)}, bf16[256,1536]{1,0:T(8,128)(2,1)S(1)}, u32[]{:S(2)}, u32[]{:S(2)}) collective-permute-start(bf16[256,1536]{1,0:T(8,128)(2,1)S(1)} %get-tuple-element.84), channel_id=1, source_target_pairs={{0,1},{1,0},{2,3},{3,2},{4,5},{5,4},{6,7},{7,6},{8,9},{9,8},{10,11... | collective-permute-start | bytes 2359304 | tf_op jit(solution)/shard_map/ppermute | solution.py:49
  522.6 12.0 %collective-permute-start.39 = (bf16[256,1536]{1,0:T(8,128)(2,1)S(1)}, bf16[256,1536]{1,0:T(8,128)(2,1)S(1)}, u32[]{:S(2)}, u32[]{:S(2)}) collective-permute-start(bf16[256,1536]{1,0:T(8,128)(2,1)S(1)} %get-tuple-element.84), channel_id=1, source_target_pairs={{0,2},{1,3},{2,0},{3,1},{4,6},{5,7},{6,4},{7,5},{8,10},{9,11},{10,... | collective-permute-start | bytes 2359304 | tf_op jit(solution)/shard_map/ppermute | solution.py:49
  545.5 234.2 %reduce-scatter.4.cloned.1.call-start = ((), (), s32[]{:S(2)}) async-start(), calls=%async_computation.4 | async-start | bytes 6488064 | tf_op jit(solution)/shard_map/reduce_scatter | solution.py:205
  557.1 288.6 %reduce-scatter.6.cloned.1.call-start = ((), (), s32[]{:S(2)}) async-start(), calls=%async_computation.5 | async-start | bytes 6488064 | tf_op jit(solution)/shard_map/reduce_scatter | solution.py:205
  568.2 343.6 %reduce-scatter.8.cloned.1.call-start = ((), (), s32[]{:S(2)}) async-start(), calls=%async_computation.6 | async-start | bytes 6488064 | tf_op jit(solution)/shard_map/reduce_scatter | solution.py:205
  579.3 434.5 %all-gather.8.cloned.1.call-start = ((), (), s32[]{:S(2)}) async-start(), calls=%async_computation.3 | async-start | bytes 7864320 | tf_op jit(solution)/shard_map/all_gather | solution.py:276
  916.0 70.2 %collective-permute-start.42 = (bf16[3,64,1408]{2,1,0:T(8,128)(2,1)}, bf16[3,64,1408]{2,1,0:T(8,128)(2,1)}, u32[]{:S(2)}, u32[]{:S(2)}) collective-permute-start(bf16[3,64,1408]{2,1,0:T(8,128)(2,1)} %get-tuple-element.69), channel_id=1, source_target_pairs={{0,1},{1,0},{2,3},{3,2},{4,5},{5,4},{6,7},{7,6},{8,9},{9,8},{10,11... | collective-permute-start | bytes 1622024 | tf_op jit(solution)/shard_map/ppermute | solution.py:49
  980.7 30.6 %collective-permute-start.43 = (bf16[3,64,1408]{2,1,0:T(8,128)(2,1)S(1)}, bf16[3,64,1408]{2,1,0:T(8,128)(2,1)S(1)}, u32[]{:S(2)}, u32[]{:S(2)}) collective-permute-start(bf16[3,64,1408]{2,1,0:T(8,128)(2,1)S(1)} %get-tuple-element.68), channel_id=1, source_target_pairs={{0,2},{1,3},{2,0},{3,1},{4,6},{5,7},{6,4},{7,5},{8,10},{9,11},{10,... | collective-permute-start | bytes 1622024 | tf_op jit(solution)/shard_map/ppermute | solution.py:49
  984.7 26.8 %collective-permute-start.44 = (bf16[3,64,1408]{2,1,0:T(8,128)(2,1)S(1)}, bf16[3,64,1408]{2,1,0:T(8,128)(2,1)S(1)}, u32[]{:S(2)}, u32[]{:S(2)}) collective-permute-start(bf16[3,64,1408]{2,1,0:T(8,128)(2,1)S(1)} %get-tuple-element.67), channel_id=1, source_target_pairs={{0,3},{1,2},{2,1},{3,0},{4,7},{5,6},{6,5},{7,4},{8,11},{9,10},{10,... | collective-permute-start | bytes 1622024 | tf_op jit(solution)/shard_map/ppermute | solution.py:49
  (71 other events, 717.9 us)
Sparse Core Ops, SparseCore 0:
  46.3 60.7 all-gather.11
  109.4 59.0 all-gather.13
  170.2 59.0 all-gather.9
  545.6 166.9 all-reduce.2
  714.7 64.9 reduce-scatter.3
  782.5 63.1 reduce-scatter.5
  848.6 63.2 reduce-scatter.7
  913.7 91.0 all-gather.7

commit v2 on v1

v2 whole, which is shorter than its diff:
```python
import functools
import math

import jax
import jax.numpy as jnp
from jax import lax
from jax.experimental import pallas as pl
from jax.experimental.pallas import tpu as pltpu
from jax.sharding import PartitionSpec as P

epsilon = 1e-05
masked_value = -1e30
low = jnp.bfloat16


def dot(left, right, contract=(1, 0)):
    return lax.dot_general(
        left,
        right,
        (((contract[0],), (contract[1],)), ((), ())),
        preferred_element_type=jnp.float32,
    )


def rescale(values, gain):
    factor = lax.rsqrt(jnp.mean(values * values, axis=-1, keepdims=True) + epsilon)
    return (values * factor * gain, factor)


def rescale_back(values, factor, gain, upstream):
    weighted = upstream * gain
    inner_mean = jnp.mean(values * weighted, axis=-1, keepdims=True)
    back = factor * weighted - values * (factor * factor * factor) * inner_mean
    return (back, jnp.sum(upstream * values * factor, axis=0))


def rotate(values, cosine, sine):
    half = values.shape[-1] // 2
    first = values[..., :half]
    second = values[..., half:]
    return jnp.concatenate(
        [first * cosine - second * sine, second * cosine + first * sine], axis=-1
    )


def rotate_back(grads, cosine, sine):
    return rotate(grads, cosine, -sine)


def swap(values, axis, bit):
    size = lax.axis_size(axis)
    return lax.ppermute(values, axis, [(i, i ^ bit) for i in range(size)])


def sending_order(size):
    if size == 4:
        return [[3], [1, 2], [0]]
    return [list(range(size))]


def gather_near(own):
    size = lax.axis_size("head")
    if size == 4:
        cut = own.shape[0] // 2
        first, second = swap(own, "head", 1), swap(own, "head", 2)
        third = jnp.concatenate(
            [swap(first[:cut], "head", 2), swap(second[cut:], "head", 1)], axis=0
        )
        return [own, first, second, third]
    blocks = [own]
    bit = 1
    while bit < size:
        blocks = blocks + [swap(block, "head", bit) for block in blocks]
        bit *= 2
    return blocks


def scatter_near(parts):
    size = len(parts)
    if size == 4:
        cut = parts[0].shape[0] // 2
        via_first = swap(parts[3][:cut], "head", 1)
        via_second = swap(parts[3][cut:], "head", 2)
        second = jnp.concatenate([parts[2][:cut] + via_first, parts[2][cut:]], axis=0)
        first = jnp.concatenate([parts[1][:cut], parts[1][cut:] + via_second], axis=0)
        return (
            parts[0].astype(jnp.float32)
            + swap(first, "head", 1).astype(jnp.float32)
            + swap(second, "head", 2).astype(jnp.float32)
        )
    bit = size // 2
    while bit:
        parts = [parts[k] + swap(parts[k + bit], "head", bit) for k in range(bit)]
        bit //= 2
    return parts[0].astype(jnp.float32)


def spread(pieces):
    return [pieces[0]] + [swap(pieces[k], "head", k) for k in range(1, len(pieces))]


def attend_kernel(
    spots, latent, up_weight, cosine, sine, keys, values, out_weight, query, mixed, partial, total
):
    block, head = pl.program_id(0), pl.program_id(1)
    count = spots.shape[0] - 2
    rows, width = query.shape
    place = spots[block]
    raw = dot(latent[...], up_weight[...])
    query[...] = rotate(raw, cosine[...], sine[...]).astype(low)
    row = place * rows + lax.broadcasted_iota(jnp.int32, (rows, 1), 0)
    first, second = spots[count], spots[count + 1]
    begin = jnp.where(row >= second, second, jnp.where(row >= first, first, 0))

    def with_keys(size):
        column = lax.broadcasted_iota(jnp.int32, (rows, size), 1)
        scores = dot(query[...], keys[:size], (1, 1)) * (1.0 / math.sqrt(width))
        scores = jnp.where((column <= row) & (column >= begin), scores, masked_value)
        raised = jnp.exp(scores - jnp.max(scores, axis=1, keepdims=True))
        shares = raised * (1.0 / jnp.sum(raised, axis=1, keepdims=True))
        mixed[...] = dot(shares.astype(low), values[:size]).astype(low)

    for number in range(keys.shape[0] // rows):
        pl.when(place == number)(functools.partial(with_keys, (number + 1) * rows))

    product = dot(mixed[...], out_weight[...])

    @pl.when(head == 0)
    def _():
        total[...] = product

    @pl.when(head > 0)
    def _():
        total[...] += product

    @pl.when(head == pl.num_programs(1) - 1)
    def _():
        partial[...] = total[...].astype(low)


def attend(spots, latent, query_up, cosine, sine, keys, values, out_weight):
    total, rank = latent.shape
    spare, head_width = keys.shape
    blocks = spots.shape[0] - 2
    rows = total // blocks
    heads = query_up.shape[1] // head_width
    width = out_weight.shape[1]
    whole = pl.BlockSpec(keys.shape, lambda i, h, s: (0, 0))
    table = pl.BlockSpec((rows, head_width // 2), lambda i, h, s: (i, 0))
    tile = pl.BlockSpec((rows, head_width), lambda i, h, s: (i, h))
    return pl.pallas_call(
        attend_kernel,
        grid_spec=pltpu.PrefetchScalarGridSpec(
            num_scalar_prefetch=1,
            grid=(blocks, heads),
            in_specs=[
                pl.BlockSpec((rows, rank), lambda i, h, s: (i, 0)),
                pl.BlockSpec((rank, head_width), lambda i, h, s: (0, h)),
                table,
                table,
                whole,
                whole,
                pl.BlockSpec((head_width, width), lambda i, h, s: (h, 0)),
            ],
            out_specs=[tile, tile, pl.BlockSpec((rows, width), lambda i, h, s: (i, 0))],
            scratch_shapes=[pltpu.VMEM((rows, width), jnp.float32)],
        ),
        out_shape=[
            jax.ShapeDtypeStruct((total, heads * head_width), low),
            jax.ShapeDtypeStruct((total, heads * head_width), low),
            jax.ShapeDtypeStruct((total, width), low),
        ],
        compiler_params=pltpu.CompilerParams(vmem_limit_bytes=40 << 20),
        cost_estimate=pl.CostEstimate(
            flops=2 * total * heads * head_width * (rank + width + 5 * spare // 4),
            bytes_accessed=2 * total * (rank + width) + blocks * 2 * query_up.size * 3,
            transcendentals=total * heads * spare,
        ),
    )(spots, latent, query_up, cosine, sine, keys, values, out_weight)


def attend_back_kernel(
    spots,
    branch,
    out_weight,
    query,
    keys,
    values,
    up_weight,
    cosine,
    sine,
    key_before,
    value_before,
    query_back,
    partial,
    key_back,
    value_back,
    total,
    grad_query,
):
    block, head = pl.program_id(0), pl.program_id(1)
    count = spots.shape[0] - 2
    rows, width = query.shape
    place = spots[block]
    scale = 1.0 / math.sqrt(width)
    mixed_back = dot(branch[...], out_weight[...], (1, 1)).astype(low)
    column = place * rows + lax.broadcasted_iota(jnp.int32, (1, rows), 1)
    first, second = spots[count], spots[count + 1]
    begin = jnp.where(column >= second, second, jnp.where(column >= first, first, 0))

    @pl.when((block == 0) & (head == 0))
    def _():
        key_back[...] = key_before[...]
        value_back[...] = value_before[...]

    def with_keys(size):
        row = lax.broadcasted_iota(jnp.int32, (size, rows), 0)
        scores = dot(keys[:size], query[...], (1, 1)) * scale
        scores = jnp.where((row <= column) & (row >= begin), scores, masked_value)
        raised = jnp.exp(scores - jnp.max(scores, axis=0, keepdims=True))
        shares = raised * (1.0 / jnp.sum(raised, axis=0, keepdims=True))
        value_back[:size] += dot(shares.astype(low), mixed_back)
        back = dot(values[:size], mixed_back, (1, 1))
        centre = jnp.sum(shares * back, axis=0, keepdims=True)
        scores_back = (shares * (back - centre)).astype(low)
        key_back[:size] += dot(scores_back, query[...]) * scale
        grad_query[...] = dot(scores_back, keys[:size], (0, 0)) * scale

    for number in range(keys.shape[0] // rows):
        pl.when(place == number)(functools.partial(with_keys, (number + 1) * rows))

    turned = rotate(grad_query[...], cosine[...], -sine[...]).astype(low)
    query_back[...] = turned
    product = dot(turned, up_weight[...], (1, 1))

    @pl.when(head == 0)
    def _():
        total[...] = product

    @pl.when(head > 0)
    def _():
        total[...] += product

    @pl.when(head == pl.num_programs(1) - 1)
    def _():
        partial[...] = total[...].astype(low)


def attend_back(
    spots,
    branch,
    out_weight,
    query,
    keys,
    values,
    query_up,
    cosine,
    sine,
    key_before,
    value_before,
):
    total, width = branch.shape
    spare, head_width = keys.shape
    rank = query_up.shape[0]
    blocks = spots.shape[0] - 2
    rows = total // blocks
    heads = query_up.shape[1] // head_width
    whole = pl.BlockSpec(keys.shape, lambda i, h, s: (0, 0))
    table = pl.BlockSpec((rows, head_width // 2), lambda i, h, s: (i, 0))
    tile = pl.BlockSpec((rows, head_width), lambda i, h, s: (i, h))
    return pl.pallas_call(
        attend_back_kernel,
        grid_spec=pltpu.PrefetchScalarGridSpec(
            num_scalar_prefetch=1,
            grid=(blocks, heads),
            in_specs=[
                pl.BlockSpec((rows, width), lambda i, h, s: (i, 0)),
                pl.BlockSpec((head_width, width), lambda i, h, s: (h, 0)),
                tile,
                whole,
                whole,
                pl.BlockSpec((rank, head_width), lambda i, h, s: (0, h)),
                table,
                table,
                whole,
                whole,
            ],
            out_specs=[
                tile,
                pl.BlockSpec((rows, rank), lambda i, h, s: (i, 0)),
                whole,
                whole,
            ],
            scratch_shapes=[
                pltpu.VMEM((rows, rank), jnp.float32),
                pltpu.VMEM((rows, head_width), jnp.float32),
            ],
        ),
        out_shape=[
            jax.ShapeDtypeStruct((total, heads * head_width), low),
            jax.ShapeDtypeStruct((total, rank), low),
            jax.ShapeDtypeStruct(keys.shape, jnp.float32),
            jax.ShapeDtypeStruct(keys.shape, jnp.float32),
        ],
        compiler_params=pltpu.CompilerParams(vmem_limit_bytes=40 << 20),
        cost_estimate=pl.CostEstimate(
            flops=2 * total * heads * head_width * (rank + width + 25 * spare // 8),
            bytes_accessed=2 * total * (rank + width) + blocks * 2 * query_up.size * 3,
            transcendentals=total * heads * spare,
        ),
    )(
        spots,
        branch,
        out_weight,
        query,
        keys,
        values,
        query_up,
        cosine,
        sine,
        key_before,
        value_before,
    )


def after(values, *others):
    return lax.optimization_barrier((values, *others))[0]


def columns_of(weights, feed_part):
    count = lax.axis_size("head")
    me = lax.axis_index("head")
    depth, strip = weights.shape[:2]
    arrived = spread(
        [
            lax.dynamic_slice_in_dim(weights, (me ^ k) * feed_part, feed_part, 2)
            for k in range(count)
        ]
    )
    columns = jnp.zeros((depth, strip * count, feed_part), low)
    for k in range(count):
        columns = lax.dynamic_update_slice(columns, arrived[k], (0, (me ^ k) * strip, 0))
    return columns


def spread_columns(sums, strip):
    count = lax.axis_size("head")
    me = lax.axis_index("head")
    return spread(
        [lax.dynamic_slice_in_dim(sums, (me ^ k) * strip, strip, 1) for k in range(count)]
    )


def placed_columns(arrived, number):
    me = lax.axis_index("head")
    strip, part = arrived[0].shape[1:]
    gradient = jnp.zeros((strip, part * len(arrived)), jnp.float32)
    for k, block in enumerate(arrived):
        gradient = lax.dynamic_update_slice(
            gradient, block[number].astype(jnp.float32), (0, (me ^ k) * part)
        )
    return gradient


def sum_over_batch(values):
    size = lax.axis_size("batch") // 2
    place = lax.axis_index("batch")
    core, line = place & 1, place >> 1
    half = values.shape[0] // 2
    piece = half // size
    given = swap(lax.dynamic_slice_in_dim(values, (1 - core) * half, half), "batch", 1)
    kept = lax.dynamic_slice_in_dim(values, core * half, half) + given
    pieces = [
        lax.dynamic_slice_in_dim(kept, (line ^ k) * piece, piece) for k in range(size)
    ]
    total = pieces[0].astype(jnp.float32)
    for k in range(1, size):
        total = total + swap(pieces[k], "batch", 2 * k).astype(jnp.float32)
    total = total.astype(values.dtype)
    whole = jnp.zeros((half,) + values.shape[1:], values.dtype)
    for k in range(size):
        block = swap(total, "batch", 2 * k) if k else total
        whole = lax.dynamic_update_slice(whole, block, ((line ^ k) * piece, 0))
    return whole


def sum_over_all(values):
    for axis in ("head", "batch"):
        bit = 1
        while bit < lax.axis_size(axis):
            values = values + swap(values, axis, bit)
            bit *= 2
    return values


def widen_kernel(order, block, *outs):
    begin = 0
    for out in outs:
        out[...] = block[:, begin : begin + out.shape[1]].astype(out.dtype)
        begin += out.shape[1]


def widen(order, blocks, widths):
    count = order.shape[0]
    rows = blocks.shape[0] // count
    return pl.pallas_call(
        widen_kernel,
        grid_spec=pltpu.PrefetchScalarGridSpec(
            num_scalar_prefetch=1,
            grid=(count,),
            in_specs=[pl.BlockSpec((rows, blocks.shape[1]), lambda i, order: (order[i], 0))],
            out_specs=[pl.BlockSpec((rows, width), lambda i, order: (i, 0)) for width in widths],
        ),
        out_shape=[
            jax.ShapeDtypeStruct((blocks.shape[0], width), jnp.float32) for width in widths
        ],
        compiler_params=pltpu.CompilerParams(vmem_limit_bytes=24 << 20),
    )(order, blocks)


def shards(
    tokens,
    attention_gain,
    query_down,
    query_gain,
    query_up,
    key_weight,
    value_weight,
    out_weight,
    feed_gain,
    gate_weight,
    up_weight,
    down_weight,
    lengths,
    cotangent,
):
    rows, width = tokens.shape
    count = lax.axis_size("head")
    me = lax.axis_index("head")
    total = rows * count
    head_width = key_weight.shape[1]
    rank = query_up.shape[0]
    feed = gate_weight.shape[1]
    feed_part = feed // count
    strip = gate_weight.shape[0]

    bounds = jnp.cumsum(lengths.reshape(-1), dtype=jnp.int32)
    index = jnp.concatenate(
        [(me ^ k) * rows + jnp.arange(rows, dtype=jnp.int32) for k in range(count)]
    )
    segment = (index >= bounds[0]).astype(jnp.int32) + (index >= bounds[1]).astype(jnp.int32)
    begin = jnp.where(segment == 0, 0, jnp.where(segment == 1, bounds[0], bounds[1]))
    half = head_width // 2
    rates = 10000.0 ** (-2.0 * jnp.arange(half, dtype=jnp.float32) / head_width)
    turns = (index - begin).astype(jnp.float32)[:, None] * rates[None, :]
    cosine, sine = jnp.cos(turns), jnp.sin(turns)
    own_cosine, own_sine = cosine[:rows], sine[:rows]
    ends = bounds[:2]

    def spots(group):
        return jnp.concatenate([me ^ jnp.array(group, jnp.int32), ends])

    def part(values, group):
        return values[group[0] * rows : (group[-1] + 1) * rows]

    groups = sending_order(count)

    def split(values, group):
        return {k: values[i * rows : (i + 1) * rows] for i, k in enumerate(group)}


    inputs = tokens.astype(jnp.float32)
    normed, first_factor = rescale(inputs, attention_gain)
    normed_low = normed.astype(low)
    latent = dot(normed_low, query_down)
    latent_in, latent_factor = rescale(latent, query_gain)
    key_own = rotate(dot(normed_low, key_weight), own_cosine, own_sine).astype(low)
    value_own = dot(normed_low, value_weight).astype(low)
    lkv_own = jnp.concatenate([latent_in.astype(low), key_own, value_own], axis=1)
    gate_up_columns = columns_of(jnp.stack([gate_weight, up_weight]), feed_part)
    gate_up_columns, lkv_own = lax.optimization_barrier((gate_up_columns, lkv_own))
    gate_up_whole = lax.all_gather(gate_up_columns, "batch", axis=1, tiled=True)
    lkv_blocks = gather_near(lkv_own)
    latent_last = lkv_blocks[-1]
    down_columns = columns_of(after(down_weight, latent_last).T[None], feed_part)
    down_whole = lax.all_gather(down_columns[0], "batch", axis=0, tiled=True)
    cotangent_all = jnp.concatenate(gather_near(after(cotangent, latent_last)), axis=0)
    latent_all = jnp.concatenate([block[:, :rank] for block in lkv_blocks], axis=0)
    keys_all, values_all = jnp.zeros((2, total, head_width), low)
    for k in range(count):
        keys_all = lax.dynamic_update_slice(
            keys_all, lkv_blocks[k][:, rank : rank + head_width], ((me ^ k) * rows, 0)
        )
        values_all = lax.dynamic_update_slice(
            values_all, lkv_blocks[k][:, rank + head_width :], ((me ^ k) * rows, 0)
        )
    queries, mixes, partials = {}, {}, {}
    last = cotangent_all
    for group in groups:
        latents = latent_all if len(groups) == 1 else part(latent_all, group)
        latents, last = lax.optimization_barrier((latents, last))
        queries[group[0]], mixes[group[0]], last = attend(
            spots(group),
            latents,
            query_up,
            part(cosine, group),
            part(sine, group),
            keys_all,
            values_all,
            out_weight,
        )
        partials.update(split(last, group))
    attention_part = scatter_near([partials[k] for k in range(count)])
    mixed_low = jnp.concatenate([mixes[group[0]] for group in sorted(groups)], axis=0)
    middle = inputs + attention_part
    inner, second_factor = rescale(middle, feed_gain)
    inner_all = jnp.concatenate(gather_near(inner.astype(low)), axis=0)
    gate_whole, up_whole = gate_up_whole[0], gate_up_whole[1]
    gate = dot(inner_all, gate_whole)
    up = dot(inner_all, up_whole)
    sigma = jax.nn.sigmoid(gate)
    swish = gate * sigma
    hidden_low = (swish * up).astype(low)

    def reduced(left, right):
        return lax.psum_scatter(
            dot(left, right, (0, 0)).astype(low), "batch", scatter_dimension=0, tiled=True
        )

    down_part = dot(cotangent_all, hidden_low, (0, 0)).astype(low)
    down_whole, down_part = lax.optimization_barrier((down_whole, down_part))
    down_sum = lax.psum_scatter(down_part, "batch", scatter_dimension=0, tiled=True)
    grad_hidden = dot(cotangent_all, down_whole)
    slope = sigma * (1.0 + gate * (1.0 - sigma))
    grad_gate_low = (grad_hidden * up * slope).astype(low)
    grad_up_low = (grad_hidden * swish).astype(low)
    grad_inner_partial = (
        dot(grad_gate_low, gate_whole, (1, 1)) + dot(grad_up_low, up_whole, (1, 1))
    ).astype(low)
    gate_part = dot(inner_all, grad_gate_low, (0, 0)).astype(low)
    up_part = dot(inner_all, grad_up_low, (0, 0)).astype(low)
    grad_inner = scatter_near(
        [grad_inner_partial[k * rows : (k + 1) * rows] for k in range(count)]
    )
    grad_inner, gate_part, up_part, hidden_low, down_sum = lax.optimization_barrier(
        (grad_inner, gate_part, up_part, hidden_low, down_sum)
    )
    feed_sum = lax.psum_scatter(
        jnp.concatenate([gate_part, up_part], axis=1), "batch", scatter_dimension=0, tiled=True
    )

    feed_partial = dot(hidden_low, down_whole, (1, 1)).astype(low)
    feed_out = scatter_near([feed_partial[k * rows : (k + 1) * rows] for k in range(count)])
    output = (middle + feed_out).astype(low)

    middle_part, feed_gain_part = rescale_back(middle, second_factor, feed_gain, grad_inner)
    grad_middle = cotangent.astype(jnp.float32) + middle_part
    branch_all = jnp.concatenate(gather_near(grad_middle.astype(low)), axis=0)
    arrived_first = spread_columns(down_sum[None], strip)
    key_grads, value_grads = jnp.zeros((2, total, head_width), jnp.float32)
    query_grads, latent_partials = {}, {}
    for group in groups:
        query_grads[group[0]], last, key_grads, value_grads = attend_back(
            spots(group),
            part(branch_all, group),
            out_weight,
            queries[group[0]],
            keys_all,
            values_all,
            query_up,
            part(cosine, group),
            part(sine, group),
            key_grads,
            value_grads,
        )
        latent_partials.update(split(last, group))
    query_grad_low = jnp.concatenate([query_grads[group[0]] for group in sorted(groups)], axis=0)
    key_value_partials = [
        jnp.concatenate(
            [
                lax.dynamic_slice_in_dim(key_grads, (me ^ k) * rows, rows),
                lax.dynamic_slice_in_dim(value_grads, (me ^ k) * rows, rows),
            ],
            axis=1,
        ).astype(low)
        for k in range(count)
    ]
    query_grad_low, key_value_partials, branch_all, arrived_first, feed_sum = (
        lax.optimization_barrier(
            (query_grad_low, key_value_partials, branch_all, arrived_first, feed_sum)
        )
    )
    latent_back = scatter_near([latent_partials[k] for k in range(count)])
    key_value_back = scatter_near(key_value_partials)
    out_part = dot(mixed_low, branch_all, (0, 0)).astype(low)
    query_part = dot(latent_all, query_grad_low, (0, 0)).astype(low)
    query_up_gradient, out_gradient = lax.psum((query_part, out_part), "batch")
    latent_grad, query_gain_part = rescale_back(latent, latent_factor, query_gain, latent_back)
    key_back = rotate_back(key_value_back[:, :head_width], own_cosine, own_sine)
    lkv_grad_low = jnp.concatenate(
        [latent_grad, key_back, key_value_back[:, head_width:]], axis=1
    ).astype(low)

    slice_width = width // count
    normed_slices = jnp.concatenate(
        spread(
            [
                lax.dynamic_slice_in_dim(normed_low, (me ^ k) * slice_width, slice_width, 1)
                for k in range(count)
            ]
        ),
        axis=0,
    )
    lkv_grad_all = jnp.concatenate(gather_near(lkv_grad_low), axis=0)
    shared_part = dot(normed_slices, lkv_grad_all, (0, 0)).astype(low)
    grad_normed = (
        dot(lkv_grad_low[:, :rank], query_down, (1, 1))
        + dot(lkv_grad_low[:, rank : rank + head_width], key_weight, (1, 1))
        + dot(lkv_grad_low[:, rank + head_width :], value_weight, (1, 1))
    )
    input_part, attention_gain_part = rescale_back(
        inputs, first_factor, attention_gain, grad_normed
    )
    input_gradient = grad_middle + input_part
    gains = sum_over_all(
        jnp.concatenate([attention_gain_part, feed_gain_part, query_gain_part]).reshape(-1, 128)
    ).reshape(-1)
    arrived_second = spread_columns(
        jnp.stack(jnp.split(after(feed_sum, shared_part), 2, axis=1)), strip
    )
    shared_half = sum_over_batch(shared_part)
    blocks = gather_near(shared_half)
    mine = jnp.concatenate(blocks + [swap(block, "batch", 1) for block in blocks], axis=0)
    spot = jnp.arange(2 * count, dtype=jnp.int32)
    order = ((spot >> 1) ^ me) + count * ((spot & 1) ^ (lax.axis_index("batch") & 1))
    query_down_gradient, key_gradient, value_gradient = widen(
        order, mine, (rank, head_width, head_width)
    )
    return (
        output,
        input_gradient,
        gains[:width],
        query_down_gradient,
        gains[2 * width :],
        query_up_gradient.astype(jnp.float32),
        key_gradient,
        value_gradient,
        out_gradient.astype(jnp.float32),
        gains[width : 2 * width],
        placed_columns(arrived_second, 0),
        placed_columns(arrived_second, 1),
        placed_columns(arrived_first, 0).T,
    )


def solution(mesh):
    rows = P(("batch", "head"), None)
    columns = P(None, ("batch", "head"))
    return jax.shard_map(
        shards,
        mesh=mesh,
        in_specs=(
            rows,
            P(),
            P(),
            P(),
            P(None, "head"),
            P(),
            P(),
            P("head", None),
            P(),
            rows,
            rows,
            columns,
            P("batch", None),
            rows,
        ),
        out_specs=(
            rows,
            rows,
            P(),
            P(),
            P(),
            P(None, "head"),
            P(),
            P(),
            P("head", None),
            P(),
            rows,
            rows,
            columns,
        ),
        check_vma=False,
    )
```

time: 1030 us -> 696 us (0.68)
  waiting for transfers between devices: 586 us -> 261 us
  matrix products: 210 us -> 123 us
  Pallas kernels: 0 us -> 80.6 us
  blocking collectives: 52.8 us -> 0 us
  starting transfers between devices: 51.4 us -> 86.5 us
    reduce_scatter x3 -> x2, waiting for transfers between devices: 190 us -> 0.01 us  [the longest x1 0.01 us: shards(): lax.psum_scatter(down_part, 'batch', scatter_dimension=0, tiled=True)]
    psum x1, waiting for transfers between devices: 133 us -> 45.9 us  [shards(): query_up_gradient, out_gradient = lax.psum((query_part, out_part), 'batch')]
    pallas_call x0 -> x7, Pallas kernels: none -> 80.6 us  [the longest x3 42 us: attend_back(): pl.pallas_call(attend_back_kernel, grid_spec=pltpu.PrefetchScalarGridSpec...]
    psum x1 -> x0, blocking collectives: 52.8 us -> none  [shards(): lax.psum(jnp.concatenate([attention_gain_part, feed_gain_part, query_gain...]
    ppermute x45 -> x75, waiting for transfers between devices: 263 us -> 215 us  [swap(): return lax.ppermute(values, axis, [(i, i ^ bit) for i in range(size)])]
    dot_general x5 -> x0, matrix products: 37.9 us -> none  [the longest x1 10.2 us: shards(): jnp.einsum('qhd,kd->hqk', grad_mixed_low, values_all, preferred_element_t...]
    dot_general x22 -> x18, matrix products: 161 us -> 123 us  [dot(): lax.dot_general(left, right, (((contract[0],), (contract[1],)), ((), ()))...]
    ppermute x45 -> x75, starting transfers between devices: 50.5 us -> 85.7 us  [swap(): return lax.ppermute(values, axis, [(i, i ^ bit) for i in range(size)])]
  transfers between devices with their start and end apart: 53 -> 80, of which waited for: 36 -> 42; matrix products, arithmetic and copies ran while one was open for 20% -> 32% of each run, Pallas kernels for 0% -> 11%
where the time goes in v2:
time: 696 us; the launch traced here: 687 us
  waiting for transfers between devices  261 us (38%)
  matrix products  123 us (18%)
  starting transfers between devices  86.5 us (12%)
  Pallas kernels  80.6 us (12%)
  other arithmetic  61.3 us (9%)
  local copies, waits for them, and re-layouts  58.6 us (8%)
  between operations  15.9 us (2%)
    ppermute x75, waiting for transfers between devices, swap(): return lax.ppermute(values, axis, [(i, i ^ bit) for i in range(size)])  215 us
    dot_general x18, matrix products, dot(): lax.dot_general(left, right, (((contract[0],), (contract[1],)), ((), ()))...  123 us
    ppermute x75, starting transfers between devices, swap(): return lax.ppermute(values, axis, [(i, i ^ bit) for i in range(size)])  85.7 us
    psum x1, waiting for transfers between devices, shards(): query_up_gradient, out_gradient = lax.psum((query_part, out_part), 'batch')  45.9 us
    pallas_call x3, Pallas kernels, attend_back(): pl.pallas_call(attend_back_kernel, grid_spec=pltpu.PrefetchScalarGridSpec...  42 us
    pallas_call x3, Pallas kernels, attend(): pl.pallas_call(attend_kernel, grid_spec=pltpu.PrefetchScalarGridSpec(num_...  32.8 us
    unnamed x208, local copies, waits for them, and re-layouts  22.2 us
  transfers between devices with their start and end apart: 80, of which 42 were waited for; matrix products, arithmetic and copies ran while one was open for 32% of the time, Pallas kernels for 11%

profile of v2, /device:TPU:0, one launch (start us, length us, event | category | flops | bytes accessed | tf_op | source)
XLA Modules:
  0.0 687.0 jit_solution(5459331874921115646)
XLA Ops:
  28.2 3.8 collective-permute-done.1
  40.6 12.2 %collective-permute-done.3 = bf16[256,1536]{1,0:T(8,128)(2,1)} collective-permute-done((bf16[256,1536]{1,0:T(8,128)(2,1)}, bf16[256,1536]{1,0:T(8,128)(2,1)}, u32[]{:S(2)}, u32[]{:S(2)}) %collective-permute-start.3) | collective-permute-done | bytes 786464 | tf_op jit(solution)/shard_map/ppermute | solution.py:52
  62.4 3.0 collective-permute-done.6
  75.1 16.4 %collective-permute-done.7 = bf16[256,2048]{1,0:T(8,128)(2,1)S(1)} collective-permute-done((bf16[256,2048]{1,0:T(8,128)(2,1)S(1)}, bf16[256,2048]{1,0:T(8,128)(2,1)S(1)}, u32[]{:S(2)}, u32[]{:S(2)}) %collective-permute-start.7) | collective-permute-done | bytes 1048608 | tf_op jit(solution)/shard_map/ppermute | solution.py:52
  93.3 3.0 collective-permute-done.8
  96.7 10.7 %collective-permute-done.9 = bf16[128,2048]{1,0:T(8,128)(2,1)S(1)} collective-permute-done((bf16[128,2048]{1,0:T(8,128)(2,1)S(1)}, bf16[128,2048]{1,0:T(8,128)(2,1)S(1)}, u32[]{:S(2)}, u32[]{:S(2)}) %collective-permute-start.9) | collective-permute-done | bytes 524320 | tf_op jit(solution)/shard_map/ppermute | solution.py:52
  107.6 9.6 %shard_map.291 = (bf16[256,1024]{1,0:T(8,128)(2,1)S(1)}, bf16[256,1024]{1,0:T(8,128)(2,1)S(1)}, bf16[256,2048]{1,0:T(8,128)(2,1)S(1)}) custom-call(s32[3]{0:T(128)S(1)} %get-tuple-element.228.spots, bf16[256,1024]{1,0:T(8,128)(2,1)S(1)} %slice.413.latent, bf16[1024,1024]{1,0:T(8,128)(2,1)S(1)} %copy-done.19, f32[256,128]{1,0:T(8,128)S(1)} %get-tuple-element.203.cosine, ...), custom_call_target="tpu_custom_call" | custom-call | flops 2281701376 | bytes 7864320 | tf_op jit(solution)/shard_map/pallas_call | solution.py:151
  118.7 16.2 %shard_map.292 = (bf16[512,1024]{1,0:T(8,128)(2,1)S(1)}, bf16[512,1024]{1,0:T(8,128)(2,1)S(1)}, bf16[512,2048]{1,0:T(8,128)(2,1)S(1)}) custom-call(s32[4]{0:T(128)S(1)} %pad_add_fusion.2.spots, bf16[512,1024]{1,0:T(8,128)(2,1)S(1)} %pad_maximum_fusion.3.latent, bf16[1024,1024]{1,0:T(8,128)(2,1)S(1)} %copy-done.19, f32[512,128]{1,0:T(8,128)S(1)} %slice.424.cosine, ...), custom_call_target="tpu_custom_call" | custom-call | flops 4563402752 | bytes 15728640 | tf_op jit(solution)/shard_map/pallas_call | solution.py:151
  146.5 7.1 %shard_map.293 = (bf16[256,1024]{1,0:T(8,128)(2,1)S(1)}, bf16[256,1024]{1,0:T(8,128)(2,1)S(1)}, bf16[256,2048]{1,0:T(8,128)(2,1)S(1)}) custom-call(s32[3]{0:T(128)S(1)} %get-tuple-element.227.spots, bf16[256,1024]{1,0:T(8,128)(2,1)S(1)} %slice.325.latent, bf16[1024,1024]{1,0:T(8,128)(2,1)S(1)} %copy-done.20, f32[256,128]{1,0:T(8,128)S(1)} %get-tuple-element.202.cosine, ...), custom_call_target="tpu_custom_call" | custom-call | flops 2281701376 | bytes 7864320 | tf_op jit(solution)/shard_map/pallas_call | solution.py:151
  164.6 20.4 %collective-permute-done.18 = bf16[256,2048]{1,0:T(8,128)(2,1)S(1)} collective-permute-done((bf16[256,2048]{1,0:T(8,128)(2,1)S(1)}, bf16[256,2048]{1,0:T(8,128)(2,1)S(1)}, u32[]{:S(2)}, u32[]{:S(2)}) %collective-permute-start.18) | collective-permute-done | bytes 1048608 | tf_op jit(solution)/shard_map/ppermute | solution.py:52
  190.2 4.1 collective-permute-done.20
  197.1 10.6 %fusion.2 = f32[1024,1408]{1,0:T(8,128)S(1)} fusion(bf16[1024,2048]{1,0:T(8,128)(2,1)} %constant_dynamic-update-slice_fusion.7, bf16[2,2048,1408]{2,1,0:T(8,128)(2,1)} %all-gather.5.cloned.1.call-done), kind=kOutput, calls=%fused_computation.13 | convolution fusion | flops 5905580032 | bytes 15728640 | tf_op jit(solution)/shard_map/dot_general | solution.py:17
  207.7 12.3 %multiply_convert_fusion.2 = (bf16[1024,1408]{1,0:T(8,128)(2,1)}, f32[1024,1408]{1,0:T(8,128)}) fusion(f32[1024,1408]{1,0:T(8,128)S(1)} %fusion.2, bf16[1024,2048]{1,0:T(8,128)(2,1)} %constant_dynamic-update-slice_fusion.7, bf16[2,2048,1408]{2,1,0:T(8,128)(2,1)S(1)} %copy-done.81), kind=kOutput, calls=%fused_computation.9 | convolution fusion | flops 5914230784 | bytes 24379392 | tf_op jit(solution)/shard_map/dot_general | solution.py:17
  220.0 10.4 %convolution_convert_fusion.2 = bf16[2048,1408]{1,0:T(8,128)(2,1)} fusion(bf16[1024,2048]{1,0:T(8,128)(2,1)S(1)} %copy-done.67, bf16[1024,1408]{1,0:T(8,128)(2,1)} %get-tuple-element.75), kind=kOutput, calls=%fused_computation.4 | convolution fusion | flops 5908463616 | bytes 12845056 | tf_op jit(solution)/shard_map/dot_general | solution.py:17
  230.5 15.8 %multiply_convert_fusion = (bf16[1024,1408]{1,0:T(8,128)(2,1)}, bf16[1024,1408]{1,0:T(8,128)(2,1)S(1)}) fusion(f32[1024,1408]{1,0:T(8,128)} %copy-done.86, f32[1024,1408]{1,0:T(8,128)} %get-tuple-element.234, bf16[1024,2048]{1,0:T(8,128)(2,1)} %copy-done.66, bf16[2048,1408]{1,0:T(8,128)(2,1)} %all-gather.3.cloned.1.call-done), kind=kOutput, calls=%fused_computation.7 | convolution fusion | flops 5924323328 | bytes 27262976 | tf_op jit(solution)/shard_map/dot_general | solution.py:17
  246.3 10.9 %fusion.1 = f32[1024,2048]{1,0:T(8,128)} fusion(bf16[1024,1408]{1,0:T(8,128)(2,1)S(1)} %get-tuple-element.131, bf16[2,2048,1408]{2,1,0:T(8,128)(2,1)} %all-gather.5.cloned.1.call-done), kind=kOutput, calls=%fused_computation.12 | convolution fusion | flops 5905580032 | bytes 17039360 | tf_op jit(solution)/shard_map/dot_general | solution.py:17
  257.3 10.1 %add_convert_fusion = bf16[1024,2048]{1,0:T(8,128)(2,1)S(1)} fusion(f32[1024,2048]{1,0:T(8,128)} %fusion.1, bf16[1024,1408]{1,0:T(8,128)(2,1)} %get-tuple-element.130, bf16[2,2048,1408]{2,1,0:T(8,128)(2,1)S(1)} %bitcast.150), kind=kOutput, calls=%fused_computation.1 | convolution fusion | flops 5909774336 | bytes 21233664 | tf_op jit(solution)/shard_map/dot_general | solution.py:17
  269.8 10.9 %convolution_convert_fusion.1 = bf16[2048,1408]{1,0:T(8,128)(2,1)} fusion(bf16[1024,2048]{1,0:T(8,128)(2,1)} %constant_dynamic-update-slice_fusion.7, bf16[1024,1408]{1,0:T(8,128)(2,1)S(1)} %get-tuple-element.131), kind=kOutput, calls=%fused_computation.3 | convolution fusion | flops 5908463616 | bytes 12845056 | tf_op jit(solution)/shard_map/dot_general | solution.py:17
  282.9 11.1 %convolution_convert_fusion = bf16[2048,1408]{1,0:T(8,128)(2,1)} fusion(bf16[1024,2048]{1,0:T(8,128)(2,1)} %constant_dynamic-update-slice_fusion.7, bf16[1024,1408]{1,0:T(8,128)(2,1)S(1)} %copy-done.87), kind=kOutput, calls=%fused_computation.2 | convolution fusion | flops 5908463616 | bytes 12845056 | tf_op jit(solution)/shard_map/dot_general | solution.py:17
  294.0 5.3 collective-permute-done.25
  301.5 9.9 %pad_maximum_fusion = bf16[2048,2816]{1,0:T(8,128)(2,1)} fusion(bf16[2048,1408]{1,0:T(8,128)(2,1)} %convolution_convert_fusion, bf16[2048,1408]{1,0:T(8,128)(2,1)} %convolution_convert_fusion.1), kind=kLoop, calls=%fused_computation | loop fusion | flops 23068672 | bytes 23068672 | tf_op jit(solution)/shard_map/concatenate | solution.py:549
  311.4 9.6 %convolution_convert_fusion.3 = bf16[1024,2048]{1,0:T(8,128)(2,1)S(1)} fusion(bf16[1024,1408]{1,0:T(8,128)(2,1)} %get-tuple-element.75, bf16[2048,1408]{1,0:T(8,128)(2,1)} %all-gather.3.cloned.1.call-done), kind=kOutput, calls=%fused_computation.22 | convolution fusion | flops 5907677184 | bytes 12845056 | tf_op jit(solution)/shard_map/dot_general | solution.py:17
  324.0 10.8 %collective-permute-done.26 = bf16[128,2048]{1,0:T(8,128)(2,1)S(1)} collective-permute-done((bf16[128,2048]{1,0:T(8,128)(2,1)S(1)}, bf16[128,2048]{1,0:T(8,128)(2,1)S(1)}, u32[]{:S(2)}, u32[]{:S(2)}) %collective-permute-start.26) | collective-permute-done | bytes 524320 | tf_op jit(solution)/shard_map/ppermute | solution.py:52
  339.5 14.2 %collective-permute-done.29 = bf16[256,2048]{1,0:T(8,128)(2,1)S(1)} collective-permute-done((bf16[256,2048]{1,0:T(8,128)(2,1)S(1)}, bf16[256,2048]{1,0:T(8,128)(2,1)S(1)}, u32[]{:S(2)}, u32[]{:S(2)}) %collective-permute-start.29) | collective-permute-done | bytes 1048608 | tf_op jit(solution)/shard_map/ppermute | solution.py:52
  370.9 15.9 %collective-permute-done.31 = bf16[256,2048]{1,0:T(8,128)(2,1)} collective-permute-done((bf16[256,2048]{1,0:T(8,128)(2,1)S(1)}, bf16[256,2048]{1,0:T(8,128)(2,1)}, u32[]{:S(2)}, u32[]{:S(2)}) %collective-permute-start.31) | collective-permute-done | bytes 1048608 | tf_op jit(solution)/shard_map/ppermute | solution.py:52
  400.4 12.3 %shard_map.294 = (bf16[256,1024]{1,0:T(8,128)(2,1)S(1)}, bf16[256,1024]{1,0:T(8,128)(2,1)S(1)}, f32[1024,256]{1,0:T(8,128)S(1)}, f32[1024,256]{1,0:T(8,128)S(1)}) custom-call(s32[3]{0:T(128)S(1)} %copy-done.14, bf16[256,2048]{1,0:T(8,128)(2,1)S(1)} %pad_maximum_fusion.10.branch, bf16[1024,2048]{1,0:T(8,128)(2,1)S(1)} %copy-done.17, ...), custom_call_target="tpu_custom_call" | custom-call | flops 3288334336 | bytes 7864320 | tf_op jit(solution)/shard_map/pallas_call | solution.py:271
  412.9 21.1 %shard_map.295 = (bf16[512,1024]{1,0:T(8,128)(2,1)S(1)}, bf16[512,1024]{1,0:T(8,128)(2,1)S(1)}, f32[1024,256]{1,0:T(8,128)S(1)}, f32[1024,256]{1,0:T(8,128)S(1)}) custom-call(s32[4]{0:T(128)S(1)} %copy-done.23, bf16[512,2048]{1,0:T(8,128)(2,1)S(1)} %pad_maximum_fusion.1.branch, bf16[1024,2048]{1,0:T(8,128)(2,1)} %out_weight.11, ...), custom_call_target="tpu_custom_call" | custom-call | flops 6576668672 | bytes 15728640 | tf_op jit(solution)/shard_map/pallas_call | solution.py:271
  436.2 8.6 %shard_map.296 = (bf16[256,1024]{1,0:T(8,128)(2,1)S(1)}, bf16[256,1024]{1,0:T(8,128)(2,1)S(1)}, f32[1024,256]{1,0:T(8,128)S(1)}, f32[1024,256]{1,0:T(8,128)S(1)}) custom-call(s32[3]{0:T(128)S(1)} %copy-done.12, bf16[256,2048]{1,0:T(8,128)(2,1)S(1)} %get-tuple-element.124.branch, bf16[1024,2048]{1,0:T(8,128)(2,1)S(1)} %copy-done.18, ...), custom_call_target="tpu_custom_call" | custom-call | flops 3288334336 | bytes 7864320 | tf_op jit(solution)/shard_map/pallas_call | solution.py:271
  448.1 4.9 collective-permute-start.37
  453.0 3.4 collective-permute-start.35
  476.2 5.9 fusion.27
  482.1 6.4 convolution_convert_fusion.4
  493.0 4.1 collective-permute-done.44
  522.9 6.5 collective-permute-done.53
  531.0 8.9 %collective-permute-done.55 = bf16[128,1536]{1,0:T(8,128)(2,1)S(1)} collective-permute-done((bf16[128,1536]{1,0:T(8,128)(2,1)S(1)}, bf16[128,1536]{1,0:T(8,128)(2,1)S(1)}, u32[]{:S(2)}, u32[]{:S(2)}) %collective-permute-start.55) | collective-permute-done | bytes 393248 | tf_op jit(solution)/shard_map/ppermute | solution.py:52
  540.0 3.1 collective-permute-done.56
  543.1 3.0 convolution_convert_fusion.5
  549.1 3.6 collective-permute-start.60
  556.6 5.7 collective-permute-done.60
  564.6 9.1 %collective-permute-done.59 = bf16[64,1536]{1,0:T(8,128)(2,1)S(1)} collective-permute-done((bf16[64,1536]{1,0:T(8,128)(2,1)S(1)}, bf16[64,1536]{1,0:T(8,128)(2,1)S(1)}, u32[]{:S(2)}, u32[]{:S(2)}) %collective-permute-start.59) | collective-permute-done | bytes 196640 | tf_op jit(solution)/shard_map/ppermute | solution.py:52
  579.3 8.6 %collective-permute-done.61 = bf16[64,1536]{1,0:T(8,128)(2,1)S(1)} collective-permute-done((bf16[64,1536]{1,0:T(8,128)(2,1)S(1)}, bf16[64,1536]{1,0:T(8,128)(2,1)S(1)}, u32[]{:S(2)}, u32[]{:S(2)}) %collective-permute-start.61) | collective-permute-done | bytes 196640 | tf_op jit(solution)/shard_map/ppermute | solution.py:52
  588.0 5.5 collective-permute-done.62
  593.5 5.5 collective-permute-done.63
  604.5 45.9 %all-reduce.3.cloned.1.call-done = (bf16[1024,1024]{1,0:T(8,128)(2,1)}, bf16[1024,2048]{1,0:T(8,128)(2,1)}) async-done(((bf16[1024,1024]{1,0:T(8,128)(2,1)}, bf16[1024,2048]{1,0:T(8,128)(2,1)}), (bf16[1024,1024]{1,0:T(8,128)(2,1)}, bf16[1024,2048]{1,0:T(8,128)(2,1)})) %all-reduce.3.cloned.1.call-update) | async-done | bytes 6291472 | tf_op jit(solution)/shard_map/psum | solution.py:597
  650.4 4.3 convert_element_type.263
  654.8 4.4 convert_element_type.265
  665.1 5.6 collective-permute-done.66
  674.5 5.8 shard_map.297
  (497 shorter events, 214.6 us)
Async XLA Ops:
  7.2 189.9 %all-gather.5.cloned.1.call-start = ((), (), s32[]{:S(2)}) async-start(), calls=%async_computation.3 | async-start | bytes 12976128 | tf_op jit(solution)/shard_map/all_gather | solution.py:482
  11.1 15.3 %collective-permute-start = (bf16[2,64,1408]{2,1,0:T(8,128)(2,1)}, bf16[2,64,1408]{2,1,0:T(8,128)(2,1)}, u32[]{:S(2)}, u32[]{:S(2)}) collective-permute-start(bf16[2,64,1408]{2,1,0:T(8,128)(2,1)} %get-tuple-element.159), channel_id=1, source_target_pairs={{0,1},{1,0},{2,3},{3,2},{4,5},{5,4},{6,7},{7,6},{8,9},{9,8},{10,11... | collective-permute-start | bytes 1081352 | tf_op jit(solution)/shard_map/ppermute | solution.py:52
  14.1 17.9 %collective-permute-start.1 = (bf16[2,64,1408]{2,1,0:T(8,128)(2,1)}, bf16[2,64,1408]{2,1,0:T(8,128)(2,1)}, u32[]{:S(2)}, u32[]{:S(2)}) collective-permute-start(bf16[2,64,1408]{2,1,0:T(8,128)(2,1)} %get-tuple-element.160), channel_id=1, source_target_pairs={{0,2},{1,3},{2,0},{3,1},{4,6},{5,7},{6,4},{7,5},{8,10},{9,11},{10,... | collective-permute-start | bytes 1081352 | tf_op jit(solution)/shard_map/ppermute | solution.py:52
  15.6 18.1 %collective-permute-start.2 = (bf16[2,64,1408]{2,1,0:T(8,128)(2,1)}, bf16[2,64,1408]{2,1,0:T(8,128)(2,1)}, u32[]{:S(2)}, u32[]{:S(2)}) collective-permute-start(bf16[2,64,1408]{2,1,0:T(8,128)(2,1)} %get-tuple-element.157), channel_id=1, source_target_pairs={{0,3},{1,2},{2,1},{3,0},{4,7},{5,6},{6,5},{7,4},{8,11},{9,10},{10,... | collective-permute-start | bytes 1081352 | tf_op jit(solution)/shard_map/ppermute | solution.py:52
  35.5 194.9 %all-gather.3.cloned.1.call-start = ((), (), s32[]{:S(2)}) async-start(), calls=%async_computation.2 | async-start | bytes 6488064 | tf_op jit(solution)/shard_map/all_gather | solution.py:486
  36.0 16.8 %collective-permute-start.3 = (bf16[256,1536]{1,0:T(8,128)(2,1)}, bf16[256,1536]{1,0:T(8,128)(2,1)}, u32[]{:S(2)}, u32[]{:S(2)}) collective-permute-start(bf16[256,1536]{1,0:T(8,128)(2,1)} %pad_maximum_fusion.11), channel_id=1, source_target_pairs={{0,1},{1,0},{2,3},{3,2},{4,5},{5,4},{6,7},{7,6},{8,9},{9,8},{10,11... | collective-permute-start | bytes 2359304 | tf_op jit(solution)/shard_map/ppermute | solution.py:52
  36.1 19.4 %collective-permute-start.4 = (bf16[256,1536]{1,0:T(8,128)(2,1)}, bf16[256,1536]{1,0:T(8,128)(2,1)}, u32[]{:S(2)}, u32[]{:S(2)}) collective-permute-start(bf16[256,1536]{1,0:T(8,128)(2,1)} %pad_maximum_fusion.11), channel_id=1, source_target_pairs={{0,2},{1,3},{2,0},{3,1},{4,6},{5,7},{6,4},{7,5},{8,10},{9,11},{10,... | collective-permute-start | bytes 2359304 | tf_op jit(solution)/shard_map/ppermute | solution.py:52
  65.4 26.2 %collective-permute-start.7 = (bf16[256,2048]{1,0:T(8,128)(2,1)S(1)}, bf16[256,2048]{1,0:T(8,128)(2,1)S(1)}, u32[]{:S(2)}, u32[]{:S(2)}) collective-permute-start(bf16[256,2048]{1,0:T(8,128)(2,1)S(1)} %copy-done.47), channel_id=1, source_target_pairs={{0,1},{1,0},{2,3},{3,2},{4,5},{5,4},{6,7},{7,6},{8,9},{9,8},{10,11... | collective-permute-start | bytes 3145736 | tf_op jit(solution)/shard_map/ppermute | solution.py:52
  68.2 28.1 %collective-permute-start.8 = (bf16[256,2048]{1,0:T(8,128)(2,1)S(1)}, bf16[256,2048]{1,0:T(8,128)(2,1)S(1)}, u32[]{:S(2)}, u32[]{:S(2)}) collective-permute-start(bf16[256,2048]{1,0:T(8,128)(2,1)S(1)} %copy-done.47), channel_id=1, source_target_pairs={{0,2},{1,3},{2,0},{3,1},{4,6},{5,7},{6,4},{7,5},{8,10},{9,11},{10,... | collective-permute-start | bytes 3145736 | tf_op jit(solution)/shard_map/ppermute | solution.py:52
  69.9 47.6 %collective-permute-start.15 = (bf16[1,64,1408]{2,1,0:T(8,128)(2,1)S(1)}, bf16[1,64,1408]{2,1,0:T(8,128)(2,1)S(1)}, u32[]{:S(2)}, u32[]{:S(2)}) collective-permute-start(bf16[1,64,1408]{2,1,0:T(8,128)(2,1)S(1)} %get-tuple-element.198), channel_id=1, source_target_pairs={{0,1},{1,0},{2,3},{3,2},{4,5},{5,4},{6,7},{7,6},{8,9},{9,8},{10,11... | collective-permute-start | bytes 540680 | tf_op jit(solution)/shard_map/ppermute | solution.py:52
  70.2 70.7 %collective-permute-start.16 = (bf16[1,64,1408]{2,1,0:T(8,128)(2,1)S(1)}, bf16[1,64,1408]{2,1,0:T(8,128)(2,1)S(1)}, u32[]{:S(2)}, u32[]{:S(2)}) collective-permute-start(bf16[1,64,1408]{2,1,0:T(8,128)(2,1)S(1)} %get-tuple-element.197), channel_id=1, source_target_pairs={{0,2},{1,3},{2,0},{3,1},{4,6},{5,7},{6,4},{7,5},{8,10},{9,11},{10,... | collective-permute-start | bytes 540680 | tf_op jit(solution)/shard_map/ppermute | solution.py:52
  70.8 70.9 %collective-permute-start.17 = (bf16[1,64,1408]{2,1,0:T(8,128)(2,1)S(1)}, bf16[1,64,1408]{2,1,0:T(8,128)(2,1)S(1)}, u32[]{:S(2)}, u32[]{:S(2)}) collective-permute-start(bf16[1,64,1408]{2,1,0:T(8,128)(2,1)S(1)} %get-tuple-element.196), channel_id=1, source_target_pairs={{0,3},{1,2},{2,1},{3,0},{4,7},{5,6},{6,5},{7,4},{8,11},{9,10},{10,... | collective-permute-start | bytes 540680 | tf_op jit(solution)/shard_map/ppermute | solution.py:52
  91.6 15.8 %collective-permute-start.9 = (bf16[128,2048]{1,0:T(8,128)(2,1)S(1)}, bf16[128,2048]{1,0:T(8,128)(2,1)S(1)}, u32[]{:S(2)}, u32[]{:S(2)}) collective-permute-start(bf16[128,2048]{1,0:T(8,128)(2,1)S(1)} %slice.414), channel_id=1, source_target_pairs={{0,2},{1,3},{2,0},{3,1},{4,6},{5,7},{6,4},{7,5},{8,10},{9,11},{10,... | collective-permute-start | bytes 1572872 | tf_op jit(solution)/shard_map/ppermute | solution.py:52
  117.3 17.6 %collective-permute-start.13 = (bf16[128,2048]{1,0:T(8,128)(2,1)S(1)}, bf16[128,2048]{1,0:T(8,128)(2,1)S(1)}, u32[]{:S(2)}, u32[]{:S(2)}) collective-permute-start(bf16[128,2048]{1,0:T(8,128)(2,1)S(1)} %get-tuple-element.180), channel_id=1, source_target_pairs={{0,1},{1,0},{2,3},{3,2},{4,5},{5,4},{6,7},{7,6},{8,9},{9,8},{10,11... | collective-permute-start | bytes 1572872 | tf_op jit(solution)/shard_map/ppermute | solution.py:52
  117.3 17.5 %collective-permute-start.11 = (bf16[128,2048]{1,0:T(8,128)(2,1)S(1)}, bf16[128,2048]{1,0:T(8,128)(2,1)S(1)}, u32[]{:S(2)}, u32[]{:S(2)}) collective-permute-start(bf16[128,2048]{1,0:T(8,128)(2,1)S(1)} %get-tuple-element.179), channel_id=1, source_target_pairs={{0,2},{1,3},{2,0},{3,1},{4,6},{5,7},{6,4},{7,5},{8,10},{9,11},{10,... | collective-permute-start | bytes 1572872 | tf_op jit(solution)/shard_map/ppermute | solution.py:52
  136.5 19.7 %collective-permute-start.14 = (bf16[256,2048]{1,0:T(8,128)(2,1)}, bf16[256,2048]{1,0:T(8,128)(2,1)}, u32[]{:S(2)}, u32[]{:S(2)}) collective-permute-start(bf16[256,2048]{1,0:T(8,128)(2,1)} %pad_maximum_fusion.5), channel_id=1, source_target_pairs={{0,2},{1,3},{2,0},{3,1},{4,6},{5,7},{6,4},{7,5},{8,10},{9,11},{10,... | collective-permute-start | bytes 3145736 | tf_op jit(solution)/shard_map/ppermute | solution.py:52
  139.1 19.2 %collective-permute-start.12 = (bf16[256,2048]{1,0:T(8,128)(2,1)}, bf16[256,2048]{1,0:T(8,128)(2,1)}, u32[]{:S(2)}, u32[]{:S(2)}) collective-permute-start(bf16[256,2048]{1,0:T(8,128)(2,1)} %pad_maximum_fusion.4), channel_id=1, source_target_pairs={{0,1},{1,0},{2,3},{3,2},{4,5},{5,4},{6,7},{7,6},{8,9},{9,8},{10,11... | collective-permute-start | bytes 3145736 | tf_op jit(solution)/shard_map/ppermute | solution.py:52
  142.4 159.1 %reduce-scatter.3.cloned.1.call-start = ((), (), s32[]{:S(2)}) async-start(), calls=%async_computation.4 | async-start | bytes 6488064 | tf_op jit(solution)/shard_map/reduce_scatter | solution.py:532
  162.5 22.5 %collective-permute-start.18 = (bf16[256,2048]{1,0:T(8,128)(2,1)S(1)}, bf16[256,2048]{1,0:T(8,128)(2,1)S(1)}, u32[]{:S(2)}, u32[]{:S(2)}) collective-permute-start(bf16[256,2048]{1,0:T(8,128)(2,1)S(1)} %get-tuple-element.127), channel_id=1, source_target_pairs={{0,1},{1,0},{2,3},{3,2},{4,5},{5,4},{6,7},{7,6},{8,9},{9,8},{10,11... | collective-permute-start | bytes 3145736 | tf_op jit(solution)/shard_map/ppermute | solution.py:52
  164.4 22.6 %collective-permute-start.19 = (bf16[256,2048]{1,0:T(8,128)(2,1)S(1)}, bf16[256,2048]{1,0:T(8,128)(2,1)S(1)}, u32[]{:S(2)}, u32[]{:S(2)}) collective-permute-start(bf16[256,2048]{1,0:T(8,128)(2,1)S(1)} %get-tuple-element.127), channel_id=1, source_target_pairs={{0,2},{1,3},{2,0},{3,1},{4,6},{5,7},{6,4},{7,5},{8,10},{9,11},{10,... | collective-permute-start | bytes 3145736 | tf_op jit(solution)/shard_map/ppermute | solution.py:52
  230.5 241.0 %reduce-scatter.5.cloned.1.call-start = ((), (), s32[]{:S(2)}) async-start(), calls=%async_computation.5 | async-start | bytes 12976128 | tf_op jit(solution)/shard_map/reduce_scatter | solution.py:548
  280.9 18.4 %collective-permute-start.25 = (bf16[256,2048]{1,0:T(8,128)(2,1)S(1)}, bf16[256,2048]{1,0:T(8,128)(2,1)S(1)}, u32[]{:S(2)}, u32[]{:S(2)}) collective-permute-start(bf16[256,2048]{1,0:T(8,128)(2,1)S(1)} %pad_maximum_fusion.7), channel_id=1, source_target_pairs={{0,2},{1,3},{2,0},{3,1},{4,6},{5,7},{6,4},{7,5},{8,10},{9,11},{10,... | collective-permute-start | bytes 3145736 | tf_op jit(solution)/shard_map/ppermute | solution.py:52
  281.9 17.8 %collective-permute-start.23 = (bf16[256,2048]{1,0:T(8,128)(2,1)S(1)}, bf16[256,2048]{1,0:T(8,128)(2,1)S(1)}, u32[]{:S(2)}, u32[]{:S(2)}) collective-permute-start(bf16[256,2048]{1,0:T(8,128)(2,1)S(1)} %pad_maximum_fusion.6), channel_id=1, source_target_pairs={{0,1},{1,0},{2,3},{3,2},{4,5},{5,4},{6,7},{7,6},{8,9},{9,8},{10,11... | collective-permute-start | bytes 3145736 | tf_op jit(solution)/shard_map/ppermute | solution.py:52
  311.4 339.0 %all-reduce.3.cloned.1.call-start = ((), (), s32[]{:S(2)}) async-start(), calls=%async_computation.6 | async-start | bytes 12582912 | tf_op jit(solution)/shard_map/psum | solution.py:597
  337.6 16.1 %collective-permute-start.29 = (bf16[256,2048]{1,0:T(8,128)(2,1)S(1)}, bf16[256,2048]{1,0:T(8,128)(2,1)S(1)}, u32[]{:S(2)}, u32[]{:S(2)}) collective-permute-start(bf16[256,2048]{1,0:T(8,128)(2,1)S(1)} %pad_maximum_fusion.9), channel_id=1, source_target_pairs={{0,2},{1,3},{2,0},{3,1},{4,6},{5,7},{6,4},{7,5},{8,10},{9,11},{10,... | collective-permute-start | bytes 3145736 | tf_op jit(solution)/shard_map/ppermute | solution.py:52
  337.9 18.6 %collective-permute-start.27 = (bf16[256,2048]{1,0:T(8,128)(2,1)S(1)}, bf16[256,2048]{1,0:T(8,128)(2,1)S(1)}, u32[]{:S(2)}, u32[]{:S(2)}) collective-permute-start(bf16[256,2048]{1,0:T(8,128)(2,1)S(1)} %pad_maximum_fusion.8), channel_id=1, source_target_pairs={{0,1},{1,0},{2,3},{3,2},{4,5},{5,4},{6,7},{7,6},{8,9},{9,8},{10,11... | collective-permute-start | bytes 3145736 | tf_op jit(solution)/shard_map/ppermute | solution.py:52
  361.1 25.7 %collective-permute-start.31 = (bf16[256,2048]{1,0:T(8,128)(2,1)S(1)}, bf16[256,2048]{1,0:T(8,128)(2,1)}, u32[]{:S(2)}, u32[]{:S(2)}) collective-permute-start(bf16[256,2048]{1,0:T(8,128)(2,1)S(1)} %get-tuple-element.124.branch), channel_id=1, source_target_pairs={{0,2},{1,3},{2,0},{3,1},{4,6},{5,7},{6,4},{7,5},{8,10},{9,11},{10,... | collective-permute-start | bytes 3145736 | tf_op jit(solution)/shard_map/ppermute | solution.py:52
  361.1 28.7 %collective-permute-start.30 = (bf16[256,2048]{1,0:T(8,128)(2,1)S(1)}, bf16[256,2048]{1,0:T(8,128)(2,1)}, u32[]{:S(2)}, u32[]{:S(2)}) collective-permute-start(bf16[256,2048]{1,0:T(8,128)(2,1)S(1)} %get-tuple-element.124.branch), channel_id=1, source_target_pairs={{0,1},{1,0},{2,3},{3,2},{4,5},{5,4},{6,7},{7,6},{8,9},{9,8},{10,11... | collective-permute-start | bytes 3145736 | tf_op jit(solution)/shard_map/ppermute | solution.py:52
  365.5 177.6 %collective-permute-start.52 = (bf16[256,512]{1,0:T(8,128)(2,1)}, bf16[256,512]{1,0:T(8,128)(2,1)}, u32[]{:S(2)}, u32[]{:S(2)}) collective-permute-start(bf16[256,512]{1,0:T(8,128)(2,1)} %get-tuple-element.164), channel_id=1, source_target_pairs={{0,3},{1,2},{2,1},{3,0},{4,7},{5,6},{6,5},{7,4},{8,11},{9,10},{10,... | collective-permute-start | bytes 786440 | tf_op jit(solution)/shard_map/ppermute | solution.py:52
  366.8 176.3 %collective-permute-start.51 = (bf16[256,512]{1,0:T(8,128)(2,1)}, bf16[256,512]{1,0:T(8,128)(2,1)}, u32[]{:S(2)}, u32[]{:S(2)}) collective-permute-start(bf16[256,512]{1,0:T(8,128)(2,1)} %get-tuple-element.165), channel_id=1, source_target_pairs={{0,2},{1,3},{2,0},{3,1},{4,6},{5,7},{6,4},{7,5},{8,10},{9,11},{10,... | collective-permute-start | bytes 786440 | tf_op jit(solution)/shard_map/ppermute | solution.py:52
  368.9 102.3 %collective-permute-start.38 = (bf16[1,64,1408]{2,1,0:T(8,128)(2,1)S(1)}, bf16[1,64,1408]{2,1,0:T(8,128)(2,1)}, u32[]{:S(2)}, u32[]{:S(2)}) collective-permute-start(bf16[1,64,1408]{2,1,0:T(8,128)(2,1)S(1)} %get-tuple-element.194), channel_id=1, source_target_pairs={{0,1},{1,0},{2,3},{3,2},{4,5},{5,4},{6,7},{7,6},{8,9},{9,8},{10,11... | collective-permute-start | bytes 540680 | tf_op jit(solution)/shard_map/ppermute | solution.py:52
  412.7 35.2 %collective-permute-start.36 = (bf16[128,1024]{1,0:T(8,128)(2,1)S(1)}, bf16[128,1024]{1,0:T(8,128)(2,1)S(1)}, u32[]{:S(2)}, u32[]{:S(2)}) collective-permute-start(bf16[128,1024]{1,0:T(8,128)(2,1)S(1)} %get-tuple-element.200), channel_id=1, source_target_pairs={{0,1},{1,0},{2,3},{3,2},{4,5},{5,4},{6,7},{7,6},{8,9},{9,8},{10,11... | collective-permute-start | bytes 786440 | tf_op jit(solution)/shard_map/ppermute | solution.py:52
  412.8 35.1 %collective-permute-start.34 = (bf16[128,1024]{1,0:T(8,128)(2,1)S(1)}, bf16[128,1024]{1,0:T(8,128)(2,1)S(1)}, u32[]{:S(2)}, u32[]{:S(2)}) collective-permute-start(bf16[128,1024]{1,0:T(8,128)(2,1)S(1)} %get-tuple-element.199), channel_id=1, source_target_pairs={{0,2},{1,3},{2,0},{3,1},{4,6},{5,7},{6,4},{7,5},{8,10},{9,11},{10,... | collective-permute-start | bytes 786440 | tf_op jit(solution)/shard_map/ppermute | solution.py:52
  473.1 16.4 %collective-permute-start.43 = (bf16[128,512]{1,0:T(8,128)(2,1)}, bf16[128,512]{1,0:T(8,128)(2,1)}, u32[]{:S(2)}, u32[]{:S(2)}) collective-permute-start(bf16[128,512]{1,0:T(8,128)(2,1)} %get-tuple-element.214), channel_id=1, source_target_pairs={{0,1},{1,0},{2,3},{3,2},{4,5},{5,4},{6,7},{7,6},{8,9},{9,8},{10,11... | collective-permute-start | bytes 393224 | tf_op jit(solution)/shard_map/ppermute | solution.py:52
  475.2 16.8 %collective-permute-start.41 = (bf16[128,512]{1,0:T(8,128)(2,1)}, bf16[128,512]{1,0:T(8,128)(2,1)S(1)}, u32[]{:S(2)}, u32[]{:S(2)}) collective-permute-start(bf16[128,512]{1,0:T(8,128)(2,1)} %get-tuple-element.213), channel_id=1, source_target_pairs={{0,2},{1,3},{2,0},{3,1},{4,6},{5,7},{6,4},{7,5},{8,10},{9,11},{10,... | collective-permute-start | bytes 393224 | tf_op jit(solution)/shard_map/ppermute | solution.py:52
  509.0 20.4 %collective-permute-start.53 = (bf16[256,1536]{1,0:T(8,128)(2,1)S(1)}, bf16[256,1536]{1,0:T(8,128)(2,1)S(1)}, u32[]{:S(2)}, u32[]{:S(2)}) collective-permute-start(bf16[256,1536]{1,0:T(8,128)(2,1)S(1)} %get-tuple-element.184), channel_id=1, source_target_pairs={{0,1},{1,0},{2,3},{3,2},{4,5},{5,4},{6,7},{7,6},{8,9},{9,8},{10,11... | collective-permute-start | bytes 2359304 | tf_op jit(solution)/shard_map/ppermute | solution.py:52
  509.0 21.3 %collective-permute-start.54 = (bf16[256,1536]{1,0:T(8,128)(2,1)S(1)}, bf16[256,1536]{1,0:T(8,128)(2,1)S(1)}, u32[]{:S(2)}, u32[]{:S(2)}) collective-permute-start(bf16[256,1536]{1,0:T(8,128)(2,1)S(1)} %get-tuple-element.184), channel_id=1, source_target_pairs={{0,2},{1,3},{2,0},{3,1},{4,6},{5,7},{6,4},{7,5},{8,10},{9,11},{10,... | collective-permute-start | bytes 2359304 | tf_op jit(solution)/shard_map/ppermute | solution.py:52
  520.1 22.9 %collective-permute-start.50 = (bf16[256,512]{1,0:T(8,128)(2,1)S(1)}, bf16[256,512]{1,0:T(8,128)(2,1)S(1)}, u32[]{:S(2)}, u32[]{:S(2)}) collective-permute-start(bf16[256,512]{1,0:T(8,128)(2,1)S(1)} %copy-done.65), channel_id=1, source_target_pairs={{0,1},{1,0},{2,3},{3,2},{4,5},{5,4},{6,7},{7,6},{8,9},{9,8},{10,11... | collective-permute-start | bytes 786440 | tf_op jit(solution)/shard_map/ppermute | solution.py:52
  546.5 27.5 %collective-permute-start.72 = (bf16[2,64,1408]{2,1,0:T(8,128)(2,1)S(1)}, bf16[2,64,1408]{2,1,0:T(8,128)(2,1)S(1)}, u32[]{:S(2)}, u32[]{:S(2)}) collective-permute-start(bf16[2,64,1408]{2,1,0:T(8,128)(2,1)S(1)} %get-tuple-element.153), channel_id=1, source_target_pairs={{0,1},{1,0},{2,3},{3,2},{4,5},{5,4},{6,7},{7,6},{8,9},{9,8},{10,11... | collective-permute-start | bytes 1081352 | tf_op jit(solution)/shard_map/ppermute | solution.py:52
  552.8 21.0 %collective-permute-start.59 = (bf16[64,1536]{1,0:T(8,128)(2,1)S(1)}, bf16[64,1536]{1,0:T(8,128)(2,1)S(1)}, u32[]{:S(2)}, u32[]{:S(2)}) collective-permute-start(bf16[64,1536]{1,0:T(8,128)(2,1)S(1)} %get-tuple-element.183), channel_id=1, source_target_pairs={{0,16},{4,20},{8,24},{12,28},{16,0},{20,4},{24,8},{28,12},{1,17},{... | collective-permute-start | bytes 589832 | tf_op jit(solution)/shard_map/ppermute | solution.py:52
  552.8 21.0 %collective-permute-start.58 = (bf16[64,1536]{1,0:T(8,128)(2,1)S(1)}, bf16[64,1536]{1,0:T(8,128)(2,1)S(1)}, u32[]{:S(2)}, u32[]{:S(2)}) collective-permute-start(bf16[64,1536]{1,0:T(8,128)(2,1)S(1)} %get-tuple-element.181), channel_id=1, source_target_pairs={{0,8},{4,12},{8,0},{12,4},{16,24},{20,28},{24,16},{28,20},{1,9},{5... | collective-permute-start | bytes 589832 | tf_op jit(solution)/shard_map/ppermute | solution.py:52
  555.5 46.2 %collective-permute-start.73 = (bf16[2,64,1408]{2,1,0:T(8,128)(2,1)S(1)}, bf16[2,64,1408]{2,1,0:T(8,128)(2,1)S(1)}, u32[]{:S(2)}, u32[]{:S(2)}) collective-permute-start(bf16[2,64,1408]{2,1,0:T(8,128)(2,1)S(1)} %get-tuple-element.154), channel_id=1, source_target_pairs={{0,2},{1,3},{2,0},{3,1},{4,6},{5,7},{6,4},{7,5},{8,10},{9,11},{10,... | collective-permute-start | bytes 1081352 | tf_op jit(solution)/shard_map/ppermute | solution.py:52
  562.3 40.4 %collective-permute-start.74 = (bf16[2,64,1408]{2,1,0:T(8,128)(2,1)S(1)}, bf16[2,64,1408]{2,1,0:T(8,128)(2,1)S(1)}, u32[]{:S(2)}, u32[]{:S(2)}) collective-permute-start(bf16[2,64,1408]{2,1,0:T(8,128)(2,1)S(1)} %get-tuple-element.151), channel_id=1, source_target_pairs={{0,3},{1,2},{2,1},{3,0},{4,7},{5,6},{6,5},{7,4},{8,11},{9,10},{10,... | collective-permute-start | bytes 1081352 | tf_op jit(solution)/shard_map/ppermute | solution.py:52
  574.9 18.5 %collective-permute-start.62 = (bf16[64,1536]{1,0:T(8,128)(2,1)S(1)}, bf16[64,1536]{1,0:T(8,128)(2,1)S(1)}, u32[]{:S(2)}, u32[]{:S(2)}) collective-permute-start(bf16[64,1536]{1,0:T(8,128)(2,1)S(1)} %get-tuple-element.122), channel_id=1, source_target_pairs={{0,16},{4,20},{8,24},{12,28},{16,0},{20,4},{24,8},{28,12},{1,17},{... | collective-permute-start | bytes 589832 | tf_op jit(solution)/shard_map/ppermute | solution.py:52
  576.9 22.0 %collective-permute-start.63 = (bf16[64,1536]{1,0:T(8,128)(2,1)S(1)}, bf16[64,1536]{1,0:T(8,128)(2,1)S(1)}, u32[]{:S(2)}, u32[]{:S(2)}) collective-permute-start(bf16[64,1536]{1,0:T(8,128)(2,1)S(1)} %get-tuple-element.122), channel_id=1, source_target_pairs={{0,24},{4,28},{8,16},{12,20},{16,8},{20,12},{24,0},{28,4},{1,25},{... | collective-permute-start | bytes 589832 | tf_op jit(solution)/shard_map/ppermute | solution.py:52
  599.0 60.2 %collective-permute-start.64 = (bf16[256,1536]{1,0:T(8,128)(2,1)S(1)}, bf16[256,1536]{1,0:T(8,128)(2,1)}, u32[]{:S(2)}, u32[]{:S(2)}) collective-permute-start(bf16[256,1536]{1,0:T(8,128)(2,1)S(1)} %constant_dynamic-update-slice_fusion.31), channel_id=1, source_target_pairs={{0,1},{1,0},{2,3},{3,2},{4,5},{5,4},{6,7},{7,6},{8,9},{9,8},{10,11... | collective-permute-start | bytes 2359304 | tf_op jit(solution)/shard_map/ppermute | solution.py:52
  600.3 61.5 %collective-permute-start.65 = (bf16[256,1536]{1,0:T(8,128)(2,1)S(1)}, bf16[256,1536]{1,0:T(8,128)(2,1)S(1)}, u32[]{:S(2)}, u32[]{:S(2)}) collective-permute-start(bf16[256,1536]{1,0:T(8,128)(2,1)S(1)} %constant_dynamic-update-slice_fusion.31), channel_id=1, source_target_pairs={{0,2},{1,3},{2,0},{3,1},{4,6},{5,7},{6,4},{7,5},{8,10},{9,11},{10,... | collective-permute-start | bytes 2359304 | tf_op jit(solution)/shard_map/ppermute | solution.py:52
  603.6 68.6 %collective-permute-start.68 = (bf16[256,1536]{1,0:T(8,128)(2,1)S(1)}, bf16[256,1536]{1,0:T(8,128)(2,1)}, u32[]{:S(2)}, u32[]{:S(2)}) collective-permute-start(bf16[256,1536]{1,0:T(8,128)(2,1)S(1)} %constant_dynamic-update-slice_fusion.31), channel_id=1, source_target_pairs={{0,4},{4,0},{8,12},{12,8},{16,20},{20,16},{24,28},{28,24},{1,5},{5... | collective-permute-start | bytes 2359304 | tf_op jit(solution)/shard_map/ppermute | solution.py:52
  (125 other events, 1687.6 us)
Sparse Core Ops, SparseCore 0:
  35.6 108.4 all-gather.4
  146.3 58.7 all-gather.2
  230.6 65.2 reduce-scatter.2
  311.5 120.3 reduce-scatter.4
  488.7 161.6 all-reduce.2

commit v3 on v2

--- a/solution.py
+++ b/solution.py
@@ -52,17 +52,27 @@
     return lax.ppermute(values, axis, [(i, i ^ bit) for i in range(size)])
 
 
+def after(values, *others):
+    return lax.optimization_barrier((values, *others))[0] if others else values
+
+
 def sending_order(size):
     if size == 4:
         return [[3], [1, 2], [0]]
     return [list(range(size))]
 
 
-def gather_near(own):
+def gather_begin(own):
+    if lax.axis_size("head") == 4:
+        return swap(own, "head", 1), swap(own, "head", 2)
+    return ()
+
+
+def gather_end(own, begun):
     size = lax.axis_size("head")
     if size == 4:
         cut = own.shape[0] // 2
-        first, second = swap(own, "head", 1), swap(own, "head", 2)
+        first, second = begun
         third = jnp.concatenate(
             [swap(first[:cut], "head", 2), swap(second[cut:], "head", 1)], axis=0
         )
@@ -75,24 +85,34 @@
     return blocks
 
 
-def scatter_near(parts):
-    size = len(parts)
+def gather_near(own, *beside):
+    return gather_end(own, tuple(after(block, *beside) for block in gather_begin(own)))
+
+
+def scatter_near(compute, groups):
+    size = lax.axis_size("head")
     if size == 4:
-        cut = parts[0].shape[0] // 2
+        parts = dict(zip(groups[0], compute(groups[0], ())))
+        cut = parts[3].shape[0] // 2
         via_first = swap(parts[3][:cut], "head", 1)
         via_second = swap(parts[3][cut:], "head", 2)
+        parts.update(zip(groups[1], compute(groups[1], (parts[3],))))
         second = jnp.concatenate([parts[2][:cut] + via_first, parts[2][cut:]], axis=0)
         first = jnp.concatenate([parts[1][:cut], parts[1][cut:] + via_second], axis=0)
+        if len(groups) > 2:
+            parts.update(zip(groups[2], compute(groups[2], (first, second))))
         return (
             parts[0].astype(jnp.float32)
             + swap(first, "head", 1).astype(jnp.float32)
             + swap(second, "head", 2).astype(jnp.float32)
-        )
+        ), (first, second)
+    parts = compute(list(range(size)), ())
+    begun = tuple(parts)
     bit = size // 2
     while bit:
         parts = [parts[k] + swap(parts[k + bit], "head", bit) for k in range(bit)]
         bit //= 2
-    return parts[0].astype(jnp.float32)
+    return parts[0].astype(jnp.float32), begun
 
 
 def spread(pieces):
@@ -323,8 +343,126 @@
     )
 
 
-def after(values, *others):
-    return lax.optimization_barrier((values, *others))[0]
+def feed_kernel(order, inner, weights, *refs):
+    hidden, by_up, by_gate = refs[-3:]
+    gate = dot(inner[...], weights[0])
+    sigma = 1.0 / (1.0 + jnp.exp(-gate))
+    swish = gate * sigma
+    up = dot(inner[...], weights[1])
+    hidden[...] = (swish * up).astype(low)
+    by_gate[...] = swish.astype(low)
+    by_up[...] = (up * (sigma * (1.0 + gate * (1.0 - sigma)))).astype(low)
+
+
+def feed(inner, weights, group, count, earlier):
+    rows = inner.shape[0] // len(group)
+    width = inner.shape[1]
+    part = weights.shape[2]
+    shape = jax.ShapeDtypeStruct((rows * count, part), low)
+    return pl.pallas_call(
+        feed_kernel,
+        grid_spec=pltpu.PrefetchScalarGridSpec(
+            num_scalar_prefetch=1,
+            grid=(len(group),),
+            in_specs=[
+                pl.BlockSpec((rows, width), lambda i, order: (i, 0)),
+                pl.BlockSpec(
+                    weights.shape, lambda i, order: (0, 0, 0), pipeline_mode=pl.Buffered(1)
+                ),
+            ]
+            + [pl.BlockSpec(memory_space=pl.ANY)] * len(earlier),
+            out_specs=[pl.BlockSpec((rows, part), lambda i, order: (order[i], 0))] * 3,
+        ),
+        out_shape=[shape, shape, shape],
+        input_output_aliases={3 + i: i for i in range(len(earlier))},
+        compiler_params=pltpu.CompilerParams(vmem_limit_bytes=40 << 20),
+        cost_estimate=pl.CostEstimate(
+            flops=4 * inner.size * part,
+            bytes_accessed=2 * rows * len(group) * (width + 3 * part) + 2 * weights.size,
+            transcendentals=rows * len(group) * part,
+        ),
+    )(jnp.array(group, jnp.int32), inner, weights, *earlier)
+
+
+def feed_back_kernel(order, cotangent, down, weights, by_up, by_gate, *refs):
+    grads, partial = refs[-2:]
+    back = dot(cotangent[...], down[...])
+    grad_gate = (back * by_up[...].astype(jnp.float32)).astype(low)
+    grad_up = (back * by_gate[...].astype(jnp.float32)).astype(low)
+    grads[0] = grad_gate
+    grads[1] = grad_up
+    partial[...] = (
+        dot(grad_gate, weights[0], (1, 1)) + dot(grad_up, weights[1], (1, 1))
+    ).astype(low)
+
+
+def feed_back(cotangent, down, weights, by_up, by_gate, group, count, earlier):
+    total, width = cotangent.shape
+    rows = total // count
+    part = weights.shape[2]
+    tile = pl.BlockSpec((rows, part), lambda i, order: (order[i], 0))
+    return pl.pallas_call(
+        feed_back_kernel,
+        grid_spec=pltpu.PrefetchScalarGridSpec(
+            num_scalar_prefetch=1,
+            grid=(len(group),),
+            in_specs=[
+                pl.BlockSpec((rows, width), lambda i, order: (order[i], 0)),
+                pl.BlockSpec(down.shape, lambda i, order: (0, 0), pipeline_mode=pl.Buffered(1)),
+                pl.BlockSpec(
+                    weights.shape, lambda i, order: (0, 0, 0), pipeline_mode=pl.Buffered(1)
+                ),
+                tile,
+                tile,
+            ]
+            + [pl.BlockSpec(memory_space=pl.ANY)] * len(earlier),
+            out_specs=[
+                pl.BlockSpec((2, rows, part), lambda i, order: (0, order[i], 0)),
+                pl.BlockSpec((rows, width), lambda i, order: (i, 0)),
+            ],
+        ),
+        out_shape=[
+            jax.ShapeDtypeStruct((2, total, part), low),
+            jax.ShapeDtypeStruct((rows * len(group), width), low),
+        ],
+        input_output_aliases={6 + i: i for i in range(len(earlier))},
+        compiler_params=pltpu.CompilerParams(vmem_limit_bytes=48 << 20),
+        cost_estimate=pl.CostEstimate(
+            flops=6 * rows * len(group) * width * part,
+            bytes_accessed=4 * rows * len(group) * (width + 2 * part) + 6 * down.size,
+            transcendentals=0,
+        ),
+    )(jnp.array(group, jnp.int32), cotangent, down, weights, by_up, by_gate, *earlier)
+
+
+def weight_kernel(left, right, out):
+    out[0] = dot(left[...], right[0], (0, 0)).astype(low)
+
+
+def weight_terms(left, right):
+    total, width = left.shape
+    number, spare, part = right.shape
+    strip = width // lax.axis_size("batch")
+    return pl.pallas_call(
+        weight_kernel,
+        grid=(number, width // strip),
+        in_specs=[
+            pl.BlockSpec((total, strip), lambda g, i: (0, i)),
+            pl.BlockSpec((1, total, part), lambda g, i: (g, 0, 0)),
+        ],
+        out_specs=pl.BlockSpec((1, strip, part), lambda g, i: (g, i, 0)),
+        out_shape=jax.ShapeDtypeStruct((number, width, part), low),
+        compiler_params=pltpu.CompilerParams(vmem_limit_bytes=40 << 20),
+        cost_estimate=pl.CostEstimate(
+            flops=2 * number * total * width * part,
+            bytes_accessed=2 * total * (width + number * part) + 2 * number * width * part,
+            transcendentals=0,
+        ),
+    )(left, right)
+
+
+def sum_over_batch_rows(values):
+    return lax.psum_scatter(values, "batch", scatter_dimension=1, tiled=True)
 
 
 def columns_of(weights, feed_part):
@@ -440,8 +578,7 @@
     total = rows * count
     head_width = key_weight.shape[1]
     rank = query_up.shape[0]
-    feed = gate_weight.shape[1]
-    feed_part = feed // count
+    feed_part = gate_weight.shape[1] // count
     strip = gate_weight.shape[0]
 
     bounds = jnp.cumsum(lengths.reshape(-1), dtype=jnp.int32)
@@ -466,7 +603,7 @@
     groups = sending_order(count)
 
     def split(values, group):
-        return {k: values[i * rows : (i + 1) * rows] for i, k in enumerate(group)}
+        return [values[i * rows : (i + 1) * rows] for i in range(len(group))]
 
 
     inputs = tokens.astype(jnp.float32)
@@ -478,13 +615,11 @@
     value_own = dot(normed_low, value_weight).astype(low)
     lkv_own = jnp.concatenate([latent_in.astype(low), key_own, value_own], axis=1)
     gate_up_columns = columns_of(jnp.stack([gate_weight, up_weight]), feed_part)
-    gate_up_columns, lkv_own = lax.optimization_barrier((gate_up_columns, lkv_own))
+    gate_up_columns = after(gate_up_columns, lkv_own)
     gate_up_whole = lax.all_gather(gate_up_columns, "batch", axis=1, tiled=True)
-    lkv_blocks = gather_near(lkv_own)
+    lkv_blocks = gather_near(lkv_own, gate_up_columns)
     latent_last = lkv_blocks[-1]
     down_columns = columns_of(after(down_weight, latent_last).T[None], feed_part)
-    down_whole = lax.all_gather(down_columns[0], "batch", axis=0, tiled=True)
-    cotangent_all = jnp.concatenate(gather_near(after(cotangent, latent_last)), axis=0)
     latent_all = jnp.concatenate([block[:, :rank] for block in lkv_blocks], axis=0)
     keys_all, values_all = jnp.zeros((2, total, head_width), low)
     for k in range(count):
@@ -494,14 +629,15 @@
         values_all = lax.dynamic_update_slice(
             values_all, lkv_blocks[k][:, rank + head_width :], ((me ^ k) * rows, 0)
         )
-    queries, mixes, partials = {}, {}, {}
-    last = cotangent_all
-    for group in groups:
-        latents = latent_all if len(groups) == 1 else part(latent_all, group)
-        latents, last = lax.optimization_barrier((latents, last))
-        queries[group[0]], mixes[group[0]], last = attend(
+    queries, mixes = {}, {}
+    cotangent_begun = gather_begin(after(cotangent, latent_last))
+
+    def attention(group, tie):
+        if group == [0]:
+            tie += cotangent_begun
+        queries[group[0]], mixes[group[0]], partial = attend(
             spots(group),
-            latents,
+            after(part(latent_all, group), *tie),
             query_up,
             part(cosine, group),
             part(sine, group),
@@ -509,60 +645,88 @@
             values_all,
             out_weight,
         )
-        partials.update(split(last, group))
-    attention_part = scatter_near([partials[k] for k in range(count)])
+        return split(partial, group)
+
+    attention_part, _ = scatter_near(attention, groups)
     mixed_low = jnp.concatenate([mixes[group[0]] for group in sorted(groups)], axis=0)
     middle = inputs + attention_part
     inner, second_factor = rescale(middle, feed_gain)
-    inner_all = jnp.concatenate(gather_near(inner.astype(low)), axis=0)
-    gate_whole, up_whole = gate_up_whole[0], gate_up_whole[1]
-    gate = dot(inner_all, gate_whole)
-    up = dot(inner_all, up_whole)
-    sigma = jax.nn.sigmoid(gate)
-    swish = gate * sigma
-    hidden_low = (swish * up).astype(low)
-
-    def reduced(left, right):
-        return lax.psum_scatter(
-            dot(left, right, (0, 0)).astype(low), "batch", scatter_dimension=0, tiled=True
+    inner_low = inner.astype(low)
+    down_whole = lax.all_gather(after(down_columns[0], inner_low), "batch", axis=0, tiled=True)
+    found = []
+
+    def forward(blocks, group, *tie):
+        rows_in = after(jnp.concatenate(blocks, axis=0), *tie)
+        found[:] = feed(rows_in, gate_up_whole, group, count, list(found))
+
+    if count == 4:
+        begun = gather_begin(inner_low)
+        forward([inner_low], [0])
+        inner_blocks = gather_end(inner_low, tuple(after(block, found[0]) for block in begun))
+        forward(inner_blocks[1:3], [1, 2])
+        forward(inner_blocks[3:], [3])
+        cotangent_begun = tuple(after(block, inner_blocks[3]) for block in cotangent_begun)
+    else:
+        inner_blocks = gather_near(inner_low)
+        forward(inner_blocks, list(range(count)))
+    cotangent_all = jnp.concatenate(gather_end(cotangent, cotangent_begun), axis=0)
+    hidden_low, by_up, by_gate = found
+    inner_all = jnp.concatenate(inner_blocks, axis=0)
+    down_terms = weight_terms(cotangent_all, hidden_low[None])
+    down_terms, by_up = lax.optimization_barrier((down_terms, by_up))
+    down_sum = sum_over_batch_rows(down_terms)[0]
+    found = []
+    slice_width = width // count
+    normed_later = after(normed_low, down_terms)
+    normed_slices = spread(
+        [
+            lax.dynamic_slice_in_dim(normed_later, (me ^ k) * slice_width, slice_width, 1)
+            for k in range(count)
+        ]
+    )
+
+    def back(group, tie):
+        if tie:
+            tie += tuple(normed_slices)
+        grads, partial = feed_back(
+            cotangent_all,
+            after(down_whole, *tie),
+            gate_up_whole,
+            by_up,
+            by_gate,
+            group,
+            count,
+            list(found),
         )
-
-    down_part = dot(cotangent_all, hidden_low, (0, 0)).astype(low)
-    down_whole, down_part = lax.optimization_barrier((down_whole, down_part))
-    down_sum = lax.psum_scatter(down_part, "batch", scatter_dimension=0, tiled=True)
-    grad_hidden = dot(cotangent_all, down_whole)
-    slope = sigma * (1.0 + gate * (1.0 - sigma))
-    grad_gate_low = (grad_hidden * up * slope).astype(low)
-    grad_up_low = (grad_hidden * swish).astype(low)
-    grad_inner_partial = (
-        dot(grad_gate_low, gate_whole, (1, 1)) + dot(grad_up_low, up_whole, (1, 1))
-    ).astype(low)
-    gate_part = dot(inner_all, grad_gate_low, (0, 0)).astype(low)
-    up_part = dot(inner_all, grad_up_low, (0, 0)).astype(low)
-    grad_inner = scatter_near(
-        [grad_inner_partial[k * rows : (k + 1) * rows] for k in range(count)]
-    )
-    grad_inner, gate_part, up_part, hidden_low, down_sum = lax.optimization_barrier(
-        (grad_inner, gate_part, up_part, hidden_low, down_sum)
-    )
-    feed_sum = lax.psum_scatter(
-        jnp.concatenate([gate_part, up_part], axis=1), "batch", scatter_dimension=0, tiled=True
-    )
-
-    feed_partial = dot(hidden_low, down_whole, (1, 1)).astype(low)
-    feed_out = scatter_near([feed_partial[k * rows : (k + 1) * rows] for k in range(count)])
-    output = (middle + feed_out).astype(low)
+        found[:] = [grads]
+        return split(partial, group)
+
+    grad_inner, begun = scatter_near(
+        back, [groups[0], sum(groups[1:], [])] if len(groups) > 1 else groups
+    )
+    feed_terms = weight_terms(inner_all, after(found[0], *begun))
+    grad_inner, feed_terms, down_sum = lax.optimization_barrier(
+        (grad_inner, feed_terms, down_sum)
+    )
+    feed_sum = sum_over_batch_rows(feed_terms)
 
     middle_part, feed_gain_part = rescale_back(middle, second_factor, feed_gain, grad_inner)
     grad_middle = cotangent.astype(jnp.float32) + middle_part
-    branch_all = jnp.concatenate(gather_near(grad_middle.astype(low)), axis=0)
+    branch_low = grad_middle.astype(low)
+    branch_all = jnp.concatenate(gather_near(branch_low), axis=0)
+    feed_partial = dot(after(hidden_low, branch_low), down_whole, (1, 1)).astype(low)
+    branch_all, feed_partial, down_sum = lax.optimization_barrier(
+        (branch_all, feed_partial, down_sum)
+    )
     arrived_first = spread_columns(down_sum[None], strip)
     key_grads, value_grads = jnp.zeros((2, total, head_width), jnp.float32)
-    query_grads, latent_partials = {}, {}
-    for group in groups:
-        query_grads[group[0]], last, key_grads, value_grads = attend_back(
+    query_grads = {}
+    totals = [key_grads, value_grads]
+
+    def attention_back(group, tie):
+        query_grads[group[0]], partial, totals[0], totals[1] = attend_back(
             spots(group),
-            part(branch_all, group),
+            after(part(branch_all, group), *tie),
             out_weight,
             queries[group[0]],
             keys_all,
@@ -570,10 +734,12 @@
             query_up,
             part(cosine, group),
             part(sine, group),
-            key_grads,
-            value_grads,
+            *totals,
         )
-        latent_partials.update(split(last, group))
+        return split(partial, group)
+
+    latent_back, _ = scatter_near(attention_back, groups)
+    key_grads, value_grads = totals
     query_grad_low = jnp.concatenate([query_grads[group[0]] for group in sorted(groups)], axis=0)
     key_value_partials = [
         jnp.concatenate(
@@ -585,15 +751,16 @@
         ).astype(low)
         for k in range(count)
     ]
-    query_grad_low, key_value_partials, branch_all, arrived_first, feed_sum = (
-        lax.optimization_barrier(
-            (query_grad_low, key_value_partials, branch_all, arrived_first, feed_sum)
-        )
-    )
-    latent_back = scatter_near([latent_partials[k] for k in range(count)])
-    key_value_back = scatter_near(key_value_partials)
     out_part = dot(mixed_low, branch_all, (0, 0)).astype(low)
     query_part = dot(latent_all, query_grad_low, (0, 0)).astype(low)
+    query_part, out_part, key_value_partials, arrived_first, feed_sum = (
+        lax.optimization_barrier(
+            (query_part, out_part, key_value_partials, arrived_first, feed_sum)
+        )
+    )
+    key_value_back, _ = scatter_near(
+        lambda group, tie: [key_value_partials[k] for k in group], groups
+    )
     query_up_gradient, out_gradient = lax.psum((query_part, out_part), "batch")
     latent_grad, query_gain_part = rescale_back(latent, latent_factor, query_gain, latent_back)
     key_back = rotate_back(key_value_back[:, :head_width], own_cosine, own_sine)
@@ -601,18 +768,14 @@
         [latent_grad, key_back, key_value_back[:, head_width:]], axis=1
     ).astype(low)
 
-    slice_width = width // count
-    normed_slices = jnp.concatenate(
-        spread(
-            [
-                lax.dynamic_slice_in_dim(normed_low, (me ^ k) * slice_width, slice_width, 1)
-                for k in range(count)
-            ]
-        ),
-        axis=0,
-    )
     lkv_grad_all = jnp.concatenate(gather_near(lkv_grad_low), axis=0)
-    shared_part = dot(normed_slices, lkv_grad_all, (0, 0)).astype(low)
+    shared_part = dot(jnp.concatenate(normed_slices, axis=0), lkv_grad_all, (0, 0)).astype(low)
+    feed_partial = after(feed_partial, shared_part)
+    feed_out, _ = scatter_near(
+        lambda group, tie: split(part(feed_partial, group), group), groups
+    )
+    output = (middle + feed_out).astype(low)
+
     grad_normed = (
         dot(lkv_grad_low[:, :rank], query_down, (1, 1))
         + dot(lkv_grad_low[:, rank : rank + head_width], key_weight, (1, 1))
@@ -625,11 +788,12 @@
     gains = sum_over_all(
         jnp.concatenate([attention_gain_part, feed_gain_part, query_gain_part]).reshape(-1, 128)
     ).reshape(-1)
-    arrived_second = spread_columns(
-        jnp.stack(jnp.split(after(feed_sum, shared_part), 2, axis=1)), strip
-    )
+    arrived_second = spread_columns(after(feed_sum, shared_part), strip)
     shared_half = sum_over_batch(shared_part)
     blocks = gather_near(shared_half)
+    blocks, query_up_gradient, out_gradient = lax.optimization_barrier(
+        (blocks, query_up_gradient, out_gradient)
+    )
     mine = jnp.concatenate(blocks + [swap(block, "batch", 1) for block in blocks], axis=0)
     spot = jnp.arange(2 * count, dtype=jnp.int32)
     order = ((spot >> 1) ^ me) + count * ((spot & 1) ^ (lax.axis_index("batch") & 1))

time: 696 us -> 635 us (0.912)
  Pallas kernels: 80.6 us -> 172 us
  matrix products: 123 us -> 33.1 us
  waiting for transfers between devices: 261 us -> 175 us
  starting transfers between devices: 86.5 us -> 98 us
  local copies, waits for them, and re-layouts: 58.6 us -> 69.9 us
    pallas_call x0 -> x7, Pallas kernels: none -> 91.3 us  [the longest x2 36.6 us: feed_back(): pl.pallas_call(feed_back_kernel, grid_spec=pltpu.PrefetchScalarGridSpec(n...]
    dot_general x18 -> x10, matrix products: 123 us -> 33.1 us  [dot(): lax.dot_general(left, right, (((contract[0],), (contract[1],)), ((), ()))...]
    psum x1, waiting for transfers between devices: 45.9 us -> 1.65 us  [shards(): query_up_gradient, out_gradient = lax.psum((query_part, out_part), 'batch')]
    ppermute x75, waiting for transfers between devices: 215 us -> 172 us  [swap(): return lax.ppermute(values, axis, [(i, i ^ bit) for i in range(size)])]
    unnamed x208 -> x243, local copies, waits for them, and re-layouts: 22.2 us -> 40.1 us
    ppermute x75, starting transfers between devices: 85.7 us -> 97.4 us  [swap(): return lax.ppermute(values, axis, [(i, i ^ bit) for i in range(size)])]
    concatenate x5 -> x2, other arithmetic: 13.5 us -> 1.85 us  [the longest x1 1.8 us: forward(): rows_in = after(jnp.concatenate(blocks, axis=0), *tie)]
  transfers between devices with their start and end apart: 80 -> 80, of which waited for: 42 -> 31; matrix products, arithmetic and copies ran while one was open for 32% -> 21% of each run, Pallas kernels for 11% -> 27%
where the time goes in v3:
time: 635 us; the launch traced here: 627 us
  waiting for transfers between devices  175 us (28%)
  Pallas kernels  172 us (27%)
  starting transfers between devices  98 us (15%)
  local copies, waits for them, and re-layouts  69.9 us (11%)
  other arithmetic  62.8 us (10%)
  matrix products  33.1 us (5%)
  between operations  15.9 us (3%)
    ppermute x75, waiting for transfers between devices, swap(): return lax.ppermute(values, axis, [(i, i ^ bit) for i in range(size)])  172 us
    ppermute x75, starting transfers between devices, swap(): return lax.ppermute(values, axis, [(i, i ^ bit) for i in range(size)])  97.4 us
    pallas_call x3, Pallas kernels, attend_back(): pl.pallas_call(attend_back_kernel, grid_spec=pltpu.PrefetchScalarGridSpec...  42 us
    unnamed x243, local copies, waits for them, and re-layouts  40.1 us
    pallas_call x2, Pallas kernels, feed_back(): pl.pallas_call(feed_back_kernel, grid_spec=pltpu.PrefetchScalarGridSpec(n...  36.6 us
    dot_general x10, matrix products, dot(): lax.dot_general(left, right, (((contract[0],), (contract[1],)), ((), ()))...  33.1 us
    pallas_call x3, Pallas kernels, attend(): pl.pallas_call(attend_kernel, grid_spec=pltpu.PrefetchScalarGridSpec(num_...  33.1 us
    pallas_call x3, Pallas kernels, feed(): pl.pallas_call(feed_kernel, grid_spec=pltpu.PrefetchScalarGridSpec(num_sc...  27.5 us
  transfers between devices with their start and end apart: 80, of which 31 were waited for; matrix products, arithmetic and copies ran while one was open for 21% of the time, Pallas kernels for 27%

profile of v3, /device:TPU:0, one launch (start us, length us, event | category | flops | bytes accessed | tf_op | source)
XLA Modules:
  0.0 626.7 jit_solution(16961017233554190719)
XLA Ops:
  8.5 2.6 fusion.39
  11.1 2.9 collective-permute-start.1
  24.8 3.1 multiply_cosine_fusion
  42.0 13.7 %collective-permute-done = bf16[256,1536]{1,0:T(8,128)(2,1)} collective-permute-done((bf16[256,1536]{1,0:T(8,128)(2,1)}, bf16[256,1536]{1,0:T(8,128)(2,1)}, u32[]{:S(2)}, u32[]{:S(2)}) %collective-permute-start) | collective-permute-done | bytes 786464 | tf_op jit(solution)/shard_map/ppermute | solution.py:52
  70.8 9.7 %shard_map.336 = (bf16[256,1024]{1,0:T(8,128)(2,1)S(1)}, bf16[256,1024]{1,0:T(8,128)(2,1)S(1)}, bf16[256,2048]{1,0:T(8,128)(2,1)S(1)}) custom-call(s32[3]{0:T(128)S(1)} %get-tuple-element.292.spots, bf16[256,1024]{1,0:T(8,128)(2,1)S(1)} %slice.399.latent, bf16[1024,1024]{1,0:T(8,128)(2,1)S(1)} %copy-done.28, f32[256,128]{1,0:T(8,128)S(1)} %copy-done.18, ...), custom_call_target="tpu_custom_call" | custom-call | flops 2281701376 | bytes 7864320 | tf_op jit(solution)/shard_map/pallas_call | solution.py:171
  82.9 16.0 %shard_map.337 = (bf16[512,1024]{1,0:T(8,128)(2,1)S(1)}, bf16[512,1024]{1,0:T(8,128)(2,1)S(1)}, bf16[512,2048]{1,0:T(8,128)(2,1)S(1)}) custom-call(s32[4]{0:T(128)S(1)} %pad_add_fusion.2.spots, bf16[512,1024]{1,0:T(8,128)(2,1)S(1)} %pad_maximum_fusion.1.latent, bf16[1024,1024]{1,0:T(8,128)(2,1)S(1)} %copy-done.28, f32[512,128]{1,0:T(8,128)S(1)} %slice.404.cosine, ...), custom_call_target="tpu_custom_call" | custom-call | flops 4563402752 | bytes 15728640 | tf_op jit(solution)/shard_map/pallas_call | solution.py:171
  100.7 6.2 collective-permute-done.19
  121.9 7.3 %shard_map.338 = (bf16[256,1024]{1,0:T(8,128)(2,1)S(1)}, bf16[256,1024]{1,0:T(8,128)(2,1)S(1)}, bf16[256,2048]{1,0:T(8,128)(2,1)S(1)}) custom-call(s32[3]{0:T(128)S(1)} %get-tuple-element.291.spots, bf16[256,1024]{1,0:T(8,128)(2,1)S(1)} %multiply_convert_fusion.1.latent, bf16[1024,1024]{1,0:T(8,128)(2,1)S(1)} %copy-done.29, f32[256,128]{1,0:T(8,128)S(1)} %copy-done.16, ...), custom_call_target="tpu_custom_call" | custom-call | flops 2281701376 | bytes 7864320 | tf_op jit(solution)/shard_map/pallas_call | solution.py:171
  129.2 4.7 collective-permute-done.11
  133.9 3.0 collective-permute-done.12
  146.5 7.8 %shard_map.339 = (bf16[1024,1408]{1,0:T(8,128)(2,1)S(1)}, bf16[1024,1408]{1,0:T(8,128)(2,1)S(1)}, bf16[1024,1408]{1,0:T(8,128)(2,1)S(1)}) custom-call(s32[1]{0:T(128)} %constant.81.clone.order, bf16[256,2048]{1,0:T(8,128)(2,1)S(1)} %get-tuple-element.191.inner, bf16[2,2048,1408]{2,1,0:T(8,128)(2,1)} %all-gather.3.cloned.1.call-done.weights), custom_call_target="tpu_custom_call" | custom-call | flops 2952790016 | bytes 14745600 | tf_op jit(solution)/shard_map/pallas_call | solution.py:362
  154.2 9.2 %collective-permute-done.15 = bf16[256,2048]{1,0:T(8,128)(2,1)} collective-permute-done((bf16[256,2048]{1,0:T(8,128)(2,1)S(1)}, bf16[256,2048]{1,0:T(8,128)(2,1)}, u32[]{:S(2)}, u32[]{:S(2)}) %collective-permute-start.15) | collective-permute-done | bytes 1048608 | tf_op jit(solution)/shard_map/ppermute | solution.py:52
  170.1 11.9 %shard_map.340 = (bf16[1024,1408]{1,0:T(8,128)(2,1)S(1)}, bf16[1024,1408]{1,0:T(8,128)(2,1)S(1)}, bf16[1024,1408]{1,0:T(8,128)(2,1)S(1)}) custom-call(s32[2]{0:T(128)S(1)} %copy-done.22, bf16[512,2048]{1,0:T(8,128)(2,1)S(1)} %pad_maximum_fusion.inner, ...), custom_call_target="tpu_custom_call", output_to_operand_aliasing={{0}: (3, {}), {1}: (4, {}), {2}: (5, {})} | custom-call | flops 5905580032 | bytes 17956864 | tf_op jit(solution)/shard_map/pallas_call | solution.py:362
  195.0 7.8 %shard_map.341 = (bf16[1024,1408]{1,0:T(8,128)(2,1)S(1)}, bf16[1024,1408]{1,0:T(8,128)(2,1)S(1)}, bf16[1024,1408]{1,0:T(8,128)(2,1)S(1)}) custom-call(s32[1]{0:T(128)} %constant.79.clone.order, bf16[256,2048]{1,0:T(8,128)(2,1)S(1)} %get-tuple-element.262.inner, ...), custom_call_target="tpu_custom_call", output_to_operand_aliasing={{0}: (3, {}), {1}: (4, {}), {2}: (5, {})} | custom-call | flops 2952790016 | bytes 14745600 | tf_op jit(solution)/shard_map/pallas_call | solution.py:362
  206.2 8.7 %shard_map.342 = bf16[1,2048,1408]{2,1,0:T(8,128)(2,1)S(1)} custom-call(bf16[1024,2048]{1,0:T(8,128)(2,1)S(1)} %constant_dynamic-update-slice_fusion.4.left.cotangent, bf16[1,1024,1408]{2,1,0:T(8,128)(2,1)S(1)} %bitcast.117), custom_call_target="tpu_custom_call" | custom-call | flops 5905580032 | bytes 12845056 | tf_op jit(solution)/shard_map/pallas_call | solution.py:446
  228.7 12.8 %shard_map.343 = (bf16[2,1024,1408]{2,1,0:T(8,128)(2,1)}, bf16[256,2048]{1,0:T(8,128)(2,1)S(1)}) custom-call(s32[1]{0:T(128)} %constant.79.clone.order, bf16[1024,2048]{1,0:T(8,128)(2,1)} %copy-done.7, bf16[2048,1408]{1,0:T(8,128)(2,1)} %all-gather.5.cloned.1.call-done.down, bf16[2,2048,1408]{2,1,0:T(8,128)(2,1)} %all-gather.3.cloned.1.call-done.weights, ...), custom_call_target="tpu_custom_call" | custom-call | flops 4429185024 | bytes 22282240 | tf_op jit(solution)/shard_map/pallas_call | solution.py:404
  244.6 23.9 %shard_map.344 = (bf16[2,1024,1408]{2,1,0:T(8,128)(2,1)}, bf16[768,2048]{1,0:T(8,128)(2,1)}) custom-call(s32[3]{0:T(128)S(1)} %copy-done.32, bf16[1024,2048]{1,0:T(8,128)(2,1)} %copy-done.7, bf16[2048,1408]{1,0:T(8,128)(2,1)} %all-gather.5.cloned.1.call-done.down, ...), custom_call_target="tpu_custom_call", output_to_operand_aliasing={{0}: (6, {})} | custom-call | flops 13287555072 | bytes 32243712 | tf_op jit(solution)/shard_map/pallas_call | solution.py:404
  273.6 2.7 copy-done.23
  276.3 18.4 %shard_map.345 = bf16[2,2048,1408]{2,1,0:T(8,128)(2,1)} custom-call(bf16[1024,2048]{1,0:T(8,128)(2,1)S(1)} %copy-done.13, bf16[2,1024,1408]{2,1,0:T(8,128)(2,1)S(1)} %copy-done.23), custom_call_target="tpu_custom_call" | custom-call | flops 11811160064 | bytes 21495808 | tf_op jit(solution)/shard_map/pallas_call | solution.py:446
  294.7 3.4 convert_add_fusion.1
  298.8 3.5 multiply_reduce_fusion
  302.3 3.9 constant_dynamic-update-slice_fusion.18
  309.1 15.3 %collective-permute-done.29 = bf16[256,2048]{1,0:T(8,128)(2,1)S(1)} collective-permute-done((bf16[256,2048]{1,0:T(8,128)(2,1)}, bf16[256,2048]{1,0:T(8,128)(2,1)S(1)}, u32[]{:S(2)}, u32[]{:S(2)}) %collective-permute-start.29) | collective-permute-done | bytes 1048608 | tf_op jit(solution)/shard_map/ppermute | solution.py:52
  325.4 11.2 %convolution_convert_fusion = bf16[1024,2048]{1,0:T(8,128)(2,1)} fusion(bf16[1024,1408]{1,0:T(8,128)(2,1)} %copy-done.5, bf16[2048,1408]{1,0:T(8,128)(2,1)} %all-gather.5.cloned.1.call-done.down), kind=kOutput, calls=%fused_computation.6 | convolution fusion | flops 5907677184 | bytes 12845056 | tf_op jit(solution)/shard_map/dot_general | solution.py:17
  338.6 7.3 %collective-permute-done.32 = bf16[128,2048]{1,0:T(8,128)(2,1)S(1)} collective-permute-done((bf16[128,2048]{1,0:T(8,128)(2,1)S(1)}, bf16[128,2048]{1,0:T(8,128)(2,1)S(1)}, u32[]{:S(2)}, u32[]{:S(2)}) %collective-permute-start.32) | collective-permute-done | bytes 524320 | tf_op jit(solution)/shard_map/ppermute | solution.py:52
  349.4 12.3 %shard_map.346 = (bf16[256,1024]{1,0:T(8,128)(2,1)S(1)}, bf16[256,1024]{1,0:T(8,128)(2,1)S(1)}, f32[1024,256]{1,0:T(8,128)S(1)}, f32[1024,256]{1,0:T(8,128)S(1)}) custom-call(s32[3]{0:T(128)S(1)} %get-tuple-element.292.spots, bf16[256,2048]{1,0:T(8,128)(2,1)S(1)} %get-tuple-element.201.branch, bf16[1024,2048]{1,0:T(8,128)(2,1)S(1)} %copy-done.26, ...), custom_call_target="tpu_custom_call" | custom-call | flops 3288334336 | bytes 7864320 | tf_op jit(solution)/shard_map/pallas_call | solution.py:291
  366.8 6.1 convolution_convert_fusion.1
  373.0 21.1 %shard_map.347 = (bf16[512,1024]{1,0:T(8,128)(2,1)S(1)}, bf16[512,1024]{1,0:T(8,128)(2,1)S(1)}, f32[1024,256]{1,0:T(8,128)S(1)}, f32[1024,256]{1,0:T(8,128)S(1)}) custom-call(s32[4]{0:T(128)S(1)} %pad_add_fusion.2.spots, bf16[512,2048]{1,0:T(8,128)(2,1)S(1)} %slice.352.branch, bf16[1024,2048]{1,0:T(8,128)(2,1)} %out_weight.11, ...), custom_call_target="tpu_custom_call" | custom-call | flops 6576668672 | bytes 15728640 | tf_op jit(solution)/shard_map/pallas_call | solution.py:291
  399.5 8.6 %shard_map.348 = (bf16[256,1024]{1,0:T(8,128)(2,1)S(1)}, bf16[256,1024]{1,0:T(8,128)(2,1)S(1)}, f32[1024,256]{1,0:T(8,128)S(1)}, f32[1024,256]{1,0:T(8,128)S(1)}) custom-call(s32[3]{0:T(128)S(1)} %get-tuple-element.291.spots, bf16[256,2048]{1,0:T(8,128)(2,1)S(1)} %get-tuple-element.140.branch, bf16[1024,2048]{1,0:T(8,128)(2,1)S(1)} %copy-done.27, ...), custom_call_target="tpu_custom_call" | custom-call | flops 3288334336 | bytes 7864320 | tf_op jit(solution)/shard_map/pallas_call | solution.py:291
  410.4 3.7 fusion.27
  420.8 3.0 collective-permute-start.40
  450.9 3.1 collective-permute-done.55
  456.5 3.6 fusion.5
  461.3 6.6 %collective-permute-done.44 = bf16[256,1536]{1,0:T(8,128)(2,1)S(1)} collective-permute-done((bf16[256,1536]{1,0:T(8,128)(2,1)S(1)}, bf16[256,1536]{1,0:T(8,128)(2,1)S(1)}, u32[]{:S(2)}, u32[]{:S(2)}) %collective-permute-start.44) | collective-permute-done | bytes 786464 | tf_op jit(solution)/shard_map/ppermute | solution.py:52
  470.4 8.6 %collective-permute-done.46 = bf16[128,1536]{1,0:T(8,128)(2,1)S(1)} collective-permute-done((bf16[128,1536]{1,0:T(8,128)(2,1)S(1)}, bf16[128,1536]{1,0:T(8,128)(2,1)S(1)}, u32[]{:S(2)}, u32[]{:S(2)}) %collective-permute-start.46) | collective-permute-done | bytes 393248 | tf_op jit(solution)/shard_map/ppermute | solution.py:52
  488.7 5.4 collective-permute-done.72
  494.1 16.8 %collective-permute-done.48 = bf16[128,2048]{1,0:T(8,128)(2,1)S(1)} collective-permute-done((bf16[128,2048]{1,0:T(8,128)(2,1)S(1)}, bf16[128,2048]{1,0:T(8,128)(2,1)S(1)}, u32[]{:S(2)}, u32[]{:S(2)}) %collective-permute-start.48) | collective-permute-done | bytes 524320 | tf_op jit(solution)/shard_map/ppermute | solution.py:52
  515.9 4.2 collective-permute-done.58
  521.8 8.5 %collective-permute-done.59 = bf16[64,1536]{1,0:T(8,128)(2,1)S(1)} collective-permute-done((bf16[64,1536]{1,0:T(8,128)(2,1)S(1)}, bf16[64,1536]{1,0:T(8,128)(2,1)S(1)}, u32[]{:S(2)}, u32[]{:S(2)}) %collective-permute-start.59) | collective-permute-done | bytes 196640 | tf_op jit(solution)/shard_map/ppermute | solution.py:52
  530.5 7.1 %collective-permute-start.61 = (bf16[64,1536]{1,0:T(8,128)(2,1)S(1)}, bf16[64,1536]{1,0:T(8,128)(2,1)S(1)}, u32[]{:S(2)}, u32[]{:S(2)}) collective-permute-start(bf16[64,1536]{1,0:T(8,128)(2,1)S(1)} %get-tuple-element.186), channel_id=1, source_target_pairs={{0,8},{4,12},{8,0},{12,4},{16,24},{20,28},{24,16},{28,20},{1,9},{5... | collective-permute-start | bytes 589832 | tf_op jit(solution)/shard_map/ppermute | solution.py:52
  539.2 7.4 %collective-permute-done.61 = bf16[64,1536]{1,0:T(8,128)(2,1)S(1)} collective-permute-done((bf16[64,1536]{1,0:T(8,128)(2,1)S(1)}, bf16[64,1536]{1,0:T(8,128)(2,1)S(1)}, u32[]{:S(2)}, u32[]{:S(2)}) %collective-permute-start.61) | collective-permute-done | bytes 196640 | tf_op jit(solution)/shard_map/ppermute | solution.py:52
  546.6 4.2 collective-permute-start.62
  550.8 13.9 %collective-permute-done.62 = bf16[64,1536]{1,0:T(8,128)(2,1)S(1)} collective-permute-done((bf16[64,1536]{1,0:T(8,128)(2,1)S(1)}, bf16[64,1536]{1,0:T(8,128)(2,1)S(1)}, u32[]{:S(2)}, u32[]{:S(2)}) %collective-permute-start.62) | collective-permute-done | bytes 196640 | tf_op jit(solution)/shard_map/ppermute | solution.py:52
  566.5 10.0 %collective-permute-done.63 = bf16[64,1536]{1,0:T(8,128)(2,1)S(1)} collective-permute-done((bf16[64,1536]{1,0:T(8,128)(2,1)S(1)}, bf16[64,1536]{1,0:T(8,128)(2,1)S(1)}, u32[]{:S(2)}, u32[]{:S(2)}) %collective-permute-start.63) | collective-permute-done | bytes 196640 | tf_op jit(solution)/shard_map/ppermute | solution.py:52
  577.7 13.6 %collective-permute-done.64 = bf16[256,1536]{1,0:T(8,128)(2,1)S(1)} collective-permute-done((bf16[256,1536]{1,0:T(8,128)(2,1)S(1)}, bf16[256,1536]{1,0:T(8,128)(2,1)S(1)}, u32[]{:S(2)}, u32[]{:S(2)}) %collective-permute-start.64) | collective-permute-done | bytes 786464 | tf_op jit(solution)/shard_map/ppermute | solution.py:52
  596.4 2.8 collective-permute-done.66
  607.0 4.4 convert_element_type.237
  614.2 5.8 shard_map.349
  (527 shorter events, 213.0 us)
Async XLA Ops:
  7.2 139.3 %all-gather.3.cloned.1.call-start = ((), (), s32[]{:S(2)}) async-start(), calls=%async_computation.2 | async-start | bytes 12976128 | tf_op jit(solution)/shard_map/all_gather | solution.py:619
  11.1 20.0 %collective-permute-start.1 = (bf16[2,64,1408]{2,1,0:T(8,128)(2,1)}, bf16[2,64,1408]{2,1,0:T(8,128)(2,1)}, u32[]{:S(2)}, u32[]{:S(2)}) collective-permute-start(bf16[2,64,1408]{2,1,0:T(8,128)(2,1)} %get-tuple-element.217), channel_id=1, source_target_pairs={{0,1},{1,0},{2,3},{3,2},{4,5},{5,4},{6,7},{7,6},{8,9},{9,8},{10,11... | collective-permute-start | bytes 1081352 | tf_op jit(solution)/shard_map/ppermute | solution.py:52
  14.1 18.9 %collective-permute-start.2 = (bf16[2,64,1408]{2,1,0:T(8,128)(2,1)}, bf16[2,64,1408]{2,1,0:T(8,128)(2,1)}, u32[]{:S(2)}, u32[]{:S(2)}) collective-permute-start(bf16[2,64,1408]{2,1,0:T(8,128)(2,1)} %get-tuple-element.218), channel_id=1, source_target_pairs={{0,2},{1,3},{2,0},{3,1},{4,6},{5,7},{6,4},{7,5},{8,10},{9,11},{10,... | collective-permute-start | bytes 1081352 | tf_op jit(solution)/shard_map/ppermute | solution.py:52
  15.6 19.2 %collective-permute-start.3 = (bf16[2,64,1408]{2,1,0:T(8,128)(2,1)}, bf16[2,64,1408]{2,1,0:T(8,128)(2,1)}, u32[]{:S(2)}, u32[]{:S(2)}) collective-permute-start(bf16[2,64,1408]{2,1,0:T(8,128)(2,1)} %get-tuple-element.215), channel_id=1, source_target_pairs={{0,3},{1,2},{2,1},{3,0},{4,7},{5,6},{6,5},{7,4},{8,11},{9,10},{10,... | collective-permute-start | bytes 1081352 | tf_op jit(solution)/shard_map/ppermute | solution.py:52
  36.6 190.2 %all-gather.5.cloned.1.call-start = ((), (), s32[]{:S(2)}) async-start(), calls=%async_computation.3 | async-start | bytes 6488064 | tf_op jit(solution)/shard_map/all_gather | solution.py:655
  36.6 19.1 %collective-permute-start = (bf16[256,1536]{1,0:T(8,128)(2,1)}, bf16[256,1536]{1,0:T(8,128)(2,1)}, u32[]{:S(2)}, u32[]{:S(2)}) collective-permute-start(bf16[256,1536]{1,0:T(8,128)(2,1)} %pad_maximum_fusion.8), channel_id=1, source_target_pairs={{0,1},{1,0},{2,3},{3,2},{4,5},{5,4},{6,7},{7,6},{8,9},{9,8},{10,11... | collective-permute-start | bytes 2359304 | tf_op jit(solution)/shard_map/ppermute | solution.py:52
  38.6 18.5 %collective-permute-start.4 = (bf16[256,1536]{1,0:T(8,128)(2,1)}, bf16[256,1536]{1,0:T(8,128)(2,1)}, u32[]{:S(2)}, u32[]{:S(2)}) collective-permute-start(bf16[256,1536]{1,0:T(8,128)(2,1)} %pad_maximum_fusion.8), channel_id=1, source_target_pairs={{0,2},{1,3},{2,0},{3,1},{4,6},{5,7},{6,4},{7,5},{8,10},{9,11},{10,... | collective-permute-start | bytes 2359304 | tf_op jit(solution)/shard_map/ppermute | solution.py:52
  69.5 48.6 %collective-permute-start.10 = (bf16[256,2048]{1,0:T(8,128)(2,1)}, bf16[256,2048]{1,0:T(8,128)(2,1)}, u32[]{:S(2)}, u32[]{:S(2)}) collective-permute-start(bf16[256,2048]{1,0:T(8,128)(2,1)} %param.38), channel_id=1, source_target_pairs={{0,2},{1,3},{2,0},{3,1},{4,6},{5,7},{6,4},{7,5},{8,10},{9,11},{10,... | collective-permute-start | bytes 3145736 | tf_op jit(solution)/shard_map/ppermute | solution.py:52
  70.0 48.1 %collective-permute-start.9 = (bf16[256,2048]{1,0:T(8,128)(2,1)}, bf16[256,2048]{1,0:T(8,128)(2,1)}, u32[]{:S(2)}, u32[]{:S(2)}) collective-permute-start(bf16[256,2048]{1,0:T(8,128)(2,1)} %param.38), channel_id=1, source_target_pairs={{0,1},{1,0},{2,3},{3,2},{4,5},{5,4},{6,7},{7,6},{8,9},{9,8},{10,11... | collective-permute-start | bytes 3145736 | tf_op jit(solution)/shard_map/ppermute | solution.py:52
  80.6 28.4 %collective-permute-start.7 = (bf16[128,2048]{1,0:T(8,128)(2,1)S(1)}, bf16[128,2048]{1,0:T(8,128)(2,1)S(1)}, u32[]{:S(2)}, u32[]{:S(2)}) collective-permute-start(bf16[128,2048]{1,0:T(8,128)(2,1)S(1)} %get-tuple-element.239), channel_id=1, source_target_pairs={{0,2},{1,3},{2,0},{3,1},{4,6},{5,7},{6,4},{7,5},{8,10},{9,11},{10,... | collective-permute-start | bytes 1572872 | tf_op jit(solution)/shard_map/ppermute | solution.py:52
  80.7 29.3 %collective-permute-start.8 = (bf16[128,2048]{1,0:T(8,128)(2,1)S(1)}, bf16[128,2048]{1,0:T(8,128)(2,1)S(1)}, u32[]{:S(2)}, u32[]{:S(2)}) collective-permute-start(bf16[128,2048]{1,0:T(8,128)(2,1)S(1)} %get-tuple-element.240), channel_id=1, source_target_pairs={{0,1},{1,0},{2,3},{3,2},{4,5},{5,4},{6,7},{7,6},{8,9},{9,8},{10,11... | collective-permute-start | bytes 1572872 | tf_op jit(solution)/shard_map/ppermute | solution.py:52
  82.1 24.8 %collective-permute-start.19 = (bf16[1,64,1408]{2,1,0:T(8,128)(2,1)S(1)}, bf16[1,64,1408]{2,1,0:T(8,128)(2,1)S(1)}, u32[]{:S(2)}, u32[]{:S(2)}) collective-permute-start(bf16[1,64,1408]{2,1,0:T(8,128)(2,1)S(1)} %get-tuple-element.258), channel_id=1, source_target_pairs={{0,1},{1,0},{2,3},{3,2},{4,5},{5,4},{6,7},{7,6},{8,9},{9,8},{10,11... | collective-permute-start | bytes 540680 | tf_op jit(solution)/shard_map/ppermute | solution.py:52
  111.3 22.7 %collective-permute-start.11 = (bf16[256,2048]{1,0:T(8,128)(2,1)}, bf16[256,2048]{1,0:T(8,128)(2,1)}, u32[]{:S(2)}, u32[]{:S(2)}) collective-permute-start(bf16[256,2048]{1,0:T(8,128)(2,1)} %pad_maximum_fusion.2), channel_id=1, source_target_pairs={{0,1},{1,0},{2,3},{3,2},{4,5},{5,4},{6,7},{7,6},{8,9},{9,8},{10,11... | collective-permute-start | bytes 3145736 | tf_op jit(solution)/shard_map/ppermute | solution.py:52
  113.9 23.0 %collective-permute-start.12 = (bf16[256,2048]{1,0:T(8,128)(2,1)}, bf16[256,2048]{1,0:T(8,128)(2,1)}, u32[]{:S(2)}, u32[]{:S(2)}) collective-permute-start(bf16[256,2048]{1,0:T(8,128)(2,1)} %pad_maximum_fusion.3), channel_id=1, source_target_pairs={{0,2},{1,3},{2,0},{3,1},{4,6},{5,7},{6,4},{7,5},{8,10},{9,11},{10,... | collective-permute-start | bytes 3145736 | tf_op jit(solution)/shard_map/ppermute | solution.py:52
  141.1 156.9 %reduce-scatter.3.cloned.1.call-start = ((), (), s32[]{:S(2)}) async-start(), calls=%async_computation.4 | async-start | bytes 6488064 | tf_op jit(solution)/shard_map/reduce_scatter | solution.py:465
  141.2 22.2 %collective-permute-start.15 = (bf16[256,2048]{1,0:T(8,128)(2,1)S(1)}, bf16[256,2048]{1,0:T(8,128)(2,1)}, u32[]{:S(2)}, u32[]{:S(2)}) collective-permute-start(bf16[256,2048]{1,0:T(8,128)(2,1)S(1)} %get-tuple-element.191.inner), channel_id=1, source_target_pairs={{0,2},{1,3},{2,0},{3,1},{4,6},{5,7},{6,4},{7,5},{8,10},{9,11},{10,... | collective-permute-start | bytes 3145736 | tf_op jit(solution)/shard_map/ppermute | solution.py:52
  142.7 20.7 %collective-permute-start.13 = (bf16[256,2048]{1,0:T(8,128)(2,1)S(1)}, bf16[256,2048]{1,0:T(8,128)(2,1)}, u32[]{:S(2)}, u32[]{:S(2)}) collective-permute-start(bf16[256,2048]{1,0:T(8,128)(2,1)S(1)} %get-tuple-element.191.inner), channel_id=1, source_target_pairs={{0,1},{1,0},{2,3},{3,2},{4,5},{5,4},{6,7},{7,6},{8,9},{9,8},{10,11... | collective-permute-start | bytes 3145736 | tf_op jit(solution)/shard_map/ppermute | solution.py:52
  164.5 22.1 %collective-permute-start.14 = (bf16[128,2048]{1,0:T(8,128)(2,1)S(1)}, bf16[128,2048]{1,0:T(8,128)(2,1)S(1)}, u32[]{:S(2)}, u32[]{:S(2)}) collective-permute-start(bf16[128,2048]{1,0:T(8,128)(2,1)S(1)} %slice.338), channel_id=1, source_target_pairs={{0,2},{1,3},{2,0},{3,1},{4,6},{5,7},{6,4},{7,5},{8,10},{9,11},{10,... | collective-permute-start | bytes 1572872 | tf_op jit(solution)/shard_map/ppermute | solution.py:52
  166.6 21.0 %collective-permute-start.16 = (bf16[128,2048]{1,0:T(8,128)(2,1)S(1)}, bf16[128,2048]{1,0:T(8,128)(2,1)S(1)}, u32[]{:S(2)}, u32[]{:S(2)}) collective-permute-start(bf16[128,2048]{1,0:T(8,128)(2,1)S(1)} %slice.339), channel_id=1, source_target_pairs={{0,1},{1,0},{2,3},{3,2},{4,5},{5,4},{6,7},{7,6},{8,9},{9,8},{10,11... | collective-permute-start | bytes 1572872 | tf_op jit(solution)/shard_map/ppermute | solution.py:52
  189.6 16.5 %collective-permute-start.17 = (bf16[128,2048]{1,0:T(8,128)(2,1)S(1)}, bf16[128,2048]{1,0:T(8,128)(2,1)S(1)}, u32[]{:S(2)}, u32[]{:S(2)}) collective-permute-start(bf16[128,2048]{1,0:T(8,128)(2,1)S(1)} %slice.340), channel_id=1, source_target_pairs={{0,2},{1,3},{2,0},{3,1},{4,6},{5,7},{6,4},{7,5},{8,10},{9,11},{10,... | collective-permute-start | bytes 1572872 | tf_op jit(solution)/shard_map/ppermute | solution.py:52
  221.1 199.6 %reduce-scatter.5.cloned.1.call-start = ((), (), s32[]{:S(2)}) async-start(), calls=%async_computation.5 | async-start | bytes 12976128 | tf_op jit(solution)/shard_map/reduce_scatter | solution.py:465
  223.3 21.3 %collective-permute-start.22 = (bf16[256,512]{1,0:T(8,128)(2,1)}, bf16[256,512]{1,0:T(8,128)(2,1)S(1)}, u32[]{:S(2)}, u32[]{:S(2)}) collective-permute-start(bf16[256,512]{1,0:T(8,128)(2,1)} %get-tuple-element.237), channel_id=1, source_target_pairs={{0,1},{1,0},{2,3},{3,2},{4,5},{5,4},{6,7},{7,6},{8,9},{9,8},{10,11... | collective-permute-start | bytes 786440 | tf_op jit(solution)/shard_map/ppermute | solution.py:52
  224.2 20.4 %collective-permute-start.23 = (bf16[256,512]{1,0:T(8,128)(2,1)}, bf16[256,512]{1,0:T(8,128)(2,1)S(1)}, u32[]{:S(2)}, u32[]{:S(2)}) collective-permute-start(bf16[256,512]{1,0:T(8,128)(2,1)} %get-tuple-element.236), channel_id=1, source_target_pairs={{0,2},{1,3},{2,0},{3,1},{4,6},{5,7},{6,4},{7,5},{8,10},{9,11},{10,... | collective-permute-start | bytes 786440 | tf_op jit(solution)/shard_map/ppermute | solution.py:52
  225.8 18.8 %collective-permute-start.24 = (bf16[256,512]{1,0:T(8,128)(2,1)}, bf16[256,512]{1,0:T(8,128)(2,1)S(1)}, u32[]{:S(2)}, u32[]{:S(2)}) collective-permute-start(bf16[256,512]{1,0:T(8,128)(2,1)} %get-tuple-element.235), channel_id=1, source_target_pairs={{0,3},{1,2},{2,1},{3,0},{4,7},{5,6},{6,5},{7,4},{8,11},{9,10},{10,... | collective-permute-start | bytes 786440 | tf_op jit(solution)/shard_map/ppermute | solution.py:52
  241.6 26.9 %collective-permute-start.25 = (bf16[128,2048]{1,0:T(8,128)(2,1)S(1)}, bf16[128,2048]{1,0:T(8,128)(2,1)S(1)}, u32[]{:S(2)}, u32[]{:S(2)}) collective-permute-start(bf16[128,2048]{1,0:T(8,128)(2,1)S(1)} %get-tuple-element.233), channel_id=1, source_target_pairs={{0,2},{1,3},{2,0},{3,1},{4,6},{5,7},{6,4},{7,5},{8,10},{9,11},{10,... | collective-permute-start | bytes 1572872 | tf_op jit(solution)/shard_map/ppermute | solution.py:52
  242.9 25.6 %collective-permute-start.27 = (bf16[128,2048]{1,0:T(8,128)(2,1)S(1)}, bf16[128,2048]{1,0:T(8,128)(2,1)S(1)}, u32[]{:S(2)}, u32[]{:S(2)}) collective-permute-start(bf16[128,2048]{1,0:T(8,128)(2,1)S(1)} %get-tuple-element.234), channel_id=1, source_target_pairs={{0,1},{1,0},{2,3},{3,2},{4,5},{5,4},{6,7},{7,6},{8,9},{9,8},{10,11... | collective-permute-start | bytes 1572872 | tf_op jit(solution)/shard_map/ppermute | solution.py:52
  271.3 23.4 %collective-permute-start.26 = (bf16[256,2048]{1,0:T(8,128)(2,1)}, bf16[256,2048]{1,0:T(8,128)(2,1)S(1)}, u32[]{:S(2)}, u32[]{:S(2)}) collective-permute-start(bf16[256,2048]{1,0:T(8,128)(2,1)} %pad_maximum_fusion.4), channel_id=1, source_target_pairs={{0,1},{1,0},{2,3},{3,2},{4,5},{5,4},{6,7},{7,6},{8,9},{9,8},{10,11... | collective-permute-start | bytes 3145736 | tf_op jit(solution)/shard_map/ppermute | solution.py:52
  272.9 21.8 %collective-permute-start.28 = (bf16[256,2048]{1,0:T(8,128)(2,1)}, bf16[256,2048]{1,0:T(8,128)(2,1)}, u32[]{:S(2)}, u32[]{:S(2)}) collective-permute-start(bf16[256,2048]{1,0:T(8,128)(2,1)} %pad_maximum_fusion.5), channel_id=1, source_target_pairs={{0,2},{1,3},{2,0},{3,1},{4,6},{5,7},{6,4},{7,5},{8,10},{9,11},{10,... | collective-permute-start | bytes 3145736 | tf_op jit(solution)/shard_map/ppermute | solution.py:52
  298.1 304.9 %all-reduce.3.cloned.1.call-start = ((), (), s32[]{:S(2)}) async-start(), calls=%async_computation.6 | async-start | bytes 12582912 | tf_op jit(solution)/shard_map/psum | solution.py:764
  306.2 18.1 %collective-permute-start.29 = (bf16[256,2048]{1,0:T(8,128)(2,1)}, bf16[256,2048]{1,0:T(8,128)(2,1)S(1)}, u32[]{:S(2)}, u32[]{:S(2)}) collective-permute-start(bf16[256,2048]{1,0:T(8,128)(2,1)} %get-tuple-element.188), channel_id=1, source_target_pairs={{0,1},{1,0},{2,3},{3,2},{4,5},{5,4},{6,7},{7,6},{8,9},{9,8},{10,11... | collective-permute-start | bytes 3145736 | tf_op jit(solution)/shard_map/ppermute | solution.py:52
  307.6 29.1 %collective-permute-start.30 = (bf16[256,2048]{1,0:T(8,128)(2,1)}, bf16[256,2048]{1,0:T(8,128)(2,1)S(1)}, u32[]{:S(2)}, u32[]{:S(2)}) collective-permute-start(bf16[256,2048]{1,0:T(8,128)(2,1)} %get-tuple-element.188), channel_id=1, source_target_pairs={{0,2},{1,3},{2,0},{3,1},{4,6},{5,7},{6,4},{7,5},{8,10},{9,11},{10,... | collective-permute-start | bytes 3145736 | tf_op jit(solution)/shard_map/ppermute | solution.py:52
  361.8 32.4 %collective-permute-start.33 = (bf16[128,1024]{1,0:T(8,128)(2,1)S(1)}, bf16[128,1024]{1,0:T(8,128)(2,1)S(1)}, u32[]{:S(2)}, u32[]{:S(2)}) collective-permute-start(bf16[128,1024]{1,0:T(8,128)(2,1)S(1)} %get-tuple-element.260), channel_id=1, source_target_pairs={{0,2},{1,3},{2,0},{3,1},{4,6},{5,7},{6,4},{7,5},{8,10},{9,11},{10,... | collective-permute-start | bytes 786440 | tf_op jit(solution)/shard_map/ppermute | solution.py:52
  361.8 32.3 %collective-permute-start.34 = (bf16[128,1024]{1,0:T(8,128)(2,1)S(1)}, bf16[128,1024]{1,0:T(8,128)(2,1)S(1)}, u32[]{:S(2)}, u32[]{:S(2)}) collective-permute-start(bf16[128,1024]{1,0:T(8,128)(2,1)S(1)} %get-tuple-element.259), channel_id=1, source_target_pairs={{0,1},{1,0},{2,3},{3,2},{4,5},{5,4},{6,7},{7,6},{8,9},{9,8},{10,11... | collective-permute-start | bytes 786440 | tf_op jit(solution)/shard_map/ppermute | solution.py:52
  363.0 57.6 %collective-permute-start.37 = (bf16[1,64,1408]{2,1,0:T(8,128)(2,1)}, bf16[1,64,1408]{2,1,0:T(8,128)(2,1)}, u32[]{:S(2)}, u32[]{:S(2)}) collective-permute-start(bf16[1,64,1408]{2,1,0:T(8,128)(2,1)} %get-tuple-element.254), channel_id=1, source_target_pairs={{0,1},{1,0},{2,3},{3,2},{4,5},{5,4},{6,7},{7,6},{8,9},{9,8},{10,11... | collective-permute-start | bytes 540680 | tf_op jit(solution)/shard_map/ppermute | solution.py:52
  364.8 55.9 %collective-permute-start.38 = (bf16[1,64,1408]{2,1,0:T(8,128)(2,1)}, bf16[1,64,1408]{2,1,0:T(8,128)(2,1)}, u32[]{:S(2)}, u32[]{:S(2)}) collective-permute-start(bf16[1,64,1408]{2,1,0:T(8,128)(2,1)} %get-tuple-element.253), channel_id=1, source_target_pairs={{0,2},{1,3},{2,0},{3,1},{4,6},{5,7},{6,4},{7,5},{8,10},{9,11},{10,... | collective-permute-start | bytes 540680 | tf_op jit(solution)/shard_map/ppermute | solution.py:52
  366.8 53.9 %collective-permute-start.39 = (bf16[1,64,1408]{2,1,0:T(8,128)(2,1)}, bf16[1,64,1408]{2,1,0:T(8,128)(2,1)}, u32[]{:S(2)}, u32[]{:S(2)}) collective-permute-start(bf16[1,64,1408]{2,1,0:T(8,128)(2,1)} %get-tuple-element.252), channel_id=1, source_target_pairs={{0,3},{1,2},{2,1},{3,0},{4,7},{5,6},{6,5},{7,4},{8,11},{9,10},{10,... | collective-permute-start | bytes 540680 | tf_op jit(solution)/shard_map/ppermute | solution.py:52
  395.1 19.0 %collective-permute-start.36 = (bf16[256,1024]{1,0:T(8,128)(2,1)}, bf16[256,1024]{1,0:T(8,128)(2,1)S(1)}, u32[]{:S(2)}, u32[]{:S(2)}) collective-permute-start(bf16[256,1024]{1,0:T(8,128)(2,1)} %pad_maximum_fusion.12), channel_id=1, source_target_pairs={{0,2},{1,3},{2,0},{3,1},{4,6},{5,7},{6,4},{7,5},{8,10},{9,11},{10,... | collective-permute-start | bytes 1572872 | tf_op jit(solution)/shard_map/ppermute | solution.py:52
  447.8 20.1 %collective-permute-start.44 = (bf16[256,1536]{1,0:T(8,128)(2,1)S(1)}, bf16[256,1536]{1,0:T(8,128)(2,1)S(1)}, u32[]{:S(2)}, u32[]{:S(2)}) collective-permute-start(bf16[256,1536]{1,0:T(8,128)(2,1)S(1)} %get-tuple-element.244), channel_id=1, source_target_pairs={{0,1},{1,0},{2,3},{3,2},{4,5},{5,4},{6,7},{7,6},{8,9},{9,8},{10,11... | collective-permute-start | bytes 2359304 | tf_op jit(solution)/shard_map/ppermute | solution.py:52
  449.7 20.2 %collective-permute-start.45 = (bf16[256,1536]{1,0:T(8,128)(2,1)S(1)}, bf16[256,1536]{1,0:T(8,128)(2,1)S(1)}, u32[]{:S(2)}, u32[]{:S(2)}) collective-permute-start(bf16[256,1536]{1,0:T(8,128)(2,1)S(1)} %get-tuple-element.244), channel_id=1, source_target_pairs={{0,2},{1,3},{2,0},{3,1},{4,6},{5,7},{6,4},{7,5},{8,10},{9,11},{10,... | collective-permute-start | bytes 2359304 | tf_op jit(solution)/shard_map/ppermute | solution.py:52
  483.1 94.4 %collective-permute-start.73 = (bf16[2,64,1408]{2,1,0:T(8,128)(2,1)S(1)}, bf16[2,64,1408]{2,1,0:T(8,128)(2,1)S(1)}, u32[]{:S(2)}, u32[]{:S(2)}) collective-permute-start(bf16[2,64,1408]{2,1,0:T(8,128)(2,1)S(1)} %get-tuple-element.213), channel_id=1, source_target_pairs={{0,2},{1,3},{2,0},{3,1},{4,6},{5,7},{6,4},{7,5},{8,10},{9,11},{10,... | collective-permute-start | bytes 1081352 | tf_op jit(solution)/shard_map/ppermute | solution.py:52
  484.6 93.1 %collective-permute-start.74 = (bf16[2,64,1408]{2,1,0:T(8,128)(2,1)S(1)}, bf16[2,64,1408]{2,1,0:T(8,128)(2,1)S(1)}, u32[]{:S(2)}, u32[]{:S(2)}) collective-permute-start(bf16[2,64,1408]{2,1,0:T(8,128)(2,1)S(1)} %get-tuple-element.212), channel_id=1, source_target_pairs={{0,3},{1,2},{2,1},{3,0},{4,7},{5,6},{6,5},{7,4},{8,11},{9,10},{10,... | collective-permute-start | bytes 1081352 | tf_op jit(solution)/shard_map/ppermute | solution.py:52
  486.4 24.5 %collective-permute-start.48 = (bf16[128,2048]{1,0:T(8,128)(2,1)S(1)}, bf16[128,2048]{1,0:T(8,128)(2,1)S(1)}, u32[]{:S(2)}, u32[]{:S(2)}) collective-permute-start(bf16[128,2048]{1,0:T(8,128)(2,1)S(1)} %get-tuple-element.197), channel_id=1, source_target_pairs={{0,2},{1,3},{2,0},{3,1},{4,6},{5,7},{6,4},{7,5},{8,10},{9,11},{10,... | collective-permute-start | bytes 1572872 | tf_op jit(solution)/shard_map/ppermute | solution.py:52
  486.8 24.1 %collective-permute-start.50 = (bf16[128,2048]{1,0:T(8,128)(2,1)S(1)}, bf16[128,2048]{1,0:T(8,128)(2,1)S(1)}, u32[]{:S(2)}, u32[]{:S(2)}) collective-permute-start(bf16[128,2048]{1,0:T(8,128)(2,1)S(1)} %get-tuple-element.196), channel_id=1, source_target_pairs={{0,1},{1,0},{2,3},{3,2},{4,5},{5,4},{6,7},{7,6},{8,9},{9,8},{10,11... | collective-permute-start | bytes 1572872 | tf_op jit(solution)/shard_map/ppermute | solution.py:52
  494.0 17.0 %collective-permute-start.57 = (bf16[256,1536]{1,0:T(8,128)(2,1)S(1)}, bf16[256,1536]{1,0:T(8,128)(2,1)S(1)}, u32[]{:S(2)}, u32[]{:S(2)}) collective-permute-start(bf16[256,1536]{1,0:T(8,128)(2,1)S(1)} %constant_dynamic-slice_fusion.6), channel_id=1, source_target_pairs={{0,4},{4,0},{8,12},{12,8},{16,20},{20,16},{24,28},{28,24},{1,5},{5... | collective-permute-start | bytes 2359304 | tf_op jit(solution)/shard_map/ppermute | solution.py:52
  511.9 18.4 %collective-permute-start.59 = (bf16[64,1536]{1,0:T(8,128)(2,1)S(1)}, bf16[64,1536]{1,0:T(8,128)(2,1)S(1)}, u32[]{:S(2)}, u32[]{:S(2)}) collective-permute-start(bf16[64,1536]{1,0:T(8,128)(2,1)S(1)} %get-tuple-element.243), channel_id=1, source_target_pairs={{0,16},{4,20},{8,24},{12,28},{16,0},{20,4},{24,8},{28,12},{1,17},{... | collective-permute-start | bytes 589832 | tf_op jit(solution)/shard_map/ppermute | solution.py:52
  520.1 74.7 %collective-permute-start.49 = (bf16[256,2048]{1,0:T(8,128)(2,1)S(1)}, bf16[256,2048]{1,0:T(8,128)(2,1)S(1)}, u32[]{:S(2)}, u32[]{:S(2)}) collective-permute-start(bf16[256,2048]{1,0:T(8,128)(2,1)S(1)} %pad_maximum_fusion.6), channel_id=1, source_target_pairs={{0,1},{1,0},{2,3},{3,2},{4,5},{5,4},{6,7},{7,6},{8,9},{9,8},{10,11... | collective-permute-start | bytes 3145736 | tf_op jit(solution)/shard_map/ppermute | solution.py:52
  537.7 57.1 %collective-permute-start.51 = (bf16[256,2048]{1,0:T(8,128)(2,1)S(1)}, bf16[256,2048]{1,0:T(8,128)(2,1)S(1)}, u32[]{:S(2)}, u32[]{:S(2)}) collective-permute-start(bf16[256,2048]{1,0:T(8,128)(2,1)S(1)} %pad_maximum_fusion.7), channel_id=1, source_target_pairs={{0,2},{1,3},{2,0},{3,1},{4,6},{5,7},{6,4},{7,5},{8,10},{9,11},{10,... | collective-permute-start | bytes 3145736 | tf_op jit(solution)/shard_map/ppermute | solution.py:52
  546.6 18.1 %collective-permute-start.62 = (bf16[64,1536]{1,0:T(8,128)(2,1)S(1)}, bf16[64,1536]{1,0:T(8,128)(2,1)S(1)}, u32[]{:S(2)}, u32[]{:S(2)}) collective-permute-start(bf16[64,1536]{1,0:T(8,128)(2,1)S(1)} %get-tuple-element.186), channel_id=1, source_target_pairs={{0,16},{4,20},{8,24},{12,28},{16,0},{20,4},{24,8},{28,12},{1,17},{... | collective-permute-start | bytes 589832 | tf_op jit(solution)/shard_map/ppermute | solution.py:52
  (143 other events, 1077.9 us)
Sparse Core Ops, SparseCore 0:
  36.7 109.7 all-gather.2
  148.1 58.7 all-gather.4
  221.2 64.6 reduce-scatter.2
  298.2 119.2 reduce-scatter.4
  447.7 155.2 all-reduce.2

commit v4 on v3

--- a/solution.py
+++ b/solution.py
@@ -662,10 +662,11 @@
     if count == 4:
         begun = gather_begin(inner_low)
         forward([inner_low], [0])
-        inner_blocks = gather_end(inner_low, tuple(after(block, found[0]) for block in begun))
+        begun = tuple(after(block, found[0]) for block in begun)
+        inner_blocks = gather_end(inner_low, begun)
         forward(inner_blocks[1:3], [1, 2])
         forward(inner_blocks[3:], [3])
-        cotangent_begun = tuple(after(block, inner_blocks[3]) for block in cotangent_begun)
+        cotangent_begun = tuple(after(block, *begun) for block in cotangent_begun)
     else:
         inner_blocks = gather_near(inner_low)
         forward(inner_blocks, list(range(count)))
@@ -713,8 +714,8 @@
     middle_part, feed_gain_part = rescale_back(middle, second_factor, feed_gain, grad_inner)
     grad_middle = cotangent.astype(jnp.float32) + middle_part
     branch_low = grad_middle.astype(low)
-    branch_all = jnp.concatenate(gather_near(branch_low), axis=0)
     feed_partial = dot(after(hidden_low, branch_low), down_whole, (1, 1)).astype(low)
+    branch_all = jnp.concatenate(gather_near(branch_low, feed_partial), axis=0)
     branch_all, feed_partial, down_sum = lax.optimization_barrier(
         (branch_all, feed_partial, down_sum)
     )
@@ -753,11 +754,10 @@
     ]
     out_part = dot(mixed_low, branch_all, (0, 0)).astype(low)
     query_part = dot(latent_all, query_grad_low, (0, 0)).astype(low)
-    query_part, out_part, key_value_partials, arrived_first, feed_sum = (
-        lax.optimization_barrier(
-            (query_part, out_part, key_value_partials, arrived_first, feed_sum)
-        )
-    )
+    query_part, out_part, arrived_first, feed_sum = lax.optimization_barrier(
+        (query_part, out_part, arrived_first, feed_sum)
+    )
+    key_value_partials = after(key_value_partials, feed_sum)
     key_value_back, _ = scatter_near(
         lambda group, tie: [key_value_partials[k] for k in group], groups
     )
@@ -786,7 +786,9 @@
     )
     input_gradient = grad_middle + input_part
     gains = sum_over_all(
-        jnp.concatenate([attention_gain_part, feed_gain_part, query_gain_part]).reshape(-1, 128)
+        after(
+            jnp.concatenate([attention_gain_part, feed_gain_part, query_gain_part]), shared_part
+        ).reshape(-1, 128)
     ).reshape(-1)
     arrived_second = spread_columns(after(feed_sum, shared_part), strip)
     shared_half = sum_over_batch(shared_part)

time: 635 us -> 629 us (level)
  starting transfers between devices: 98 us -> 90.7 us
    ppermute x75, starting transfers between devices: 97.4 us -> 90.1 us  [swap(): return lax.ppermute(values, axis, [(i, i ^ bit) for i in range(size)])]
    unnamed x243 -> x235, local copies, waits for them, and re-layouts: 40.1 us -> 39.2 us
  transfers between devices with their start and end apart: 80 -> 80, of which waited for: 31 -> 33; matrix products, arithmetic and copies ran while one was open for 21% -> 23% of each run, Pallas kernels for 27% -> 27%
where the time goes in v4:
time: 629 us; the launch traced here: 622 us
  Pallas kernels  174 us (28%)
  waiting for transfers between devices  172 us (27%)
  starting transfers between devices  90.7 us (14%)
  local copies, waits for them, and re-layouts  73.4 us (12%)
  other arithmetic  60.8 us (10%)
  matrix products  35.4 us (6%)
  between operations  16.1 us (3%)
    ppermute x75, waiting for transfers between devices, swap(): return lax.ppermute(values, axis, [(i, i ^ bit) for i in range(size)])  168 us
    ppermute x75, starting transfers between devices, swap(): return lax.ppermute(values, axis, [(i, i ^ bit) for i in range(size)])  90.1 us
    pallas_call x3, Pallas kernels, attend_back(): pl.pallas_call(attend_back_kernel, grid_spec=pltpu.PrefetchScalarGridSpec...  42 us
    unnamed x235, local copies, waits for them, and re-layouts  39.2 us
    pallas_call x2, Pallas kernels, feed_back(): pl.pallas_call(feed_back_kernel, grid_spec=pltpu.PrefetchScalarGridSpec(n...  36.7 us
    dot_general x10, matrix products, dot(): lax.dot_general(left, right, (((contract[0],), (contract[1],)), ((), ()))...  35.4 us
    pallas_call x3, Pallas kernels, attend(): pl.pallas_call(attend_kernel, grid_spec=pltpu.PrefetchScalarGridSpec(num_...  33 us
    pallas_call x3, Pallas kernels, feed(): pl.pallas_call(feed_kernel, grid_spec=pltpu.PrefetchScalarGridSpec(num_sc...  29.2 us
  transfers between devices with their start and end apart: 80, of which 33 were waited for; matrix products, arithmetic and copies ran while one was open for 23% of the time, Pallas kernels for 27%

profile of v4, /device:TPU:0, one launch (start us, length us, event | category | flops | bytes accessed | tf_op | source)
XLA Modules:
  0.0 622.4 jit_solution(17565054069302688036)
XLA Ops:
  11.1 3.9 collective-permute-start.3
  41.3 14.6 %collective-permute-done.4 = bf16[256,1536]{1,0:T(8,128)(2,1)} collective-permute-done((bf16[256,1536]{1,0:T(8,128)(2,1)}, bf16[256,1536]{1,0:T(8,128)(2,1)}, u32[]{:S(2)}, u32[]{:S(2)}) %collective-permute-start.4) | collective-permute-done | bytes 786464 | tf_op jit(solution)/shard_map/ppermute | solution.py:52
  65.8 2.9 collective-permute-done.5
  72.5 9.7 %shard_map.336 = (bf16[256,1024]{1,0:T(8,128)(2,1)S(1)}, bf16[256,1024]{1,0:T(8,128)(2,1)S(1)}, bf16[256,2048]{1,0:T(8,128)(2,1)S(1)}) custom-call(s32[3]{0:T(128)S(1)} %get-tuple-element.294.spots, bf16[256,1024]{1,0:T(8,128)(2,1)S(1)} %slice.399.latent, bf16[1024,1024]{1,0:T(8,128)(2,1)S(1)} %copy-done.29, f32[256,128]{1,0:T(8,128)S(1)} %get-tuple-element.269.cosine, ...), custom_call_target="tpu_custom_call" | custom-call | flops 2281701376 | bytes 7864320 | tf_op jit(solution)/shard_map/pallas_call | solution.py:171
  83.1 16.0 %shard_map.337 = (bf16[512,1024]{1,0:T(8,128)(2,1)S(1)}, bf16[512,1024]{1,0:T(8,128)(2,1)S(1)}, bf16[512,2048]{1,0:T(8,128)(2,1)S(1)}) custom-call(s32[4]{0:T(128)S(1)} %pad_add_fusion.2.spots, bf16[512,1024]{1,0:T(8,128)(2,1)S(1)} %pad_maximum_fusion.1.latent, bf16[1024,1024]{1,0:T(8,128)(2,1)S(1)} %copy-done.29, f32[512,128]{1,0:T(8,128)S(1)} %slice.404.cosine, ...), custom_call_target="tpu_custom_call" | custom-call | flops 4563402752 | bytes 15728640 | tf_op jit(solution)/shard_map/pallas_call | solution.py:171
  105.2 3.5 collective-permute-done.8
  119.0 7.3 %shard_map.338 = (bf16[256,1024]{1,0:T(8,128)(2,1)S(1)}, bf16[256,1024]{1,0:T(8,128)(2,1)S(1)}, bf16[256,2048]{1,0:T(8,128)(2,1)S(1)}) custom-call(s32[3]{0:T(128)S(1)} %get-tuple-element.293.spots, bf16[256,1024]{1,0:T(8,128)(2,1)S(1)} %multiply_convert_fusion.1.latent, bf16[1024,1024]{1,0:T(8,128)(2,1)S(1)} %copy-done.30, ...), custom_call_target="tpu_custom_call" | custom-call | flops 2281701376 | bytes 7864320 | tf_op jit(solution)/shard_map/pallas_call | solution.py:171
  126.4 6.5 %collective-permute-done.12 = bf16[256,2048]{1,0:T(8,128)(2,1)} collective-permute-done((bf16[256,2048]{1,0:T(8,128)(2,1)}, bf16[256,2048]{1,0:T(8,128)(2,1)}, u32[]{:S(2)}, u32[]{:S(2)}) %collective-permute-start.12) | collective-permute-done | bytes 1048608 | tf_op jit(solution)/shard_map/ppermute | solution.py:52
  141.8 3.8 all-gather.3.cloned.1.call-done.weights
  145.6 7.8 %shard_map.339 = (bf16[1024,1408]{1,0:T(8,128)(2,1)S(1)}, bf16[1024,1408]{1,0:T(8,128)(2,1)S(1)}, bf16[1024,1408]{1,0:T(8,128)(2,1)S(1)}) custom-call(s32[1]{0:T(128)} %constant.81.clone.order, bf16[256,2048]{1,0:T(8,128)(2,1)S(1)} %get-tuple-element.197.inner, bf16[2,2048,1408]{2,1,0:T(8,128)(2,1)} %all-gather.3.cloned.1.call-done.weights), custom_call_target="tpu_custom_call" | custom-call | flops 2952790016 | bytes 14745600 | tf_op jit(solution)/shard_map/pallas_call | solution.py:362
  153.3 5.5 collective-permute-done.14
  170.3 12.2 %shard_map.340 = (bf16[1024,1408]{1,0:T(8,128)(2,1)S(1)}, bf16[1024,1408]{1,0:T(8,128)(2,1)S(1)}, bf16[1024,1408]{1,0:T(8,128)(2,1)S(1)}) custom-call(s32[2]{0:T(128)S(1)} %copy-done.23, bf16[512,2048]{1,0:T(8,128)(2,1)S(1)} %pad_maximum_fusion.inner, ...), custom_call_target="tpu_custom_call", output_to_operand_aliasing={{0}: (3, {}), {1}: (4, {}), {2}: (5, {})} | custom-call | flops 5905580032 | bytes 17956864 | tf_op jit(solution)/shard_map/pallas_call | solution.py:362
  186.6 9.2 %shard_map.341 = (bf16[1024,1408]{1,0:T(8,128)(2,1)S(1)}, bf16[1024,1408]{1,0:T(8,128)(2,1)S(1)}, bf16[1024,1408]{1,0:T(8,128)(2,1)S(1)}) custom-call(s32[1]{0:T(128)} %constant.79.clone.order, bf16[256,2048]{1,0:T(8,128)(2,1)S(1)} %pad_maximum_fusion.4.inner, ...), custom_call_target="tpu_custom_call", output_to_operand_aliasing={{0}: (3, {}), {1}: (4, {}), {2}: (5, {})} | custom-call | flops 2952790016 | bytes 14745600 | tf_op jit(solution)/shard_map/pallas_call | solution.py:362
  199.2 8.7 %shard_map.342 = bf16[1,2048,1408]{2,1,0:T(8,128)(2,1)S(1)} custom-call(bf16[1024,2048]{1,0:T(8,128)(2,1)S(1)} %constant_dynamic-update-slice_fusion.2.left.cotangent, bf16[1,1024,1408]{2,1,0:T(8,128)(2,1)S(1)} %bitcast.115), custom_call_target="tpu_custom_call" | custom-call | flops 5905580032 | bytes 12845056 | tf_op jit(solution)/shard_map/pallas_call | solution.py:446
  223.6 12.9 %shard_map.343 = (bf16[2,1024,1408]{2,1,0:T(8,128)(2,1)}, bf16[256,2048]{1,0:T(8,128)(2,1)S(1)}) custom-call(s32[1]{0:T(128)} %constant.79.clone.order, bf16[1024,2048]{1,0:T(8,128)(2,1)} %copy-done.8, bf16[2048,1408]{1,0:T(8,128)(2,1)} %all-gather.5.cloned.1.call-done.down, bf16[2,2048,1408]{2,1,0:T(8,128)(2,1)} %all-gather.3.cloned.1.call-done.weights, ...), custom_call_target="tpu_custom_call" | custom-call | flops 4429185024 | bytes 22282240 | tf_op jit(solution)/shard_map/pallas_call | solution.py:404
  238.4 23.8 %shard_map.344 = (bf16[2,1024,1408]{2,1,0:T(8,128)(2,1)}, bf16[768,2048]{1,0:T(8,128)(2,1)}) custom-call(s32[3]{0:T(128)S(1)} %copy-done.33, bf16[1024,2048]{1,0:T(8,128)(2,1)} %copy-done.8, bf16[2048,1408]{1,0:T(8,128)(2,1)} %all-gather.5.cloned.1.call-done.down, ...), custom_call_target="tpu_custom_call", output_to_operand_aliasing={{0}: (6, {})} | custom-call | flops 13287555072 | bytes 32243712 | tf_op jit(solution)/shard_map/pallas_call | solution.py:404
  268.9 18.4 %shard_map.345 = bf16[2,2048,1408]{2,1,0:T(8,128)(2,1)} custom-call(bf16[1024,2048]{1,0:T(8,128)(2,1)S(1)} %constant_dynamic-update-slice_fusion.7.left, bf16[2,1024,1408]{2,1,0:T(8,128)(2,1)S(1)} %copy-done.24), custom_call_target="tpu_custom_call" | custom-call | flops 11811160064 | bytes 21495808 | tf_op jit(solution)/shard_map/pallas_call | solution.py:446
  287.3 3.4 convert_add_fusion.1
  291.4 3.5 multiply_reduce_fusion
  294.9 4.4 constant_dynamic-update-slice_fusion.16
  300.6 11.0 %convolution_convert_fusion = bf16[1024,2048]{1,0:T(8,128)(2,1)} fusion(bf16[1024,1408]{1,0:T(8,128)(2,1)S(1)} %copy-done.6, bf16[2048,1408]{1,0:T(8,128)(2,1)} %all-gather.5.cloned.1.call-done.down), kind=kOutput, calls=%fused_computation.6 | convolution fusion | flops 5907677184 | bytes 12845056 | tf_op jit(solution)/shard_map/dot_general | solution.py:17
  311.6 9.8 %collective-permute-done.29 = bf16[256,2048]{1,0:T(8,128)(2,1)S(1)} collective-permute-done((bf16[256,2048]{1,0:T(8,128)(2,1)}, bf16[256,2048]{1,0:T(8,128)(2,1)S(1)}, u32[]{:S(2)}, u32[]{:S(2)}) %collective-permute-start.29) | collective-permute-done | bytes 1048608 | tf_op jit(solution)/shard_map/ppermute | solution.py:52
  328.1 7.6 %collective-permute-done.31 = bf16[128,2048]{1,0:T(8,128)(2,1)} collective-permute-done((bf16[128,2048]{1,0:T(8,128)(2,1)}, bf16[128,2048]{1,0:T(8,128)(2,1)}, u32[]{:S(2)}, u32[]{:S(2)}) %collective-permute-start.31) | collective-permute-done | bytes 524320 | tf_op jit(solution)/shard_map/ppermute | solution.py:52
  348.0 12.3 %shard_map.346 = (bf16[256,1024]{1,0:T(8,128)(2,1)S(1)}, bf16[256,1024]{1,0:T(8,128)(2,1)S(1)}, f32[1024,256]{1,0:T(8,128)S(1)}, f32[1024,256]{1,0:T(8,128)S(1)}) custom-call(s32[3]{0:T(128)S(1)} %get-tuple-element.294.spots, bf16[256,2048]{1,0:T(8,128)(2,1)S(1)} %get-tuple-element.206.branch, bf16[1024,2048]{1,0:T(8,128)(2,1)S(1)} %copy-done.27, ...), custom_call_target="tpu_custom_call" | custom-call | flops 3288334336 | bytes 7864320 | tf_op jit(solution)/shard_map/pallas_call | solution.py:291
  360.6 8.5 %convolution_convert_fusion.1 = bf16[1024,2048]{1,0:T(8,128)(2,1)} fusion(bf16[1024,2048]{1,0:T(8,128)(2,1)} %constant_dynamic-update-slice_fusion.12, bf16[256,1024]{1,0:T(8,128)(2,1)S(1)} %copy-done.35, bf16[512,1024]{1,0:T(8,128)(2,1)S(1)} %copy-done.45, bf16[256,1024]{1,0:T(8,128)(2,1)S(1)} %copy-done.41), kind=kOutput, calls=%fused_computation.7 | convolution fusion | flops 4303355904 | bytes 10485760 | tf_op jit(solution)/shard_map/dot_general | solution.py:17
  369.2 21.2 %shard_map.347 = (bf16[512,1024]{1,0:T(8,128)(2,1)S(1)}, bf16[512,1024]{1,0:T(8,128)(2,1)S(1)}, f32[1024,256]{1,0:T(8,128)S(1)}, f32[1024,256]{1,0:T(8,128)S(1)}) custom-call(s32[4]{0:T(128)S(1)} %pad_add_fusion.2.spots, bf16[512,2048]{1,0:T(8,128)(2,1)S(1)} %slice.352.branch, bf16[1024,2048]{1,0:T(8,128)(2,1)} %out_weight.11, ...), custom_call_target="tpu_custom_call" | custom-call | flops 6576668672 | bytes 15728640 | tf_op jit(solution)/shard_map/pallas_call | solution.py:291
  396.1 8.6 %shard_map.348 = (bf16[256,1024]{1,0:T(8,128)(2,1)S(1)}, bf16[256,1024]{1,0:T(8,128)(2,1)S(1)}, f32[1024,256]{1,0:T(8,128)S(1)}, f32[1024,256]{1,0:T(8,128)S(1)}) custom-call(s32[3]{0:T(128)S(1)} %get-tuple-element.293.spots, bf16[256,2048]{1,0:T(8,128)(2,1)S(1)} %get-tuple-element.145.branch, bf16[1024,2048]{1,0:T(8,128)(2,1)S(1)} %copy-done.28, ...), custom_call_target="tpu_custom_call" | custom-call | flops 3288334336 | bytes 7864320 | tf_op jit(solution)/shard_map/pallas_call | solution.py:291
  407.0 3.7 fusion.27
  417.3 2.9 collective-permute-start.40
  430.8 6.0 collective-permute-done.43
  444.2 8.2 %collective-permute-done.44 = bf16[256,1536]{1,0:T(8,128)(2,1)S(1)} collective-permute-done((bf16[256,1536]{1,0:T(8,128)(2,1)S(1)}, bf16[256,1536]{1,0:T(8,128)(2,1)S(1)}, u32[]{:S(2)}, u32[]{:S(2)}) %collective-permute-start.44) | collective-permute-done | bytes 786464 | tf_op jit(solution)/shard_map/ppermute | solution.py:52
  456.2 8.2 %collective-permute-done.46 = bf16[128,1536]{1,0:T(8,128)(2,1)S(1)} collective-permute-done((bf16[128,1536]{1,0:T(8,128)(2,1)S(1)}, bf16[128,1536]{1,0:T(8,128)(2,1)S(1)}, u32[]{:S(2)}, u32[]{:S(2)}) %collective-permute-start.46) | collective-permute-done | bytes 393248 | tf_op jit(solution)/shard_map/ppermute | solution.py:52
  465.7 3.1 convolution_convert_fusion.2
  491.8 6.1 collective-permute-done.50
  497.9 4.2 collective-permute-done.48
  506.6 8.8 %collective-permute-done.58 = bf16[64,1536]{1,0:T(8,128)(2,1)S(1)} collective-permute-done((bf16[64,1536]{1,0:T(8,128)(2,1)S(1)}, bf16[64,1536]{1,0:T(8,128)(2,1)S(1)}, u32[]{:S(2)}, u32[]{:S(2)}) %collective-permute-start.58) | collective-permute-done | bytes 196640 | tf_op jit(solution)/shard_map/ppermute | solution.py:52
  517.0 7.9 %collective-permute-done.60 = bf16[64,1536]{1,0:T(8,128)(2,1)S(1)} collective-permute-done((bf16[64,1536]{1,0:T(8,128)(2,1)S(1)}, bf16[64,1536]{1,0:T(8,128)(2,1)S(1)}, u32[]{:S(2)}, u32[]{:S(2)}) %collective-permute-start.60) | collective-permute-done | bytes 196640 | tf_op jit(solution)/shard_map/ppermute | solution.py:52
  524.8 6.0 collective-permute-done.59
  535.1 6.3 %collective-permute-done.61 = bf16[64,1536]{1,0:T(8,128)(2,1)S(1)} collective-permute-done((bf16[64,1536]{1,0:T(8,128)(2,1)S(1)}, bf16[64,1536]{1,0:T(8,128)(2,1)S(1)}, u32[]{:S(2)}, u32[]{:S(2)}) %collective-permute-start.61) | collective-permute-done | bytes 196640 | tf_op jit(solution)/shard_map/ppermute | solution.py:52
  541.4 3.8 collective-permute-start.62
  545.2 13.5 %collective-permute-done.62 = bf16[64,1536]{1,0:T(8,128)(2,1)S(1)} collective-permute-done((bf16[64,1536]{1,0:T(8,128)(2,1)S(1)}, bf16[64,1536]{1,0:T(8,128)(2,1)S(1)}, u32[]{:S(2)}, u32[]{:S(2)}) %collective-permute-start.62) | collective-permute-done | bytes 196640 | tf_op jit(solution)/shard_map/ppermute | solution.py:52
  558.8 2.8 collective-permute-start.63
  561.6 8.9 %collective-permute-done.63 = bf16[64,1536]{1,0:T(8,128)(2,1)S(1)} collective-permute-done((bf16[64,1536]{1,0:T(8,128)(2,1)S(1)}, bf16[64,1536]{1,0:T(8,128)(2,1)S(1)}, u32[]{:S(2)}, u32[]{:S(2)}) %collective-permute-start.63) | collective-permute-done | bytes 196640 | tf_op jit(solution)/shard_map/ppermute | solution.py:52
  573.0 13.7 %collective-permute-done.65 = bf16[256,1536]{1,0:T(8,128)(2,1)S(1)} collective-permute-done((bf16[256,1536]{1,0:T(8,128)(2,1)S(1)}, bf16[256,1536]{1,0:T(8,128)(2,1)S(1)}, u32[]{:S(2)}, u32[]{:S(2)}) %collective-permute-start.65) | collective-permute-done | bytes 786464 | tf_op jit(solution)/shard_map/ppermute | solution.py:52
  591.6 3.2 collective-permute-done.67
  594.8 2.9 collective-permute-done.66
  605.2 4.4 convert_element_type.237
  609.9 5.8 shard_map.349
  (520 shorter events, 218.9 us)
Async XLA Ops:
  7.2 138.4 %all-gather.3.cloned.1.call-start = ((), (), s32[]{:S(2)}) async-start(), calls=%async_computation.2 | async-start | bytes 12976128 | tf_op jit(solution)/shard_map/all_gather | solution.py:619
  11.1 24.2 %collective-permute-start.3 = (bf16[2,64,1408]{2,1,0:T(8,128)(2,1)}, bf16[2,64,1408]{2,1,0:T(8,128)(2,1)}, u32[]{:S(2)}, u32[]{:S(2)}) collective-permute-start(bf16[2,64,1408]{2,1,0:T(8,128)(2,1)} %get-tuple-element.221), channel_id=1, source_target_pairs={{0,3},{1,2},{2,1},{3,0},{4,7},{5,6},{6,5},{7,4},{8,11},{9,10},{10,... | collective-permute-start | bytes 1081352 | tf_op jit(solution)/shard_map/ppermute | solution.py:52
  15.0 16.7 %collective-permute-start.1 = (bf16[2,64,1408]{2,1,0:T(8,128)(2,1)}, bf16[2,64,1408]{2,1,0:T(8,128)(2,1)}, u32[]{:S(2)}, u32[]{:S(2)}) collective-permute-start(bf16[2,64,1408]{2,1,0:T(8,128)(2,1)} %get-tuple-element.223), channel_id=1, source_target_pairs={{0,1},{1,0},{2,3},{3,2},{4,5},{5,4},{6,7},{7,6},{8,9},{9,8},{10,11... | collective-permute-start | bytes 1081352 | tf_op jit(solution)/shard_map/ppermute | solution.py:52
  15.6 18.0 %collective-permute-start.2 = (bf16[2,64,1408]{2,1,0:T(8,128)(2,1)}, bf16[2,64,1408]{2,1,0:T(8,128)(2,1)}, u32[]{:S(2)}, u32[]{:S(2)}) collective-permute-start(bf16[2,64,1408]{2,1,0:T(8,128)(2,1)} %get-tuple-element.224), channel_id=1, source_target_pairs={{0,2},{1,3},{2,0},{3,1},{4,6},{5,7},{6,4},{7,5},{8,10},{9,11},{10,... | collective-permute-start | bytes 1081352 | tf_op jit(solution)/shard_map/ppermute | solution.py:52
  37.1 184.7 %all-gather.5.cloned.1.call-start = ((), (), s32[]{:S(2)}) async-start(), calls=%async_computation.3 | async-start | bytes 6488064 | tf_op jit(solution)/shard_map/all_gather | solution.py:655
  37.1 18.8 %collective-permute-start.4 = (bf16[256,1536]{1,0:T(8,128)(2,1)}, bf16[256,1536]{1,0:T(8,128)(2,1)}, u32[]{:S(2)}, u32[]{:S(2)}) collective-permute-start(bf16[256,1536]{1,0:T(8,128)(2,1)} %pad_maximum_fusion.9), channel_id=1, source_target_pairs={{0,2},{1,3},{2,0},{3,1},{4,6},{5,7},{6,4},{7,5},{8,10},{9,11},{10,... | collective-permute-start | bytes 2359304 | tf_op jit(solution)/shard_map/ppermute | solution.py:52
  37.5 18.8 %collective-permute-start = (bf16[256,1536]{1,0:T(8,128)(2,1)}, bf16[256,1536]{1,0:T(8,128)(2,1)}, u32[]{:S(2)}, u32[]{:S(2)}) collective-permute-start(bf16[256,1536]{1,0:T(8,128)(2,1)} %pad_maximum_fusion.9), channel_id=1, source_target_pairs={{0,1},{1,0},{2,3},{3,2},{4,5},{5,4},{6,7},{7,6},{8,9},{9,8},{10,11... | collective-permute-start | bytes 2359304 | tf_op jit(solution)/shard_map/ppermute | solution.py:52
  68.8 46.3 %collective-permute-start.10 = (bf16[256,2048]{1,0:T(8,128)(2,1)}, bf16[256,2048]{1,0:T(8,128)(2,1)}, u32[]{:S(2)}, u32[]{:S(2)}) collective-permute-start(bf16[256,2048]{1,0:T(8,128)(2,1)} %param.38), channel_id=1, source_target_pairs={{0,2},{1,3},{2,0},{3,1},{4,6},{5,7},{6,4},{7,5},{8,10},{9,11},{10,... | collective-permute-start | bytes 3145736 | tf_op jit(solution)/shard_map/ppermute | solution.py:52
  70.2 44.9 %collective-permute-start.9 = (bf16[256,2048]{1,0:T(8,128)(2,1)}, bf16[256,2048]{1,0:T(8,128)(2,1)}, u32[]{:S(2)}, u32[]{:S(2)}) collective-permute-start(bf16[256,2048]{1,0:T(8,128)(2,1)} %param.38), channel_id=1, source_target_pairs={{0,1},{1,0},{2,3},{3,2},{4,5},{5,4},{6,7},{7,6},{8,9},{9,8},{10,11... | collective-permute-start | bytes 3145736 | tf_op jit(solution)/shard_map/ppermute | solution.py:52
  70.8 30.0 %collective-permute-start.17 = (bf16[1,64,1408]{2,1,0:T(8,128)(2,1)S(1)}, bf16[1,64,1408]{2,1,0:T(8,128)(2,1)S(1)}, u32[]{:S(2)}, u32[]{:S(2)}) collective-permute-start(bf16[1,64,1408]{2,1,0:T(8,128)(2,1)S(1)} %get-tuple-element.264), channel_id=1, source_target_pairs={{0,1},{1,0},{2,3},{3,2},{4,5},{5,4},{6,7},{7,6},{8,9},{9,8},{10,11... | collective-permute-start | bytes 540680 | tf_op jit(solution)/shard_map/ppermute | solution.py:52
  82.3 22.0 %collective-permute-start.7 = (bf16[128,2048]{1,0:T(8,128)(2,1)S(1)}, bf16[128,2048]{1,0:T(8,128)(2,1)S(1)}, u32[]{:S(2)}, u32[]{:S(2)}) collective-permute-start(bf16[128,2048]{1,0:T(8,128)(2,1)S(1)} %get-tuple-element.245), channel_id=1, source_target_pairs={{0,2},{1,3},{2,0},{3,1},{4,6},{5,7},{6,4},{7,5},{8,10},{9,11},{10,... | collective-permute-start | bytes 1572872 | tf_op jit(solution)/shard_map/ppermute | solution.py:52
  83.1 25.6 %collective-permute-start.8 = (bf16[128,2048]{1,0:T(8,128)(2,1)S(1)}, bf16[128,2048]{1,0:T(8,128)(2,1)S(1)}, u32[]{:S(2)}, u32[]{:S(2)}) collective-permute-start(bf16[128,2048]{1,0:T(8,128)(2,1)S(1)} %get-tuple-element.246), channel_id=1, source_target_pairs={{0,1},{1,0},{2,3},{3,2},{4,5},{5,4},{6,7},{7,6},{8,9},{9,8},{10,11... | collective-permute-start | bytes 1572872 | tf_op jit(solution)/shard_map/ppermute | solution.py:52
  110.0 22.9 %collective-permute-start.12 = (bf16[256,2048]{1,0:T(8,128)(2,1)}, bf16[256,2048]{1,0:T(8,128)(2,1)}, u32[]{:S(2)}, u32[]{:S(2)}) collective-permute-start(bf16[256,2048]{1,0:T(8,128)(2,1)} %pad_maximum_fusion.3), channel_id=1, source_target_pairs={{0,2},{1,3},{2,0},{3,1},{4,6},{5,7},{6,4},{7,5},{8,10},{9,11},{10,... | collective-permute-start | bytes 3145736 | tf_op jit(solution)/shard_map/ppermute | solution.py:52
  113.7 19.5 %collective-permute-start.11 = (bf16[256,2048]{1,0:T(8,128)(2,1)}, bf16[256,2048]{1,0:T(8,128)(2,1)}, u32[]{:S(2)}, u32[]{:S(2)}) collective-permute-start(bf16[256,2048]{1,0:T(8,128)(2,1)} %pad_maximum_fusion.2), channel_id=1, source_target_pairs={{0,1},{1,0},{2,3},{3,2},{4,5},{5,4},{6,7},{7,6},{8,9},{9,8},{10,11... | collective-permute-start | bytes 3145736 | tf_op jit(solution)/shard_map/ppermute | solution.py:52
  137.4 153.3 %reduce-scatter.3.cloned.1.call-start = ((), (), s32[]{:S(2)}) async-start(), calls=%async_computation.4 | async-start | bytes 6488064 | tf_op jit(solution)/shard_map/reduce_scatter | solution.py:465
  137.4 21.4 %collective-permute-start.14 = (bf16[256,2048]{1,0:T(8,128)(2,1)S(1)}, bf16[256,2048]{1,0:T(8,128)(2,1)}, u32[]{:S(2)}, u32[]{:S(2)}) collective-permute-start(bf16[256,2048]{1,0:T(8,128)(2,1)S(1)} %get-tuple-element.197.inner), channel_id=1, source_target_pairs={{0,2},{1,3},{2,0},{3,1},{4,6},{5,7},{6,4},{7,5},{8,10},{9,11},{10,... | collective-permute-start | bytes 3145736 | tf_op jit(solution)/shard_map/ppermute | solution.py:52
  138.6 21.4 %collective-permute-start.13 = (bf16[256,2048]{1,0:T(8,128)(2,1)S(1)}, bf16[256,2048]{1,0:T(8,128)(2,1)}, u32[]{:S(2)}, u32[]{:S(2)}) collective-permute-start(bf16[256,2048]{1,0:T(8,128)(2,1)S(1)} %get-tuple-element.197.inner), channel_id=1, source_target_pairs={{0,1},{1,0},{2,3},{3,2},{4,5},{5,4},{6,7},{7,6},{8,9},{9,8},{10,11... | collective-permute-start | bytes 3145736 | tf_op jit(solution)/shard_map/ppermute | solution.py:52
  164.4 22.1 %collective-permute-start.21 = (bf16[128,2048]{1,0:T(8,128)(2,1)S(1)}, bf16[128,2048]{1,0:T(8,128)(2,1)S(1)}, u32[]{:S(2)}, u32[]{:S(2)}) collective-permute-start(bf16[128,2048]{1,0:T(8,128)(2,1)S(1)} %slice.341), channel_id=1, source_target_pairs={{0,1},{1,0},{2,3},{3,2},{4,5},{5,4},{6,7},{7,6},{8,9},{9,8},{10,11... | collective-permute-start | bytes 1572872 | tf_op jit(solution)/shard_map/ppermute | solution.py:52
  165.9 20.6 %collective-permute-start.20 = (bf16[128,2048]{1,0:T(8,128)(2,1)S(1)}, bf16[128,2048]{1,0:T(8,128)(2,1)S(1)}, u32[]{:S(2)}, u32[]{:S(2)}) collective-permute-start(bf16[128,2048]{1,0:T(8,128)(2,1)S(1)} %slice.340), channel_id=1, source_target_pairs={{0,2},{1,3},{2,0},{3,1},{4,6},{5,7},{6,4},{7,5},{8,10},{9,11},{10,... | collective-permute-start | bytes 1572872 | tf_op jit(solution)/shard_map/ppermute | solution.py:52
  166.5 19.9 %collective-permute-start.16 = (bf16[128,2048]{1,0:T(8,128)(2,1)S(1)}, bf16[128,2048]{1,0:T(8,128)(2,1)S(1)}, u32[]{:S(2)}, u32[]{:S(2)}) collective-permute-start(bf16[128,2048]{1,0:T(8,128)(2,1)S(1)} %slice.339), channel_id=1, source_target_pairs={{0,1},{1,0},{2,3},{3,2},{4,5},{5,4},{6,7},{7,6},{8,9},{9,8},{10,11... | collective-permute-start | bytes 1572872 | tf_op jit(solution)/shard_map/ppermute | solution.py:52
  167.1 19.3 %collective-permute-start.15 = (bf16[128,2048]{1,0:T(8,128)(2,1)S(1)}, bf16[128,2048]{1,0:T(8,128)(2,1)S(1)}, u32[]{:S(2)}, u32[]{:S(2)}) collective-permute-start(bf16[128,2048]{1,0:T(8,128)(2,1)S(1)} %slice.338), channel_id=1, source_target_pairs={{0,2},{1,3},{2,0},{3,1},{4,6},{5,7},{6,4},{7,5},{8,10},{9,11},{10,... | collective-permute-start | bytes 1572872 | tf_op jit(solution)/shard_map/ppermute | solution.py:52
  212.1 205.2 %reduce-scatter.5.cloned.1.call-start = ((), (), s32[]{:S(2)}) async-start(), calls=%async_computation.5 | async-start | bytes 12976128 | tf_op jit(solution)/shard_map/reduce_scatter | solution.py:465
  218.3 19.6 %collective-permute-start.24 = (bf16[256,512]{1,0:T(8,128)(2,1)}, bf16[256,512]{1,0:T(8,128)(2,1)}, u32[]{:S(2)}, u32[]{:S(2)}) collective-permute-start(bf16[256,512]{1,0:T(8,128)(2,1)} %get-tuple-element.241), channel_id=1, source_target_pairs={{0,3},{1,2},{2,1},{3,0},{4,7},{5,6},{6,5},{7,4},{8,11},{9,10},{10,... | collective-permute-start | bytes 786440 | tf_op jit(solution)/shard_map/ppermute | solution.py:52
  218.9 19.1 %collective-permute-start.23 = (bf16[256,512]{1,0:T(8,128)(2,1)}, bf16[256,512]{1,0:T(8,128)(2,1)}, u32[]{:S(2)}, u32[]{:S(2)}) collective-permute-start(bf16[256,512]{1,0:T(8,128)(2,1)} %get-tuple-element.242), channel_id=1, source_target_pairs={{0,2},{1,3},{2,0},{3,1},{4,6},{5,7},{6,4},{7,5},{8,10},{9,11},{10,... | collective-permute-start | bytes 786440 | tf_op jit(solution)/shard_map/ppermute | solution.py:52
  220.1 17.8 %collective-permute-start.22 = (bf16[256,512]{1,0:T(8,128)(2,1)}, bf16[256,512]{1,0:T(8,128)(2,1)}, u32[]{:S(2)}, u32[]{:S(2)}) collective-permute-start(bf16[256,512]{1,0:T(8,128)(2,1)} %get-tuple-element.243), channel_id=1, source_target_pairs={{0,1},{1,0},{2,3},{3,2},{4,5},{5,4},{6,7},{7,6},{8,9},{9,8},{10,11... | collective-permute-start | bytes 786440 | tf_op jit(solution)/shard_map/ppermute | solution.py:52
  236.6 25.6 %collective-permute-start.25 = (bf16[128,2048]{1,0:T(8,128)(2,1)S(1)}, bf16[128,2048]{1,0:T(8,128)(2,1)S(1)}, u32[]{:S(2)}, u32[]{:S(2)}) collective-permute-start(bf16[128,2048]{1,0:T(8,128)(2,1)S(1)} %get-tuple-element.239), channel_id=1, source_target_pairs={{0,2},{1,3},{2,0},{3,1},{4,6},{5,7},{6,4},{7,5},{8,10},{9,11},{10,... | collective-permute-start | bytes 1572872 | tf_op jit(solution)/shard_map/ppermute | solution.py:52
  237.5 24.7 %collective-permute-start.27 = (bf16[128,2048]{1,0:T(8,128)(2,1)S(1)}, bf16[128,2048]{1,0:T(8,128)(2,1)S(1)}, u32[]{:S(2)}, u32[]{:S(2)}) collective-permute-start(bf16[128,2048]{1,0:T(8,128)(2,1)S(1)} %get-tuple-element.240), channel_id=1, source_target_pairs={{0,1},{1,0},{2,3},{3,2},{4,5},{5,4},{6,7},{7,6},{8,9},{9,8},{10,11... | collective-permute-start | bytes 1572872 | tf_op jit(solution)/shard_map/ppermute | solution.py:52
  265.2 22.0 %collective-permute-start.28 = (bf16[256,2048]{1,0:T(8,128)(2,1)}, bf16[256,2048]{1,0:T(8,128)(2,1)S(1)}, u32[]{:S(2)}, u32[]{:S(2)}) collective-permute-start(bf16[256,2048]{1,0:T(8,128)(2,1)} %pad_maximum_fusion.6), channel_id=1, source_target_pairs={{0,2},{1,3},{2,0},{3,1},{4,6},{5,7},{6,4},{7,5},{8,10},{9,11},{10,... | collective-permute-start | bytes 3145736 | tf_op jit(solution)/shard_map/ppermute | solution.py:52
  267.2 20.1 %collective-permute-start.26 = (bf16[256,2048]{1,0:T(8,128)(2,1)}, bf16[256,2048]{1,0:T(8,128)(2,1)}, u32[]{:S(2)}, u32[]{:S(2)}) collective-permute-start(bf16[256,2048]{1,0:T(8,128)(2,1)} %pad_maximum_fusion.5), channel_id=1, source_target_pairs={{0,1},{1,0},{2,3},{3,2},{4,5},{5,4},{6,7},{7,6},{8,9},{9,8},{10,11... | collective-permute-start | bytes 3145736 | tf_op jit(solution)/shard_map/ppermute | solution.py:52
  290.7 307.1 %all-reduce.3.cloned.1.call-start = ((), (), s32[]{:S(2)}) async-start(), calls=%async_computation.6 | async-start | bytes 12582912 | tf_op jit(solution)/shard_map/psum | solution.py:764
  299.3 23.6 %collective-permute-start.30 = (bf16[256,2048]{1,0:T(8,128)(2,1)}, bf16[256,2048]{1,0:T(8,128)(2,1)S(1)}, u32[]{:S(2)}, u32[]{:S(2)}) collective-permute-start(bf16[256,2048]{1,0:T(8,128)(2,1)} %get-tuple-element.194), channel_id=1, source_target_pairs={{0,2},{1,3},{2,0},{3,1},{4,6},{5,7},{6,4},{7,5},{8,10},{9,11},{10,... | collective-permute-start | bytes 3145736 | tf_op jit(solution)/shard_map/ppermute | solution.py:52
  299.8 21.7 %collective-permute-start.29 = (bf16[256,2048]{1,0:T(8,128)(2,1)}, bf16[256,2048]{1,0:T(8,128)(2,1)S(1)}, u32[]{:S(2)}, u32[]{:S(2)}) collective-permute-start(bf16[256,2048]{1,0:T(8,128)(2,1)} %get-tuple-element.194), channel_id=1, source_target_pairs={{0,1},{1,0},{2,3},{3,2},{4,5},{5,4},{6,7},{7,6},{8,9},{9,8},{10,11... | collective-permute-start | bytes 3145736 | tf_op jit(solution)/shard_map/ppermute | solution.py:52
  339.2 78.0 %collective-permute-start.39 = (bf16[1,64,1408]{2,1,0:T(8,128)(2,1)}, bf16[1,64,1408]{2,1,0:T(8,128)(2,1)}, u32[]{:S(2)}, u32[]{:S(2)}) collective-permute-start(bf16[1,64,1408]{2,1,0:T(8,128)(2,1)} %get-tuple-element.258), channel_id=1, source_target_pairs={{0,3},{1,2},{2,1},{3,0},{4,7},{5,6},{6,5},{7,4},{8,11},{9,10},{10,... | collective-permute-start | bytes 540680 | tf_op jit(solution)/shard_map/ppermute | solution.py:52
  340.6 76.7 %collective-permute-start.38 = (bf16[1,64,1408]{2,1,0:T(8,128)(2,1)}, bf16[1,64,1408]{2,1,0:T(8,128)(2,1)}, u32[]{:S(2)}, u32[]{:S(2)}) collective-permute-start(bf16[1,64,1408]{2,1,0:T(8,128)(2,1)} %get-tuple-element.259), channel_id=1, source_target_pairs={{0,2},{1,3},{2,0},{3,1},{4,6},{5,7},{6,4},{7,5},{8,10},{9,11},{10,... | collective-permute-start | bytes 540680 | tf_op jit(solution)/shard_map/ppermute | solution.py:52
  340.6 76.7 %collective-permute-start.37 = (bf16[1,64,1408]{2,1,0:T(8,128)(2,1)}, bf16[1,64,1408]{2,1,0:T(8,128)(2,1)}, u32[]{:S(2)}, u32[]{:S(2)}) collective-permute-start(bf16[1,64,1408]{2,1,0:T(8,128)(2,1)} %get-tuple-element.260), channel_id=1, source_target_pairs={{0,1},{1,0},{2,3},{3,2},{4,5},{5,4},{6,7},{7,6},{8,9},{9,8},{10,11... | collective-permute-start | bytes 540680 | tf_op jit(solution)/shard_map/ppermute | solution.py:52
  360.4 29.9 %collective-permute-start.34 = (bf16[128,1024]{1,0:T(8,128)(2,1)S(1)}, bf16[128,1024]{1,0:T(8,128)(2,1)S(1)}, u32[]{:S(2)}, u32[]{:S(2)}) collective-permute-start(bf16[128,1024]{1,0:T(8,128)(2,1)S(1)} %get-tuple-element.265), channel_id=1, source_target_pairs={{0,1},{1,0},{2,3},{3,2},{4,5},{5,4},{6,7},{7,6},{8,9},{9,8},{10,11... | collective-permute-start | bytes 786440 | tf_op jit(solution)/shard_map/ppermute | solution.py:52
  360.5 29.9 %collective-permute-start.33 = (bf16[128,1024]{1,0:T(8,128)(2,1)S(1)}, bf16[128,1024]{1,0:T(8,128)(2,1)S(1)}, u32[]{:S(2)}, u32[]{:S(2)}) collective-permute-start(bf16[128,1024]{1,0:T(8,128)(2,1)S(1)} %get-tuple-element.266), channel_id=1, source_target_pairs={{0,2},{1,3},{2,0},{3,1},{4,6},{5,7},{6,4},{7,5},{8,10},{9,11},{10,... | collective-permute-start | bytes 786440 | tf_op jit(solution)/shard_map/ppermute | solution.py:52
  391.3 19.5 %collective-permute-start.35 = (bf16[256,1024]{1,0:T(8,128)(2,1)}, bf16[256,1024]{1,0:T(8,128)(2,1)S(1)}, u32[]{:S(2)}, u32[]{:S(2)}) collective-permute-start(bf16[256,1024]{1,0:T(8,128)(2,1)} %pad_maximum_fusion.12), channel_id=1, source_target_pairs={{0,1},{1,0},{2,3},{3,2},{4,5},{5,4},{6,7},{7,6},{8,9},{9,8},{10,11... | collective-permute-start | bytes 1572872 | tf_op jit(solution)/shard_map/ppermute | solution.py:52
  394.1 16.7 %collective-permute-start.36 = (bf16[256,1024]{1,0:T(8,128)(2,1)}, bf16[256,1024]{1,0:T(8,128)(2,1)}, u32[]{:S(2)}, u32[]{:S(2)}) collective-permute-start(bf16[256,1024]{1,0:T(8,128)(2,1)} %pad_maximum_fusion.13), channel_id=1, source_target_pairs={{0,2},{1,3},{2,0},{3,1},{4,6},{5,7},{6,4},{7,5},{8,10},{9,11},{10,... | collective-permute-start | bytes 1572872 | tf_op jit(solution)/shard_map/ppermute | solution.py:52
  475.2 97.7 %collective-permute-start.74 = (bf16[2,64,1408]{2,1,0:T(8,128)(2,1)S(1)}, bf16[2,64,1408]{2,1,0:T(8,128)(2,1)S(1)}, u32[]{:S(2)}, u32[]{:S(2)}) collective-permute-start(bf16[2,64,1408]{2,1,0:T(8,128)(2,1)S(1)} %get-tuple-element.218), channel_id=1, source_target_pairs={{0,3},{1,2},{2,1},{3,0},{4,7},{5,6},{6,5},{7,4},{8,11},{9,10},{10,... | collective-permute-start | bytes 1081352 | tf_op jit(solution)/shard_map/ppermute | solution.py:52
  476.8 94.2 %collective-permute-start.73 = (bf16[2,64,1408]{2,1,0:T(8,128)(2,1)S(1)}, bf16[2,64,1408]{2,1,0:T(8,128)(2,1)S(1)}, u32[]{:S(2)}, u32[]{:S(2)}) collective-permute-start(bf16[2,64,1408]{2,1,0:T(8,128)(2,1)S(1)} %get-tuple-element.219), channel_id=1, source_target_pairs={{0,2},{1,3},{2,0},{3,1},{4,6},{5,7},{6,4},{7,5},{8,10},{9,11},{10,... | collective-permute-start | bytes 1081352 | tf_op jit(solution)/shard_map/ppermute | solution.py:52
  504.2 20.6 %collective-permute-start.60 = (bf16[64,1536]{1,0:T(8,128)(2,1)S(1)}, bf16[64,1536]{1,0:T(8,128)(2,1)S(1)}, u32[]{:S(2)}, u32[]{:S(2)}) collective-permute-start(bf16[64,1536]{1,0:T(8,128)(2,1)S(1)} %get-tuple-element.248), channel_id=1, source_target_pairs={{0,24},{4,28},{8,16},{12,20},{16,8},{20,12},{24,0},{28,4},{1,25},{... | collective-permute-start | bytes 589832 | tf_op jit(solution)/shard_map/ppermute | solution.py:52
  506.5 24.3 %collective-permute-start.59 = (bf16[64,1536]{1,0:T(8,128)(2,1)S(1)}, bf16[64,1536]{1,0:T(8,128)(2,1)S(1)}, u32[]{:S(2)}, u32[]{:S(2)}) collective-permute-start(bf16[64,1536]{1,0:T(8,128)(2,1)S(1)} %get-tuple-element.249), channel_id=1, source_target_pairs={{0,16},{4,20},{8,24},{12,28},{16,0},{20,4},{24,8},{28,12},{1,17},{... | collective-permute-start | bytes 589832 | tf_op jit(solution)/shard_map/ppermute | solution.py:52
  515.4 74.5 %collective-permute-start.51 = (bf16[256,2048]{1,0:T(8,128)(2,1)S(1)}, bf16[256,2048]{1,0:T(8,128)(2,1)S(1)}, u32[]{:S(2)}, u32[]{:S(2)}) collective-permute-start(bf16[256,2048]{1,0:T(8,128)(2,1)S(1)} %pad_maximum_fusion.8), channel_id=1, source_target_pairs={{0,2},{1,3},{2,0},{3,1},{4,6},{5,7},{6,4},{7,5},{8,10},{9,11},{10,... | collective-permute-start | bytes 3145736 | tf_op jit(solution)/shard_map/ppermute | solution.py:52
  532.4 57.5 %collective-permute-start.49 = (bf16[256,2048]{1,0:T(8,128)(2,1)S(1)}, bf16[256,2048]{1,0:T(8,128)(2,1)S(1)}, u32[]{:S(2)}, u32[]{:S(2)}) collective-permute-start(bf16[256,2048]{1,0:T(8,128)(2,1)S(1)} %pad_maximum_fusion.7), channel_id=1, source_target_pairs={{0,1},{1,0},{2,3},{3,2},{4,5},{5,4},{6,7},{7,6},{8,9},{9,8},{10,11... | collective-permute-start | bytes 3145736 | tf_op jit(solution)/shard_map/ppermute | solution.py:52
  541.4 17.4 %collective-permute-start.62 = (bf16[64,1536]{1,0:T(8,128)(2,1)S(1)}, bf16[64,1536]{1,0:T(8,128)(2,1)S(1)}, u32[]{:S(2)}, u32[]{:S(2)}) collective-permute-start(bf16[64,1536]{1,0:T(8,128)(2,1)S(1)} %get-tuple-element.192), channel_id=1, source_target_pairs={{0,16},{4,20},{8,24},{12,28},{16,0},{20,4},{24,8},{28,12},{1,17},{... | collective-permute-start | bytes 589832 | tf_op jit(solution)/shard_map/ppermute | solution.py:52
  570.5 16.3 %collective-permute-start.65 = (bf16[256,1536]{1,0:T(8,128)(2,1)S(1)}, bf16[256,1536]{1,0:T(8,128)(2,1)S(1)}, u32[]{:S(2)}, u32[]{:S(2)}) collective-permute-start(bf16[256,1536]{1,0:T(8,128)(2,1)S(1)} %constant_dynamic-update-slice_fusion.30), channel_id=1, source_target_pairs={{0,2},{1,3},{2,0},{3,1},{4,6},{5,7},{6,4},{7,5},{8,10},{9,11},{10,... | collective-permute-start | bytes 2359304 | tf_op jit(solution)/shard_map/ppermute | solution.py:52
  571.0 18.1 %collective-permute-start.64 = (bf16[256,1536]{1,0:T(8,128)(2,1)S(1)}, bf16[256,1536]{1,0:T(8,128)(2,1)S(1)}, u32[]{:S(2)}, u32[]{:S(2)}) collective-permute-start(bf16[256,1536]{1,0:T(8,128)(2,1)S(1)} %constant_dynamic-update-slice_fusion.30), channel_id=1, source_target_pairs={{0,1},{1,0},{2,3},{3,2},{4,5},{5,4},{6,7},{7,6},{8,9},{9,8},{10,11... | collective-permute-start | bytes 2359304 | tf_op jit(solution)/shard_map/ppermute | solution.py:52
  (139 other events, 1146.9 us)
Sparse Core Ops, SparseCore 0:
  37.2 108.3 all-gather.2
  147.2 58.7 all-gather.4
  212.3 63.8 reduce-scatter.2
  290.8 118.2 reduce-scatter.4
  427.9 164.8 all-reduce.2
